TPU v7x, 256 devices: a whole 4x4x8 slice. The times are simulated.
256 devices in a mesh: patch: 32 (over y, z_lo, core), guide: 8 (over x, z_hi).
Axes of the slice: x: 4, y: 4, z: 8 (z_hi: 2, z_lo: 4; z = z_hi * 4 + z_lo), core: 2. Of those that a mesh axis runs over, the one named last changes fastest.
Arguments:
- hidden_in: bfloat16 [8, 2048, 1152], P('guide', 'patch'), may hold values from -6 to 6
- stale_in: bfloat16 [8, 2048, 1152], P('guide', 'patch'), may hold values from -6 to 6
- modulation: float32 [8, 5, 1152], P('guide'), may hold values from -3 to 3
- latent: float32 [8, 256, 128], P('guide', 'patch'), may hold values from -6 to 6
- timestep: int32 [4], replicated, may hold values from 100 to 799
- w_qkv: bfloat16 [1152, 3456], replicated, may hold values from -1.26689965 to 1.26689965
- w_out: bfloat16 [1152, 1152], replicated, may hold values from -0.1875 to 0.1875
- w_final: bfloat16 [1152, 16], replicated, may hold values from -0.1875 to 0.1875
Outputs:
- next_latent: float32 [8, 256, 128], P('guide', 'patch')
All inputs are finite; a program needn't handle non-finite values.
Results may differ from a plain program's by a relative error of at most 0.0025.
Values may be sent and summed in bfloat16 or wider, within the bound.
No kernel may reach another device: no remote copies, remote signals or barrier semaphores. Data moves between devices by JAX's collectives and lax.ppermute only.
A program may use at most 128 MiB of HBM per device.

v0:
```python
import math

import jax
import jax.numpy as jnp
from jax import lax
from jax.sharding import PartitionSpec as P

HEADS = 16
STRIDE = 50


def partner_2(value, axis, distance):
    mask = 2**distance
    pairs = [(source, source ^ mask) for source in range(lax.axis_size(axis))]
    return lax.ppermute(value, axis, pairs)


def layer_norm(values):
    mean = jnp.mean(values, axis=-1, keepdims=True)
    centred = values - mean
    var = jnp.mean(centred * centred, axis=-1, keepdims=True)
    return centred / jnp.sqrt(var + 1e-06)


def alpha_bar(step_index):
    angle = (step_index.astype(jnp.float32) / 1000.0 + 0.008) / 1.008 * (math.pi / 2.0)
    return jnp.cos(angle) ** 2


def body(hidden_in, stale_in, modulation, latent, timestep, w_qkv, w_out, w_final):
    width = hidden_in.shape[2]
    tok_rows = hidden_in.shape[1]
    head_count = HEADS
    head_size = width // head_count
    image = lax.axis_index("guide")
    patch_id = lax.axis_index("patch")
    mod = modulation[0]
    source = hidden_in[0].astype(jnp.float32)
    attn_in = (layer_norm(source) * (1.0 + mod[1]) + mod[0]).astype(jnp.bfloat16)
    fresh = jnp.dot(attn_in, w_qkv, preferred_element_type=jnp.float32).astype(jnp.bfloat16)
    w_keyval = w_qkv[:, width:]
    stale_kv = jnp.dot(stale_in[0], w_keyval, preferred_element_type=jnp.float32).astype(
        jnp.bfloat16
    )
    all_kv = lax.all_gather(stale_kv, "patch", axis=0, tiled=True)
    all_kv = lax.dynamic_update_slice_in_dim(all_kv, fresh[:, width:], patch_id * tok_rows, 0)
    query_heads = fresh[:, :width].reshape(tok_rows, head_count, head_size)
    key_heads = all_kv[:, :width].reshape(-1, head_count, head_size)
    value_heads = all_kv[:, width:].reshape(-1, head_count, head_size)
    scores = jnp.einsum(
        "qhd,khd->hqk", query_heads, key_heads, preferred_element_type=jnp.float32
    ) * head_size ** (-0.5)
    top = jnp.max(scores, axis=-1, keepdims=True)
    expo = jnp.exp(scores - top)
    prob = (expo / jnp.sum(expo, axis=-1, keepdims=True)).astype(jnp.bfloat16)
    attended = jnp.einsum("hqk,khd->qhd", prob, value_heads, preferred_element_type=jnp.float32)
    attended = attended.astype(jnp.bfloat16).reshape(tok_rows, width)
    mixed = source + mod[2] * jnp.dot(attended, w_out, preferred_element_type=jnp.float32)
    final_in = (layer_norm(mixed) * (1.0 + mod[4]) + mod[3]).astype(jnp.bfloat16)
    noise = jnp.dot(final_in, w_final, preferred_element_type=jnp.float32).reshape(-1, 128)
    partner = partner_2(noise, "guide", 0)
    is_cond = image % 2 == 0
    cond = jnp.where(is_cond, noise, partner)
    uncond = jnp.where(is_cond, partner, noise)
    guided = uncond + 4.5 * (cond - uncond)
    now = timestep[image // 2]
    bar_now = alpha_bar(now)
    bar_prev = alpha_bar(now - STRIDE)
    clean = (latent[0] - jnp.sqrt(1.0 - bar_now) * guided) / jnp.sqrt(bar_now)
    result = jnp.sqrt(bar_prev) * clean + jnp.sqrt(1.0 - bar_prev) * guided
    return result[None]


def solution(mesh):
    in_specs = (
        P("guide", "patch", None),
        P("guide", "patch", None),
        P("guide", None, None),
        P("guide", "patch", None),
        P(),
        P(),
        P(),
        P(),
    )
    out_specs = P("guide", "patch", None)
    return jax.shard_map(body, mesh=mesh, in_specs=in_specs, out_specs=out_specs, check_vma=False)
```

profile of v0, /device:TPU:2, one launch (start us, length us, event | category | flops | bytes accessed | tf_op | source)
XLA Modules:
  0.0 138.6 jit_solution(17198681384871473736)
XLA Ops:
  6.5 0.0 copy-start
  6.5 0.0 all-gather.2.cloned.1.call-start
  6.5 4.3 %fusion.8 = bf16[64,2304]{1,0:T(8,128)(2,1)} fusion(bf16[1152,3456]{1,0:T(8,128)(2,1)} %param.13, bf16[1,64,1152]{2,1,0:T(8,128)(2,1)} %param.9), kind=kOutput, calls=%fused_computation.10 | convolution fusion | flops 339886080 | bytes 5750784 | tf_op jit(solution)/shard_map/dot_general | solution.py:42
  10.8 0.0 all-gather.2.cloned.1.call-update
  10.9 0.8 add_reduce_fusion
  11.7 1.0 convert_reduce_fusion
  12.7 1.1 fusion.19
  13.9 4.7 %convolution_convert_fusion = bf16[64,3456]{1,0:T(8,128)(2,1)S(1)} fusion(bf16[1152,3456]{1,0:T(8,128)(2,1)} %param.13, bf16[1,64,1152]{2,1,0:T(8,128)(2,1)} %param.8, f32[1152]{0:T(1024)S(1)} %get-tuple-element.6, f32[1152]{0:T(1024)S(1)} %get-tuple-element.7, f32[64]{0:T(128)S(1)} %add_sqrt_fusion.1, f32[64]{0:T(128)S(1)} %broadcast_multiply_fusion.1), kind=kOutput, calls=%fused_computation.7 | convolution fusion | flops 510271488 | bytes 8562176 | tf_op jit(solution)/shard_map/dot_general | solution.py:40
  18.6 0.5 reshape.81
  19.1 65.4 %all-gather.2.cloned.1.call-done = bf16[2048,2304]{1,0:T(8,128)(2,1)} async-done(((bf16[64,2304]{1,0:T(8,128)(2,1)}), bf16[2048,2304]{1,0:T(8,128)(2,1)}) %all-gather.2.cloned.1.call-update) | async-done | bytes 9437200 | tf_op jit(solution)/shard_map/all_gather | solution.py:45
  84.5 0.7 slice_dynamic-update-slice_fusion
  85.2 8.2 %fusion.42 = (bf16[2048,1152]{1,0:T(8,128)(2,1)}, bf16[2048,1152]{1,0:T(8,128)(2,1)}) fusion(bf16[2048,2304]{1,0:T(8,128)(2,1)} %slice_dynamic-update-slice_fusion), kind=kLoop, calls=%fused_computation.52 | loop fusion | bytes 18874368 | tf_op jit(solution)/shard_map/slice | solution.py:48
  93.4 6.7 %copy.13 = bf16[2048,1152]{0,1:T(8,128)(2,1)} copy(bf16[2048,1152]{1,0:T(8,128)(2,1)} %get-tuple-element.10) | data formatting | bytes 9437184 | tf_op jit(solution)/shard_map/slice | solution.py:48
  100.1 6.7 %copy.12 = bf16[2048,1152]{0,1:T(8,128)(2,1)} copy(bf16[2048,1152]{1,0:T(8,128)(2,1)} %get-tuple-element.11) | data formatting | bytes 9437184 | tf_op jit(solution)/shard_map/slice | solution.py:49
  106.8 8.7 %fusion.43 = (f32[16,64]{1,0:T(8,128)S(1)}, f32[16,64,2048]{2,1,0:T(8,128)}) fusion(bf16[2048,16,72]{0,2,1:T(8,128)(2,1)} %bitcast.49, bf16[64,16,72]{2,1,0:T(8,128)(2,1)S(1)} %reshape.81), kind=kOutput, calls=%fused_computation.53 | convolution fusion | flops 308283392 | bytes 13258752 | tf_op jit(solution)/shard_map/sub | solution.py:54
  115.5 0.0 copy-start.1
  115.5 6.3 %fusion.13 = bf16[64,16,72]{2,0,1:T(8,128)(2,1)S(1)} fusion(bf16[2048,16,72]{0,2,1:T(8,128)(2,1)} %bitcast.50, f32[16,64,2048]{2,1,0:T(8,128)} %get-tuple-element.13, f32[16,64]{1,0:T(8,128)S(1)} %get-tuple-element.12), kind=kOutput, calls=%fused_computation.14 | convolution fusion | flops 306257920 | bytes 13258752 | tf_op jit(solution)/shard_map/hqk,khd->qhd/dot_general | solution.py:56
  121.8 0.2 copy.15
  122.0 0.3 reshape.83
  122.3 0.0 copy-done
  122.3 0.0 copy-done.1
  122.3 0.7 fusion.48
  123.0 0.2 multiply_reduce_fusion.1
  123.2 0.0 copy-done.3
  123.3 0.2 fusion.36
  123.5 0.1 reshape.84
  123.6 4.2 %collective-permute-start = (f32[8,128]{1,0:T(8,128)S(1)}, f32[8,128]{1,0:T(8,128)S(1)}, u32[]{:S(2)}, u32[]{:S(2)}) collective-permute-start(f32[8,128]{1,0:T(8,128)S(1)} %reshape.84), channel_id=1, source_target_pairs={{0,1},{1,0},{2,3},{3,2},{4,5},{5,4},{6,7},{7,6},{8,9},{9,8},{10,11... | collective-permute-start | bytes 12296 | tf_op jit(solution)/shard_map/ppermute | solution.py:15
  127.8 0.0 copy-done.4
  127.8 0.6 dynamic_slice.3
  130.0 1.1 collective-permute-done
  131.1 0.0 copy-done.2
  131.1 0.6 fusion.40
  (8 shorter events, 0.0 us)
Async XLA Ops:
  6.5 115.8 %copy-start = (bf16[1152,1152]{1,0:T(8,128)(2,1)S(1)}, bf16[1152,1152]{1,0:T(8,128)(2,1)}, u32[]{:S(2)}) copy-start(bf16[1152,1152]{1,0:T(8,128)(2,1)} %param.14) | copy-start | bytes 7962628
  6.5 78.0 %all-gather.2.cloned.1.call-start = ((), (), s32[]{:S(2)}) async-start(), calls=%async_computation | async-start | bytes 9732096 | tf_op jit(solution)/shard_map/all_gather | solution.py:45
  115.5 6.8 %copy-start.1 = (bf16[1,64,1152]{2,1,0:T(8,128)(2,1)S(1)}, bf16[1,64,1152]{2,1,0:T(8,128)(2,1)}, u32[]{:S(2)}) copy-start(bf16[1,64,1152]{2,1,0:T(8,128)(2,1)} %param.8) | copy-start | bytes 442372
  115.5 7.7 %copy-start.3 = (bf16[1152,16]{0,1:T(8,128)(2,1)S(1)}, bf16[1152,16]{0,1:T(8,128)(2,1)}, u32[]{:S(2)}) copy-start(bf16[1152,16]{0,1:T(8,128)(2,1)} %param.15) | copy-start | bytes 110596
  115.5 12.3 %copy-start.4 = (s32[4]{0:T(128)S(1)}, s32[4]{0:T(128)}, u32[]{:S(2)}) copy-start(s32[4]{0:T(128)} %param.12) | copy-start | bytes 52
  115.5 15.6 %copy-start.2 = (f32[1,8,128]{2,1,0:T(8,128)S(1)}, f32[1,8,128]{2,1,0:T(8,128)}, u32[]{:S(2)}) copy-start(f32[1,8,128]{2,1,0:T(8,128)} %param.11) | copy-start | bytes 12292
  123.6 7.5 %collective-permute-start = (f32[8,128]{1,0:T(8,128)S(1)}, f32[8,128]{1,0:T(8,128)S(1)}, u32[]{:S(2)}, u32[]{:S(2)}) collective-permute-start(f32[8,128]{1,0:T(8,128)S(1)} %reshape.84), channel_id=1, source_target_pairs={{0,1},{1,0},{2,3},{3,2},{4,5},{5,4},{6,7},{7,6},{8,9},{9,8},{10,11... | collective-permute-start | bytes 12296 | tf_op jit(solution)/shard_map/ppermute | solution.py:15
Sparse Core Ops, SparseCore 0:
  11.0 73.4 all-gather.1
where the time goes:
time: 139 us
  waiting for transfers between devices  66.5 us (48%)
  matrix products  25 us (18%)
  local copies, waits for them, and re-layouts  23.9 us (17%)
  between operations  15.1 us (11%)
  starting transfers between devices  4.2 us (3%)
  other arithmetic  3.8 us (3%)
    all_gather x1, waiting for transfers between devices, body(): all_kv = lax.all_gather(stale_kv, 'patch', axis=0, tiled=True)  65.4 us
    slice x2, local copies, waits for them, and re-layouts, body(): key_heads = all_kv[:, :width].reshape(-1, head_count, head_size)  14.9 us
    sub x1, matrix products, body(): expo = jnp.exp(scores - top)  8.68 us
    slice x1, local copies, waits for them, and re-layouts, body(): value_heads = all_kv[:, width:].reshape(-1, head_count, head_size)  6.74 us
    dot_general x1, matrix products, body(): jnp.einsum('hqk,khd->qhd', prob, value_heads, preferred_element_type=jnp....  6.31 us
    dot_general x1, matrix products, body(): jnp.dot(attn_in, w_qkv, preferred_element_type=jnp.float32)  4.75 us
    dot_general x1, matrix products, body(): jnp.dot(stale_in[0], w_keyval, preferred_element_type=jnp.float32)  4.29 us
    ppermute x1, starting transfers between devices, partner_2(): return lax.ppermute(value, axis, pairs)  4.2 us
  transfers between devices with their start and end apart: 2, of which 2 were waited for; matrix products, arithmetic and copies ran while one was open for 6% of the time, Pallas kernels for 0%

commit v1 on v0

v1 whole, which is shorter than its diff:
```python
import functools
import math

import jax
import jax.numpy as jnp
from jax import lax
from jax.experimental import pallas as pl
from jax.experimental.pallas import tpu as pltpu
from jax.sharding import PartitionSpec as P

HEADS = 16
HEAD = 72
WIDTH = 1152
STRIDE = 50
NY, NZ, NC = 4, 4, 2
STATS = 128
BF16, F32 = jnp.bfloat16, jnp.float32
VMEM_LIMIT = 48 * 1024 * 1024


def layer_norm(values):
    mean = jnp.mean(values, axis=-1, keepdims=True)
    centred = values - mean
    var = jnp.mean(centred * centred, axis=-1, keepdims=True)
    return centred / jnp.sqrt(var + 1e-06)


def alpha_bar(step_index):
    angle = (step_index.astype(F32) / 1000.0 + 0.008) / 1.008 * (math.pi / 2.0)
    return jnp.cos(angle) ** 2


def patch_pairs(dy, dz, dc):
    pairs = []
    for y in range(NY):
        for z in range(NZ):
            for c in range(NC):
                target = (((y + dy) % NY) * NZ + (z + dz) % NZ) * NC + (c + dc) % NC
                pairs.append(((y * NZ + z) * NC + c, target))
    return pairs


def send(value, dy=0, dz=0, dc=0):
    return lax.ppermute(value, "patch", patch_pairs(dy, dz, dc))


def fresh_kernel(hidden_ref, mod_ref, w_ref, out_ref, attn_in):
    @pl.when(pl.program_id(0) == 0)
    def _():
        source = hidden_ref[...].astype(F32)
        attn_in[...] = (
            layer_norm(source) * (1.0 + mod_ref[1:2, :]) + mod_ref[0:1, :]
        ).astype(BF16)

    out_ref[...] = jnp.dot(
        attn_in[...], w_ref[...], preferred_element_type=F32
    ).astype(BF16)


def project_fresh(hidden, mod, w_qkv):
    rows, width = hidden.shape
    cols = w_qkv.shape[1]
    block = 384
    return pl.pallas_call(
        fresh_kernel,
        grid=(cols // block,),
        in_specs=[
            pl.BlockSpec((rows, width), lambda i: (0, 0)),
            pl.BlockSpec(mod.shape, lambda i: (0, 0)),
            pl.BlockSpec((width, block), lambda i: (0, i)),
        ],
        out_specs=pl.BlockSpec((rows, block), lambda i: (0, i)),
        out_shape=jax.ShapeDtypeStruct((rows, cols), BF16),
        scratch_shapes=[pltpu.VMEM((rows, width), BF16)],
        compiler_params=pltpu.CompilerParams(vmem_limit_bytes=VMEM_LIMIT),
        cost_estimate=pl.CostEstimate(
            flops=2 * rows * width * cols, bytes_accessed=2 * width * cols, transcendentals=0
        ),
        name="fresh_qkv",
    )(hidden, mod, w_qkv)


def head_window(head):
    start = min(head * HEAD // 128 * 128, WIDTH - 256)
    return start, head * HEAD - start


def attend_kernel(own, *refs):
    if own:
        q_ref, kv_ref, fresh_ref, out_ref, acc = refs
    else:
        q_ref, kv_ref, out_ref, acc = refs
    rows = q_ref.shape[0]
    scale = HEAD ** (-0.5)
    lane = lax.broadcasted_iota(jnp.int32, (rows, 256), 1)
    stat_lane = lax.broadcasted_iota(jnp.int32, (rows, STATS), 1)
    stats = jnp.zeros((rows, STATS), F32)
    acc[...] = jnp.zeros_like(acc)

    def keyval(start):
        cols = pl.ds(start, 256)
        if own:
            n_own = fresh_ref.shape[0]
            return jnp.concatenate([fresh_ref[:, cols], kv_ref[n_own:, cols]], axis=0)
        return kv_ref[:, cols]

    for head in range(HEADS):
        start, offset = head_window(head)
        inside = (lane >= offset) & (lane < offset + HEAD)
        query = jnp.where(inside, q_ref[:, start : start + 256], jnp.zeros((), BF16))
        scores = lax.dot_general(
            query, keyval(start), (((1,), (1,)), ((), ())), preferred_element_type=F32
        ) * scale
        top = jnp.max(scores, axis=-1, keepdims=True)
        expo = jnp.exp(scores - top)
        total = jnp.sum(expo, axis=-1, keepdims=True)
        value = jnp.dot(expo.astype(BF16), keyval(WIDTH + start), preferred_element_type=F32)
        value = jnp.where(inside, value / total, 0.0)
        acc[:, start : start + 256] += value
        stats = jnp.where(stat_lane % HEADS == head, top + jnp.log(total), stats)
    high = stats.astype(BF16)
    rest = stats - high.astype(F32)
    middle = rest.astype(BF16)
    low = (rest - middle.astype(F32)).astype(BF16)
    packed = jnp.where(
        stat_lane < HEADS,
        high.astype(F32),
        jnp.where(
            stat_lane < 2 * HEADS,
            middle.astype(F32),
            jnp.where(stat_lane < 3 * HEADS, low.astype(F32), 0.0),
        ),
    )
    out_ref[:, :WIDTH] = acc[...].astype(BF16)
    out_ref[:, WIDTH:] = packed.astype(BF16)


def attend(query, keyval, fresh=None):
    rows = query.shape[0]
    keys = keyval.shape[0]
    args = (query, keyval) if fresh is None else (query, keyval, fresh)
    return pl.pallas_call(
        functools.partial(attend_kernel, fresh is not None),
        in_specs=[pl.BlockSpec(memory_space=pltpu.VMEM)] * len(args),
        out_specs=pl.BlockSpec(memory_space=pltpu.VMEM),
        out_shape=jax.ShapeDtypeStruct((rows, WIDTH + STATS), BF16),
        scratch_shapes=[pltpu.VMEM((rows, WIDTH), F32)],
        compiler_params=pltpu.CompilerParams(vmem_limit_bytes=VMEM_LIMIT),
        cost_estimate=pl.CostEstimate(
            flops=4 * HEADS * rows * keys * 256,
            bytes_accessed=4 * keys * WIDTH,
            transcendentals=HEADS * rows * keys,
        ),
        name="attend_own" if fresh is not None else "attend",
    )(*args)


def post_kernel(p0, p1, p2, p3, hidden_ref, mod_ref, w_out_ref, w_final_ref, out_ref):
    row = lax.broadcasted_iota(jnp.int32, (STATS, WIDTH), 0)
    col = lax.broadcasted_iota(jnp.int32, (STATS, WIDTH), 1)
    offset = col - (row % HEADS) * HEAD
    pick = (row < 3 * HEADS) & (offset >= 0) & (offset < HEAD)
    pick = jnp.where(pick, 1.0, 0.0).astype(BF16)
    parts = (p0, p1, p2, p3)
    sums = [jnp.dot(p[:, WIDTH:], pick, preferred_element_type=F32) for p in parts]
    top = functools.reduce(jnp.maximum, sums)
    weights = [jnp.exp(s - top) for s in sums]
    total = functools.reduce(jnp.add, weights)
    mix = functools.reduce(
        jnp.add, [w * p[:, :WIDTH].astype(F32) for w, p in zip(weights, parts)]
    )
    attended = (mix / total).astype(BF16)
    source = hidden_ref[...].astype(F32)
    mixed = source + mod_ref[2:3, :] * jnp.dot(
        attended, w_out_ref[...], preferred_element_type=F32
    )
    final_in = (layer_norm(mixed) * (1.0 + mod_ref[4:5, :]) + mod_ref[3:4, :]).astype(BF16)
    wide = jnp.dot(final_in, w_final_ref[...], preferred_element_type=F32)
    rows = wide.shape[0]
    token = lax.broadcasted_iota(jnp.int32, wide.shape, 0) % 8
    place = lax.broadcasted_iota(jnp.int32, wide.shape, 1) // 16
    wide = jnp.where(token == place, wide, 0.0)
    out_ref[...] = jnp.sum(wide.reshape(rows // 8, 8, 128), axis=1)


def post(parts, hidden, mod, w_out, w_final_wide):
    rows = hidden.shape[0]
    return pl.pallas_call(
        post_kernel,
        in_specs=[pl.BlockSpec(memory_space=pltpu.VMEM)] * 8,
        out_specs=pl.BlockSpec(memory_space=pltpu.VMEM),
        out_shape=jax.ShapeDtypeStruct((rows // 8, 128), F32),
        compiler_params=pltpu.CompilerParams(vmem_limit_bytes=VMEM_LIMIT),
        cost_estimate=pl.CostEstimate(
            flops=2 * rows * WIDTH * WIDTH, bytes_accessed=2 * WIDTH * WIDTH, transcendentals=0
        ),
        name="post",
    )(*parts, hidden, mod, w_out, w_final_wide)


def body(hidden_in, stale_in, modulation, latent, timestep, w_qkv, w_out, w_final):
    image = lax.axis_index("guide")
    hidden, stale, mod = hidden_in[0], stale_in[0], modulation[0]

    stale_z = [send(stale, dz=k) for k in (2, 1, 3)]
    w_final_wide = jnp.tile(w_final, (1, 8))
    now = timestep[image // 2]
    bar_now = alpha_bar(now)
    bar_prev = alpha_bar(now - STRIDE)
    latent_gain = jnp.sqrt(bar_prev) / jnp.sqrt(bar_now)
    noise_gain = jnp.sqrt(1.0 - bar_prev) - latent_gain * jnp.sqrt(1.0 - bar_now)

    fresh = project_fresh(hidden, mod, w_qkv)
    query = fresh[:, :WIDTH]
    fresh_kv = fresh[:, WIDTH:]
    query_y = [send(query, dy=k) for k in (2, 1, 3)]

    mine = jnp.concatenate([stale] + stale_z, axis=0)
    other = send(mine, dc=1)
    keys_in = jnp.concatenate([mine, other], axis=0)
    keyval = jnp.dot(keys_in, w_qkv[:, WIDTH:], preferred_element_type=F32).astype(BF16)

    back = []
    for q, k in zip(query_y, (2, 1, 3)):
        back.append(send(attend(q, keyval), dy=-k))
    own = attend(query, keyval, fresh_kv)
    noise = post([own] + back, hidden, mod, w_out, w_final_wide)

    partner = lax.ppermute(
        noise, "guide", [(i, i ^ 1) for i in range(lax.axis_size("guide"))]
    )
    is_cond = image % 2 == 0
    cond = jnp.where(is_cond, noise, partner)
    uncond = jnp.where(is_cond, partner, noise)
    guided = uncond + 4.5 * (cond - uncond)
    return (latent_gain * latent[0] + noise_gain * guided)[None]


def solution(mesh):
    in_specs = (
        P("guide", "patch", None),
        P("guide", "patch", None),
        P("guide", None, None),
        P("guide", "patch", None),
        P(),
        P(),
        P(),
        P(),
    )
    out_specs = P("guide", "patch", None)
    return jax.shard_map(body, mesh=mesh, in_specs=in_specs, out_specs=out_specs, check_vma=False)
```

time: 139 us -> 67.2 us (0.48)
  waiting for transfers between devices: 66.5 us -> 1.94 us
  Pallas kernels: 0 us -> 32.8 us
  matrix products: 25 us -> 3.41 us
  local copies, waits for them, and re-layouts: 23.9 us -> 4.34 us
  starting transfers between devices: 4.2 us -> 22 us
  between operations: 15.1 us -> 1.87 us
  other arithmetic: 3.8 us -> 0.65 us
    all_gather x1 -> x0, waiting for transfers between devices: 65.4 us -> none  [body(): all_kv = lax.all_gather(stale_kv, 'patch', axis=0, tiled=True)]
    pallas_call x0 -> x6, Pallas kernels: none -> 32.8 us  [the longest x4 21.8 us: attend(): pl.pallas_call(functools.partial(attend_kernel, fresh is not None), in_sp...]
    slice x4 -> x2, local copies, waits for them, and re-layouts: 21.6 us -> 0.03 us  [the longest x1 0.02 us: body(): fresh_kv = fresh[:, WIDTH:]]
    ppermute x1 -> x11, starting transfers between devices: 4.2 us -> 22 us  [the longest x10 16.5 us: send(): return lax.ppermute(value, 'patch', patch_pairs(dy, dz, dc))]
    dot_general x5 -> x1, matrix products: 16.3 us -> 3.41 us  [body(): jnp.dot(keys_in, w_qkv[:, WIDTH:], preferred_element_type=F32).astype(BF16)]
    sub x1 -> x0, matrix products: 8.68 us -> none  [body(): expo = jnp.exp(scores - top)]
    reduce_sum x3 -> x0, other arithmetic: 2.35 us -> none  [the longest x2 1.32 us: layer_norm(): var = jnp.mean(centred * centred, axis=-1, keepdims=True)]
    another operation x0 -> x2, local copies, waits for them, and re-layouts: none -> 1.9 us  [body(): w_final_wide = jnp.tile(w_final, (1, 8))]
  transfers between devices with their start and end apart: 2 -> 11, of which waited for: 2 -> 1; matrix products, arithmetic and copies ran while one was open for 6% -> 10% of each run, Pallas kernels for 0% -> 45%
where the time goes in v1:
time: 67.2 us; the launch traced here: 66.9 us
  Pallas kernels  32.8 us (49%)
  starting transfers between devices  22 us (33%)
  local copies, waits for them, and re-layouts  4.34 us (6%)
  matrix products  3.41 us (5%)
  waiting for transfers between devices  1.94 us (3%)
  between operations  1.87 us (3%)
    pallas_call x4, Pallas kernels, attend(): pl.pallas_call(functools.partial(attend_kernel, fresh is not None), in_sp...  21.8 us
    ppermute x10, starting transfers between devices, send(): return lax.ppermute(value, 'patch', patch_pairs(dy, dz, dc))  16.5 us
    pallas_call x1, Pallas kernels, project_fresh(): pl.pallas_call(fresh_kernel, grid=(cols // block,), in_specs=[pl.BlockSpe...  8.42 us
    ppermute x1, starting transfers between devices, body(): lax.ppermute(noise, 'guide', [(i, i ^ 1) for i in range(lax.axis_size('gu...  5.48 us
    dot_general x1, matrix products, body(): jnp.dot(keys_in, w_qkv[:, WIDTH:], preferred_element_type=F32).astype(BF16)  3.41 us
    pallas_call x1, Pallas kernels, post(): pl.pallas_call(post_kernel, in_specs=[pl.BlockSpec(memory_space=pltpu.VME...  2.53 us
    ppermute x10, waiting for transfers between devices, send(): return lax.ppermute(value, 'patch', patch_pairs(dy, dz, dc))  1.94 us
    another operation x2, local copies, waits for them, and re-layouts, body(): w_final_wide = jnp.tile(w_final, (1, 8))  1.9 us
  transfers between devices with their start and end apart: 11, of which 1 were waited for; matrix products, arithmetic and copies ran while one was open for 10% of the time, Pallas kernels for 45%

profile of v1, /device:TPU:2, one launch (start us, length us, event | category | flops | bytes accessed | tf_op | source)
XLA Modules:
  0.0 66.9 jit_solution(11835508892335238750)
XLA Ops:
  0.0 3.3 %collective-permute-start = (bf16[64,1152]{1,0:T(8,128)(2,1)}, bf16[64,1152]{1,0:T(8,128)(2,1)S(1)}, u32[]{:S(2)}, u32[]{:S(2)}) collective-permute-start(bf16[64,1152]{1,0:T(8,128)(2,1)} %bitcast.22), channel_id=1, source_target_pairs={{0,32},{8,40},{16,48},{24,56},{32,0},{40,8},{48,16},{56,24},{64,96... | collective-permute-start | bytes 442376 | tf_op jit(solution)/shard_map/ppermute | solution.py:44
  3.3 1.9 %collective-permute-start.1 = (bf16[64,1152]{1,0:T(8,128)(2,1)}, bf16[64,1152]{1,0:T(8,128)(2,1)S(1)}, u32[]{:S(2)}, u32[]{:S(2)}) collective-permute-start(bf16[64,1152]{1,0:T(8,128)(2,1)} %bitcast.23), channel_id=1, source_target_pairs={{0,16},{8,24},{16,32},{24,40},{32,48},{40,56},{48,0},{56,8},{64,80... | collective-permute-start | bytes 442376 | tf_op jit(solution)/shard_map/ppermute | solution.py:44
  5.2 1.9 %collective-permute-start.2 = (bf16[64,1152]{1,0:T(8,128)(2,1)}, bf16[64,1152]{1,0:T(8,128)(2,1)S(1)}, u32[]{:S(2)}, u32[]{:S(2)}) collective-permute-start(bf16[64,1152]{1,0:T(8,128)(2,1)} %bitcast.24), channel_id=1, source_target_pairs={{0,48},{8,56},{16,0},{24,8},{32,16},{40,24},{48,32},{56,40},{64,11... | collective-permute-start | bytes 442376 | tf_op jit(solution)/shard_map/ppermute | solution.py:44
  7.1 0.7 %copy.13 = f32[1,5,1152]{2,1,0:T(8,128)S(1)} copy(f32[1,5,1152]{2,0,1:T(1,128)} %param.10) | data formatting | bytes 46080
  7.8 0.9 %copy-done.1 = bf16[1,64,1152]{2,1,0:T(8,128)(2,1)S(1)} copy-done((bf16[1,64,1152]{2,1,0:T(8,128)(2,1)S(1)}, bf16[1,64,1152]{2,1,0:T(8,128)(2,1)}, u32[]{:S(2)}) %copy-start.1) | copy-done | bytes 147480
  8.8 8.4 %fresh_qkv.1 = bf16[64,3456]{1,0:T(8,128)(2,1)S(1)} custom-call(bf16[64,1152]{1,0:T(8,128)(2,1)S(1)} %bitcast.17, f32[5,1152]{1,0:T(8,128)S(1)} %bitcast.19, bf16[1152,3456]{1,0:T(8,128)(2,1)} %w_ref.1), custom_call_target="tpu_custom_call" | custom-call | flops 509607936 | bytes 7962624 | tf_op jit(solution)/shard_map/fresh_qkv/pallas_call | solution.py:64
  17.2 1.7 %collective-permute-start.6 = (bf16[64,1152]{1,0:T(8,128)(2,1)S(1)}, bf16[64,1152]{1,0:T(8,128)(2,1)S(1)}, u32[]{:S(2)}, u32[]{:S(2)}) collective-permute-start(bf16[64,1152]{1,0:T(8,128)(2,1)S(1)} %slice.12.refs_0_), channel_id=1, source_target_pairs={{0,64},{8,72},{16,80},{24,88},{32,96},{40,104},{48,112},{56,120},{... | collective-permute-start | bytes 442376 | tf_op jit(solution)/shard_map/ppermute | solution.py:44
  18.8 1.7 %collective-permute-start.8 = (bf16[64,1152]{1,0:T(8,128)(2,1)S(1)}, bf16[64,1152]{1,0:T(8,128)(2,1)S(1)}, u32[]{:S(2)}, u32[]{:S(2)}) collective-permute-start(bf16[64,1152]{1,0:T(8,128)(2,1)S(1)} %slice.12.refs_0_), channel_id=1, source_target_pairs={{0,192},{8,200},{16,208},{24,216},{32,224},{40,232},{48,240},{56,2... | collective-permute-start | bytes 442376 | tf_op jit(solution)/shard_map/ppermute | solution.py:44
  20.5 0.0 collective-permute-done
  20.5 2.1 %collective-permute-start.4 = (bf16[64,1152]{1,0:T(8,128)(2,1)S(1)}, bf16[64,1152]{1,0:T(8,128)(2,1)S(1)}, u32[]{:S(2)}, u32[]{:S(2)}) collective-permute-start(bf16[64,1152]{1,0:T(8,128)(2,1)S(1)} %slice.12.refs_0_), channel_id=1, source_target_pairs={{0,128},{8,136},{16,144},{24,152},{32,160},{40,168},{48,176},{56,1... | collective-permute-start | bytes 442376 | tf_op jit(solution)/shard_map/ppermute | solution.py:44
  22.6 0.0 collective-permute-done.1
  22.7 0.1 collective-permute-start.3
  22.8 1.9 %collective-permute-done.3 = bf16[256,1152]{1,0:T(8,128)(2,1)S(1)} collective-permute-done((bf16[256,1152]{1,0:T(8,128)(2,1)S(1)}, bf16[256,1152]{1,0:T(8,128)(2,1)S(1)}, u32[]{:S(2)}, u32[]{:S(2)}) %collective-permute-start.3) | collective-permute-done | bytes 589856 | tf_op jit(solution)/shard_map/ppermute | solution.py:44
  24.8 0.1 constant_dynamic-update-slice_fusion
  24.8 3.4 %fusion.2.refs_1_ = bf16[512,2304]{1,0:T(8,128)(2,1)S(1)} fusion(bf16[512,1152]{1,0:T(8,128)(2,1)S(1)} %constant_dynamic-update-slice_fusion, bf16[1152,3456]{1,0:T(8,128)(2,1)S(1)} %copy-done.3), kind=kOutput, calls=%fused_computation.2 | convolution fusion | flops 2719088640 | bytes 8847360 | tf_op jit(solution)/shard_map/dot_general | solution.py:221
  28.3 5.3 %attend.4 = bf16[64,1280]{1,0:T(8,128)(2,1)S(1)} custom-call(bf16[64,1152]{1,0:T(8,128)(2,1)S(1)} %collective-permute-done.6.refs_0_, bf16[512,2304]{1,0:T(8,128)(2,1)S(1)} %fusion.2.refs_1_), custom_call_target="tpu_custom_call" | custom-call | flops 536870912 | bytes 2359296 | tf_op jit(solution)/shard_map/attend/pallas_call | solution.py:142
  33.6 1.1 %collective-permute-start.7 = (bf16[64,1280]{1,0:T(8,128)(2,1)S(1)}, bf16[64,1280]{1,0:T(8,128)(2,1)}, u32[]{:S(2)}, u32[]{:S(2)}) collective-permute-start(bf16[64,1280]{1,0:T(8,128)(2,1)S(1)} %attend.4), channel_id=1, source_target_pairs={{0,192},{8,200},{16,208},{24,216},{32,224},{40,232},{48,240},{56,2... | collective-permute-start | bytes 491528 | tf_op jit(solution)/shard_map/ppermute | solution.py:44
  34.7 5.3 %attend.5 = bf16[64,1280]{1,0:T(8,128)(2,1)S(1)} custom-call(bf16[64,1152]{1,0:T(8,128)(2,1)S(1)} %collective-permute-done.8.refs_0_, bf16[512,2304]{1,0:T(8,128)(2,1)S(1)} %fusion.2.refs_1_), custom_call_target="tpu_custom_call" | custom-call | flops 536870912 | bytes 2359296 | tf_op jit(solution)/shard_map/attend/pallas_call | solution.py:142
  40.0 0.0 copy-start.5
  40.0 1.2 %collective-permute-start.9 = (bf16[64,1280]{1,0:T(8,128)(2,1)S(1)}, bf16[64,1280]{1,0:T(8,128)(2,1)}, u32[]{:S(2)}, u32[]{:S(2)}) collective-permute-start(bf16[64,1280]{1,0:T(8,128)(2,1)S(1)} %attend.5), channel_id=1, source_target_pairs={{0,64},{8,72},{16,80},{24,88},{32,96},{40,104},{48,112},{56,120},{... | collective-permute-start | bytes 491528 | tf_op jit(solution)/shard_map/ppermute | solution.py:44
  41.2 6.0 %attend.3 = bf16[64,1280]{1,0:T(8,128)(2,1)} custom-call(bf16[64,1152]{1,0:T(8,128)(2,1)S(1)} %collective-permute-done.4.refs_0_, bf16[512,2304]{1,0:T(8,128)(2,1)S(1)} %fusion.2.refs_1_), custom_call_target="tpu_custom_call" | custom-call | flops 536870912 | bytes 2359296 | tf_op jit(solution)/shard_map/attend/pallas_call | solution.py:142
  47.2 1.5 %collective-permute-start.5 = (bf16[64,1280]{1,0:T(8,128)(2,1)}, bf16[64,1280]{1,0:T(8,128)(2,1)}, u32[]{:S(2)}, u32[]{:S(2)}) collective-permute-start(bf16[64,1280]{1,0:T(8,128)(2,1)} %attend.3), channel_id=1, source_target_pairs={{0,128},{8,136},{16,144},{24,152},{32,160},{40,168},{48,176},{56,1... | collective-permute-start | bytes 491528 | tf_op jit(solution)/shard_map/ppermute | solution.py:44
  48.8 0.7 %tile.4 = bf16[1152,8,16]{0,2,1:T(8,128)(2,1)} broadcast(bf16[1152,16]{0,1:T(8,128)(2,1)S(1)} %copy-done.5), dimensions={0,2} | broadcast | bytes 331776 | tf_op jit(solution)/shard_map/tile | solution.py:206
  49.5 1.2 %copy.10.w_final_ref = bf16[1152,128]{1,0:T(8,128)(2,1)S(1)} copy(bf16[1152,128]{0,1:T(8,128)(2,1)} %bitcast.21) | data formatting | bytes 589824 | tf_op jit(solution)/shard_map/tile | solution.py:206
  50.7 0.0 copy-start.2
  50.7 5.3 %attend_own.1.p0 = bf16[64,1280]{1,0:T(8,128)(2,1)S(1)} custom-call(bf16[64,1152]{1,0:T(8,128)(2,1)S(1)} %slice.12.refs_0_, bf16[512,2304]{1,0:T(8,128)(2,1)S(1)} %fusion.2.refs_1_, bf16[64,2304]{1,0:T(8,128)(2,1)S(1)} %slice.13.refs_2_), custom_call_target="tpu_custom_call" | custom-call | flops 536870912 | bytes 2359296 | tf_op jit(solution)/shard_map/attend_own/pallas_call | solution.py:142
  56.0 0.0 copy-start.7
  56.0 0.0 copy-start.6
  56.1 2.5 %post.1 = f32[8,128]{1,0:T(8,128)S(1)} custom-call(bf16[64,1280]{1,0:T(8,128)(2,1)S(1)} %attend_own.1.p0, bf16[64,1280]{1,0:T(8,128)(2,1)} %collective-permute-done.5.p1, bf16[64,1280]{1,0:T(8,128)(2,1)} %collective-permute-done.7.p2, bf16[64,1280]{1,0:T(8,128)(2,1)} %collective-permute-done.9.p3, bf16[64,1152]{1,0:T(8,128)(2,1)S(1)} %bitcast.18, ...), custom_call_target="tpu_custom_call" | custom-call | flops 169869312 | bytes 2654208 | tf_op jit(solution)/shard_map/post/pallas_call | solution.py:188
  58.6 5.5 %collective-permute-start.10 = (f32[8,128]{1,0:T(8,128)S(1)}, f32[8,128]{1,0:T(8,128)S(1)}, u32[]{:S(2)}, u32[]{:S(2)}) collective-permute-start(f32[8,128]{1,0:T(8,128)S(1)} %post.1), channel_id=1, source_target_pairs={{0,1},{1,0},{2,3},{3,2},{4,5},{5,4},{6,7},{7,6},{8,9},{9,8},{10,11... | collective-permute-start | bytes 12296 | tf_op jit(solution)/shard_map/ppermute | solution.py:229
  64.1 0.6 dynamic_slice.3
  66.3 0.6 fusion.5
  (26 shorter events, 0.2 us)
Async XLA Ops:
  0.0 20.5 %collective-permute-start = (bf16[64,1152]{1,0:T(8,128)(2,1)}, bf16[64,1152]{1,0:T(8,128)(2,1)S(1)}, u32[]{:S(2)}, u32[]{:S(2)}) collective-permute-start(bf16[64,1152]{1,0:T(8,128)(2,1)} %bitcast.22), channel_id=1, source_target_pairs={{0,32},{8,40},{16,48},{24,56},{32,0},{40,8},{48,16},{56,24},{64,96... | collective-permute-start | bytes 442376 | tf_op jit(solution)/shard_map/ppermute | solution.py:44
  3.3 19.3 %collective-permute-start.1 = (bf16[64,1152]{1,0:T(8,128)(2,1)}, bf16[64,1152]{1,0:T(8,128)(2,1)S(1)}, u32[]{:S(2)}, u32[]{:S(2)}) collective-permute-start(bf16[64,1152]{1,0:T(8,128)(2,1)} %bitcast.23), channel_id=1, source_target_pairs={{0,16},{8,24},{16,32},{24,40},{32,48},{40,56},{48,0},{56,8},{64,80... | collective-permute-start | bytes 442376 | tf_op jit(solution)/shard_map/ppermute | solution.py:44
  5.2 17.4 %collective-permute-start.2 = (bf16[64,1152]{1,0:T(8,128)(2,1)}, bf16[64,1152]{1,0:T(8,128)(2,1)S(1)}, u32[]{:S(2)}, u32[]{:S(2)}) collective-permute-start(bf16[64,1152]{1,0:T(8,128)(2,1)} %bitcast.24), channel_id=1, source_target_pairs={{0,48},{8,56},{16,0},{24,8},{32,16},{40,24},{48,32},{56,40},{64,11... | collective-permute-start | bytes 442376 | tf_op jit(solution)/shard_map/ppermute | solution.py:44
  7.8 0.9 %copy-start.1 = (bf16[1,64,1152]{2,1,0:T(8,128)(2,1)S(1)}, bf16[1,64,1152]{2,1,0:T(8,128)(2,1)}, u32[]{:S(2)}) copy-start(bf16[1,64,1152]{2,1,0:T(8,128)(2,1)} %param.8) | copy-start | bytes 442372
  8.7 11.8 %copy-start.4 = (bf16[1,64,1152]{2,1,0:T(8,128)(2,1)S(1)}, bf16[1,64,1152]{2,1,0:T(8,128)(2,1)}, u32[]{:S(2)}) copy-start(bf16[1,64,1152]{2,1,0:T(8,128)(2,1)} %param.9) | copy-start | bytes 442372
  8.7 16.1 %copy-start.3 = (bf16[1152,3456]{1,0:T(8,128)(2,1)S(1)}, bf16[1152,3456]{1,0:T(8,128)(2,1)}, u32[]{:S(2)}) copy-start(bf16[1152,3456]{1,0:T(8,128)(2,1)} %w_ref.1) | copy-start | bytes 23887876
  17.2 11.1 %collective-permute-start.6 = (bf16[64,1152]{1,0:T(8,128)(2,1)S(1)}, bf16[64,1152]{1,0:T(8,128)(2,1)S(1)}, u32[]{:S(2)}, u32[]{:S(2)}) collective-permute-start(bf16[64,1152]{1,0:T(8,128)(2,1)S(1)} %slice.12.refs_0_), channel_id=1, source_target_pairs={{0,64},{8,72},{16,80},{24,88},{32,96},{40,104},{48,112},{56,120},{... | collective-permute-start | bytes 442376 | tf_op jit(solution)/shard_map/ppermute | solution.py:44
  18.8 15.9 %collective-permute-start.8 = (bf16[64,1152]{1,0:T(8,128)(2,1)S(1)}, bf16[64,1152]{1,0:T(8,128)(2,1)S(1)}, u32[]{:S(2)}, u32[]{:S(2)}) collective-permute-start(bf16[64,1152]{1,0:T(8,128)(2,1)S(1)} %slice.12.refs_0_), channel_id=1, source_target_pairs={{0,192},{8,200},{16,208},{24,216},{32,224},{40,232},{48,240},{56,2... | collective-permute-start | bytes 442376 | tf_op jit(solution)/shard_map/ppermute | solution.py:44
  20.5 20.7 %collective-permute-start.4 = (bf16[64,1152]{1,0:T(8,128)(2,1)S(1)}, bf16[64,1152]{1,0:T(8,128)(2,1)S(1)}, u32[]{:S(2)}, u32[]{:S(2)}) collective-permute-start(bf16[64,1152]{1,0:T(8,128)(2,1)S(1)} %slice.12.refs_0_), channel_id=1, source_target_pairs={{0,128},{8,136},{16,144},{24,152},{32,160},{40,168},{48,176},{56,1... | collective-permute-start | bytes 442376 | tf_op jit(solution)/shard_map/ppermute | solution.py:44
  22.7 2.1 %collective-permute-start.3 = (bf16[256,1152]{1,0:T(8,128)(2,1)S(1)}, bf16[256,1152]{1,0:T(8,128)(2,1)S(1)}, u32[]{:S(2)}, u32[]{:S(2)}) collective-permute-start(bf16[256,1152]{1,0:T(8,128)(2,1)S(1)} %pad_maximum_fusion), channel_id=1, source_target_pairs={{0,8},{8,0},{16,24},{24,16},{32,40},{40,32},{48,56},{56,48},{64,72... | collective-permute-start | bytes 1769480 | tf_op jit(solution)/shard_map/ppermute | solution.py:44
  33.6 22.4 %collective-permute-start.7 = (bf16[64,1280]{1,0:T(8,128)(2,1)S(1)}, bf16[64,1280]{1,0:T(8,128)(2,1)}, u32[]{:S(2)}, u32[]{:S(2)}) collective-permute-start(bf16[64,1280]{1,0:T(8,128)(2,1)S(1)} %attend.4), channel_id=1, source_target_pairs={{0,192},{8,200},{16,208},{24,216},{32,224},{40,232},{48,240},{56,2... | collective-permute-start | bytes 491528 | tf_op jit(solution)/shard_map/ppermute | solution.py:44
  40.0 8.8 %copy-start.5 = (bf16[1152,16]{0,1:T(8,128)(2,1)S(1)}, bf16[1152,16]{0,1:T(8,128)(2,1)}, u32[]{:S(2)}) copy-start(bf16[1152,16]{0,1:T(8,128)(2,1)} %param.15) | copy-start | bytes 110596
  40.0 16.0 %collective-permute-start.9 = (bf16[64,1280]{1,0:T(8,128)(2,1)S(1)}, bf16[64,1280]{1,0:T(8,128)(2,1)}, u32[]{:S(2)}, u32[]{:S(2)}) collective-permute-start(bf16[64,1280]{1,0:T(8,128)(2,1)S(1)} %attend.5), channel_id=1, source_target_pairs={{0,64},{8,72},{16,80},{24,88},{32,96},{40,104},{48,112},{56,120},{... | collective-permute-start | bytes 491528 | tf_op jit(solution)/shard_map/ppermute | solution.py:44
  47.2 8.8 %collective-permute-start.5 = (bf16[64,1280]{1,0:T(8,128)(2,1)}, bf16[64,1280]{1,0:T(8,128)(2,1)}, u32[]{:S(2)}, u32[]{:S(2)}) collective-permute-start(bf16[64,1280]{1,0:T(8,128)(2,1)} %attend.3), channel_id=1, source_target_pairs={{0,128},{8,136},{16,144},{24,152},{32,160},{40,168},{48,176},{56,1... | collective-permute-start | bytes 491528 | tf_op jit(solution)/shard_map/ppermute | solution.py:44
  50.7 5.4 %copy-start = (bf16[1152,1152]{1,0:T(8,128)(2,1)S(1)}, bf16[1152,1152]{1,0:T(8,128)(2,1)}, u32[]{:S(2)}) copy-start(bf16[1152,1152]{1,0:T(8,128)(2,1)} %w_out_ref.1) | copy-start | bytes 7962628
  50.7 5.4 %copy-start.2 = (bf16[1,64,1152]{2,1,0:T(8,128)(2,1)S(1)}, bf16[1,64,1152]{2,1,0:T(8,128)(2,1)}, u32[]{:S(2)}) copy-start(bf16[1,64,1152]{2,1,0:T(8,128)(2,1)} %param.8) | copy-start | bytes 442372
  56.0 8.1 %copy-start.7 = (s32[4]{0:T(128)S(1)}, s32[4]{0:T(128)}, u32[]{:S(2)}) copy-start(s32[4]{0:T(128)} %param.12) | copy-start | bytes 52
  56.0 10.3 %copy-start.6 = (f32[1,8,128]{2,1,0:T(8,128)S(1)}, f32[1,8,128]{2,1,0:T(8,128)}, u32[]{:S(2)}) copy-start(f32[1,8,128]{2,1,0:T(8,128)} %param.11) | copy-start | bytes 12292
  58.6 7.7 %collective-permute-start.10 = (f32[8,128]{1,0:T(8,128)S(1)}, f32[8,128]{1,0:T(8,128)S(1)}, u32[]{:S(2)}, u32[]{:S(2)}) collective-permute-start(f32[8,128]{1,0:T(8,128)S(1)} %post.1), channel_id=1, source_target_pairs={{0,1},{1,0},{2,3},{3,2},{4,5},{5,4},{6,7},{7,6},{8,9},{9,8},{10,11... | collective-permute-start | bytes 12296 | tf_op jit(solution)/shard_map/ppermute | solution.py:229

commit v2 on v1

v2 whole, which is shorter than its diff:
```python
import functools
import math

import jax
import jax.numpy as jnp
from jax import lax
from jax.experimental import pallas as pl
from jax.experimental.pallas import tpu as pltpu
from jax.sharding import PartitionSpec as P

HEADS = 16
HEAD = 72
WIDTH = 1152
STRIDE = 50
NY, NZ, NC = 4, 4, 2
STATS = 128
CHUNK = 384
BF16, F32 = jnp.bfloat16, jnp.float32
VMEM_LIMIT = 32 * 1024 * 1024


def layer_norm(values):
    mean = jnp.mean(values, axis=-1, keepdims=True)
    centred = values - mean
    var = jnp.mean(centred * centred, axis=-1, keepdims=True)
    return centred / jnp.sqrt(var + 1e-06)


def alpha_bar(step_index):
    angle = (step_index.astype(F32) / 1000.0 + 0.008) / 1.008 * (math.pi / 2.0)
    return jnp.cos(angle) ** 2


def patch_pairs(dy, dz, dc):
    pairs = []
    for y in range(NY):
        for z in range(NZ):
            for c in range(NC):
                target = (((y + dy) % NY) * NZ + (z + dz) % NZ) * NC + (c + dc) % NC
                pairs.append(((y * NZ + z) * NC + c, target))
    return pairs


def send(value, dy=0, dz=0, dc=0):
    return lax.ppermute(value, "patch", patch_pairs(dy, dz, dc))


def selector_kernel(out_ref):
    row = lax.broadcasted_iota(jnp.int32, (STATS, WIDTH), 0)
    col = lax.broadcasted_iota(jnp.int32, (STATS, WIDTH), 1)
    offset = col - (row % HEADS) * HEAD
    pick = (row < 3 * HEADS) & (offset >= 0) & (offset < HEAD)
    out_ref[...] = jnp.where(pick, 1.0, 0.0).astype(BF16)


def head_selector():
    return pl.pallas_call(
        selector_kernel,
        out_specs=pl.BlockSpec(memory_space=pltpu.VMEM),
        out_shape=jax.ShapeDtypeStruct((STATS, WIDTH), BF16),
        compiler_params=pltpu.CompilerParams(vmem_limit_bytes=4 * 1024 * 1024),
        cost_estimate=pl.CostEstimate(
            flops=2 * 10**10, bytes_accessed=4 * 10**7, transcendentals=0
        ),
        name="head_selector",
    )()


def fresh_kernel(hidden_ref, mod_ref, w_ref, out_ref):
    source = hidden_ref[...].astype(F32)
    attn_in = (layer_norm(source) * (1.0 + mod_ref[1]) + mod_ref[0]).astype(BF16)
    for start in range(0, w_ref.shape[1], CHUNK):
        out_ref[:, start : start + CHUNK] = jnp.dot(
            attn_in, w_ref[:, start : start + CHUNK], preferred_element_type=F32
        ).astype(BF16)


def project_fresh(hidden, mod, w_qkv):
    rows, width = hidden.shape
    cols = w_qkv.shape[1]
    return pl.pallas_call(
        fresh_kernel,
        in_specs=[pl.BlockSpec(memory_space=pltpu.VMEM)] * 3,
        out_specs=pl.BlockSpec(memory_space=pltpu.VMEM),
        out_shape=jax.ShapeDtypeStruct((rows, cols), BF16),
        compiler_params=pltpu.CompilerParams(vmem_limit_bytes=VMEM_LIMIT),
        cost_estimate=pl.CostEstimate(
            flops=2 * rows * width * cols, bytes_accessed=2 * width * cols, transcendentals=0
        ),
        name="fresh_qkv",
    )(hidden, mod, w_qkv)


def stale_kernel(first, x0, x1, x2, x3, w_ref, out_ref):
    keys = jnp.concatenate([x0[...], x1[...], x2[...], x3[...]], axis=0)
    for start in range(0, out_ref.shape[1], CHUNK):
        out_ref[:, start : start + CHUNK] = jnp.dot(
            keys,
            w_ref[:, first + start : first + start + CHUNK],
            preferred_element_type=F32,
        ).astype(BF16)


def project_stale(blocks, w_qkv, first, name):
    rows = len(blocks) * blocks[0].shape[0]
    width = w_qkv.shape[0]
    return pl.pallas_call(
        functools.partial(stale_kernel, first),
        in_specs=[pl.BlockSpec(memory_space=pltpu.VMEM)] * 5,
        out_specs=pl.BlockSpec(memory_space=pltpu.VMEM),
        out_shape=jax.ShapeDtypeStruct((rows, width), BF16),
        compiler_params=pltpu.CompilerParams(vmem_limit_bytes=VMEM_LIMIT),
        cost_estimate=pl.CostEstimate(
            flops=2 * rows * width * width, bytes_accessed=2 * width * width, transcendentals=0
        ),
        name=name,
    )(*blocks, w_qkv)


WINDOWS = (
    (0, (0, 1, 2)),
    (128, (3, 4)),
    (256, (5, 6)),
    (384, (7,)),
    (512, (8,)),
    (640, (9, 10, 11)),
    (768, (12,)),
    (896, (13, 14, 15)),
)


def attend_kernel(q_ref, k_mine, k_other, v_mine, v_other, out_ref, fresh_ref=None):
    rows = q_ref.shape[0]
    scale = HEAD ** (-0.5)
    lane = lax.broadcasted_iota(jnp.int32, (rows, 256), 1)
    stat_lane = lax.broadcasted_iota(jnp.int32, (rows, STATS), 1)
    stats = jnp.zeros((rows, STATS), F32)
    blocks = [None] * (WIDTH // 128)

    def window(mine_ref, other_ref, first, start):
        cols = slice(start, start + 256)
        if fresh_ref is not None:
            n_own = fresh_ref.shape[0]
            pieces = [fresh_ref[:, first + start : first + start + 256], mine_ref[n_own:, cols]]
        else:
            pieces = [mine_ref[:, cols]]
        return jnp.concatenate(pieces + [other_ref[:, cols]], axis=0)

    def inside(start, head):
        first = head * HEAD - start
        return (lane >= first) & (lane < first + HEAD)

    for part in (WINDOWS[:4], WINDOWS[4:]):
        scores = []
        for start, heads in part:
            query = q_ref[:, start : start + 256]
            zero = jnp.zeros((), BF16)
            stack = [jnp.where(inside(start, head), query, zero) for head in heads]
            scores.append(
                lax.dot_general(
                    jnp.concatenate(stack, axis=0),
                    window(k_mine, k_other, WIDTH, start),
                    (((1,), (1,)), ((), ())),
                    preferred_element_type=F32,
                )
            )
        tops = [jnp.max(s, axis=-1, keepdims=True) for s in scores]
        expos = [jnp.exp((s - t) * scale) for s, t in zip(scores, tops)]
        totals = [jnp.sum(e, axis=-1, keepdims=True) for e in expos]
        for (start, heads), top, expo, total in zip(part, tops, expos, totals):
            value = jnp.dot(
                expo.astype(BF16),
                window(v_mine, v_other, 2 * WIDTH, start),
                preferred_element_type=F32,
            )
            value = value * (1.0 / total)
            stat = top * scale + jnp.log(total)
            for n, head in enumerate(heads):
                mine = slice(n * rows, (n + 1) * rows)
                picked = jnp.where(inside(start, head), value[mine], 0.0)
                for j in (0, 1):
                    block = start // 128 + j
                    piece = picked[:, 128 * j : 128 * j + 128]
                    blocks[block] = piece if blocks[block] is None else blocks[block] + piece
                stats = jnp.where(stat_lane % HEADS == head, stat[mine], stats)
    high = stats.astype(BF16)
    rest = stats - high.astype(F32)
    middle = rest.astype(BF16)
    low = (rest - middle.astype(F32)).astype(BF16)
    split = stat_lane // HEADS
    packed = jnp.where(split == 2, low.astype(F32), 0.0)
    packed = jnp.where(split == 1, middle.astype(F32), packed)
    packed = jnp.where(split == 0, high.astype(F32), packed)
    for block, values in enumerate(blocks):
        out_ref[:, 128 * block : 128 * block + 128] = values.astype(BF16)
    out_ref[:, WIDTH:] = packed.astype(BF16)


def attend_cost(rows, keys):
    return pl.CostEstimate(
        flops=4 * HEADS * rows * keys * 256,
        bytes_accessed=4 * keys * WIDTH,
        transcendentals=HEADS * rows * keys,
    )


def attend(query, keyval):
    rows = query.shape[0]
    return pl.pallas_call(
        attend_kernel,
        in_specs=[pl.BlockSpec(memory_space=pltpu.VMEM)] * 5,
        out_specs=pl.BlockSpec(memory_space=pltpu.VMEM),
        out_shape=jax.ShapeDtypeStruct((rows, WIDTH + STATS), BF16),
        compiler_params=pltpu.CompilerParams(vmem_limit_bytes=VMEM_LIMIT),
        cost_estimate=attend_cost(rows, 2 * keyval[0].shape[0]),
        name="attend",
    )(query, *keyval)


def attend_own_kernel(
    q_ref, k_mine, k_other, v_mine, v_other, fresh_ref, time_ref, latent_ref,
    out_ref, base_ref, gain_ref,
):
    image = lax.axis_index("guide")
    now = jnp.full(latent_ref.shape, time_ref[image // 2], jnp.int32)
    bar_now = alpha_bar(now)
    bar_prev = alpha_bar(now - STRIDE)
    latent_gain = jnp.sqrt(bar_prev) / jnp.sqrt(bar_now)
    noise_gain = jnp.sqrt(1.0 - bar_prev) - latent_gain * jnp.sqrt(1.0 - bar_now)
    is_cond = jnp.full(latent_ref.shape, image % 2, jnp.int32) == 0
    base_ref[...] = latent_gain * latent_ref[...]
    gain_ref[0] = noise_gain * jnp.where(is_cond, 4.5, -3.5)
    gain_ref[1] = noise_gain * jnp.where(is_cond, -3.5, 4.5)
    attend_kernel(q_ref, k_mine, k_other, v_mine, v_other, out_ref, fresh_ref)


def attend_own(query, keyval, fresh, timestep, latent):
    rows = query.shape[0]
    vmem = pl.BlockSpec(memory_space=pltpu.VMEM)
    return pl.pallas_call(
        attend_own_kernel,
        in_specs=[vmem] * 6 + [pl.BlockSpec(memory_space=pltpu.SMEM), vmem],
        out_specs=[vmem] * 3,
        out_shape=[
            jax.ShapeDtypeStruct((rows, WIDTH + STATS), BF16),
            jax.ShapeDtypeStruct(latent.shape, F32),
            jax.ShapeDtypeStruct((2, *latent.shape), F32),
        ],
        compiler_params=pltpu.CompilerParams(vmem_limit_bytes=VMEM_LIMIT),
        cost_estimate=attend_cost(rows, 2 * keyval[0].shape[0]),
        name="attend_own",
    )(query, *keyval, fresh, timestep, latent)


def post_kernel(
    p0, p1, p2, p3, hidden_ref, mod_ref, w_out_ref, w_final_ref, scaled_ref, gain_ref,
    pick_ref, noise_ref, base_ref,
):
    pick = pick_ref[...]
    parts = (p0, p1, p2, p3)
    sums = [jnp.dot(p[:, WIDTH:], pick, preferred_element_type=F32) for p in parts]
    top = functools.reduce(jnp.maximum, sums)
    weights = [jnp.exp(s - top) for s in sums]
    total = functools.reduce(jnp.add, weights)
    mix = functools.reduce(
        jnp.add, [w * p[:, :WIDTH].astype(F32) for w, p in zip(weights, parts)]
    )
    attended = (mix / total).astype(BF16)
    source = hidden_ref[...].astype(F32)
    mixed = source + mod_ref[2] * jnp.dot(
        attended, w_out_ref[...], preferred_element_type=F32
    )
    final_in = (layer_norm(mixed) * (1.0 + mod_ref[4]) + mod_ref[3]).astype(BF16)
    w_wide = jnp.concatenate([w_final_ref[...]] * 8, axis=0)
    wide = lax.dot_general(
        final_in, w_wide, (((1,), (1,)), ((), ())), preferred_element_type=F32
    )
    rows = wide.shape[0]
    token = lax.broadcasted_iota(jnp.int32, wide.shape, 0) % 8
    place = lax.broadcasted_iota(jnp.int32, wide.shape, 1) // 16
    wide = jnp.where(token == place, wide, 0.0)
    noise = jnp.sum(wide.reshape(rows // 8, 8, 128), axis=1)
    noise_ref[...] = noise
    base_ref[...] = scaled_ref[...] + gain_ref[0] * noise


def post(parts, hidden, mod, w_out, w_final_t, scaled, gain, pick):
    rows = parts[0].shape[0]
    return pl.pallas_call(
        post_kernel,
        in_specs=[pl.BlockSpec(memory_space=pltpu.VMEM)] * 11,
        out_specs=[pl.BlockSpec(memory_space=pltpu.VMEM)] * 2,
        out_shape=[jax.ShapeDtypeStruct(scaled.shape, F32)] * 2,
        compiler_params=pltpu.CompilerParams(vmem_limit_bytes=VMEM_LIMIT),
        cost_estimate=pl.CostEstimate(
            flops=2 * rows * WIDTH * WIDTH, bytes_accessed=2 * WIDTH * WIDTH, transcendentals=0
        ),
        name="post",
    )(*parts, hidden, mod, w_out, w_final_t, scaled, gain, pick)


def body(hidden_in, stale_in, modulation, latent, timestep, w_qkv, w_out, w_final):
    hidden, stale = hidden_in[0], stale_in[0]
    mod = jnp.transpose(modulation, (1, 0, 2))
    rows = hidden.shape[0]

    stale, pick = lax.optimization_barrier((stale, head_selector()))
    stale_z = [send(stale, dz=k) for k in (2, 1, 3)]
    fresh = project_fresh(hidden, mod, w_qkv)
    query = fresh[:, :WIDTH]
    query_y = [send(query, dy=k) for k in (2, 1, 3)]

    blocks = [stale] + stale_z
    blocks, query_y[0] = lax.optimization_barrier((blocks, query_y[0]))
    k_mine = project_stale(blocks, w_qkv, WIDTH, "stale_keys")
    k_other = send(k_mine, dc=1)
    blocks, k_mine, query_y = lax.optimization_barrier((blocks, k_mine, query_y))
    v_mine = project_stale(blocks, w_qkv, 2 * WIDTH, "stale_values")
    v_other = send(v_mine, dc=1)
    keyval = (k_mine, k_other, v_mine, v_other)

    partial = attend(jnp.concatenate(query_y, axis=0), keyval)
    back = [
        send(partial[n * rows : (n + 1) * rows], dy=-k) for n, k in enumerate((2, 1, 3))
    ]
    own, scaled, gain = attend_own(query, keyval, fresh, timestep, latent[0])
    noise, base = post([own] + back, hidden, mod, w_out, w_final.T, scaled, gain, pick)
    partner = lax.ppermute(
        noise, "guide", [(i, i ^ 1) for i in range(lax.axis_size("guide"))]
    )
    return (base + gain[1] * partner)[None]


def solution(mesh):
    in_specs = (
        P("guide", "patch", None),
        P("guide", "patch", None),
        P("guide", None, None),
        P("guide", "patch", None),
        P(),
        P(),
        P(),
        P(),
    )
    out_specs = P("guide", "patch", None)
    return jax.shard_map(body, mesh=mesh, in_specs=in_specs, out_specs=out_specs, check_vma=False)
```

time: 67.2 us -> 48.6 us (0.72)
  Pallas kernels: 32.8 us -> 10.3 us
  waiting for transfers between devices: 1.94 us -> 14.1 us
  local copies, waits for them, and re-layouts: 4.34 us -> 0.92 us
  matrix products: 3.41 us -> 0 us
  between operations: 1.87 us -> 0.15 us
    pallas_call x5 -> x6, Pallas kernels: 30.2 us -> 8.82 us  [the longest x1 2.87 us: attend(): pl.pallas_call(attend_kernel, in_specs=[pl.BlockSpec(memory_space=pltpu.V...]
    ppermute x10 -> x11, waiting for transfers between devices: 1.94 us -> 12.2 us  [send(): return lax.ppermute(value, 'patch', patch_pairs(dy, dz, dc))]
    dot_general x1 -> x0, matrix products: 3.41 us -> none  [body(): jnp.dot(keys_in, w_qkv[:, WIDTH:], preferred_element_type=F32).astype(BF16)]
    ppermute x1, waiting for transfers between devices: 0.01 us -> 1.95 us  [body(): lax.ppermute(noise, 'guide', [(i, i ^ 1) for i in range(lax.axis_size('gu...]
    another operation x2 -> x0, local copies, waits for them, and re-layouts: 1.9 us -> none  [body(): w_final_wide = jnp.tile(w_final, (1, 8))]
    pallas_call x1, Pallas kernels: 2.53 us -> 1.51 us  [post(): pl.pallas_call(post_kernel, in_specs=[pl.BlockSpec(memory_space=pltpu.VME...]
    unnamed x21 -> x16, local copies, waits for them, and re-layouts: 1.75 us -> 0.87 us
    ppermute x10 -> x11, starting transfers between devices: 16.5 us -> 16.7 us  [send(): return lax.ppermute(value, 'patch', patch_pairs(dy, dz, dc))]
  transfers between devices with their start and end apart: 11 -> 12, of which waited for: 1 -> 8; matrix products, arithmetic and copies ran while one was open for 10% -> 0% of each run, Pallas kernels for 45% -> 10%
where the time goes in v2:
time: 48.6 us; the launch traced here: 48.5 us
  starting transfers between devices  22.3 us (46%)
  waiting for transfers between devices  14.1 us (29%)
  Pallas kernels  10.3 us (21%)
  local copies, waits for them, and re-layouts  0.92 us (2%)
  other arithmetic  0.63 us (1%)
    ppermute x11, starting transfers between devices, send(): return lax.ppermute(value, 'patch', patch_pairs(dy, dz, dc))  16.7 us
    ppermute x11, waiting for transfers between devices, send(): return lax.ppermute(value, 'patch', patch_pairs(dy, dz, dc))  12.2 us
    ppermute x1, starting transfers between devices, body(): lax.ppermute(noise, 'guide', [(i, i ^ 1) for i in range(lax.axis_size('gu...  5.65 us
    pallas_call x1, Pallas kernels, attend(): pl.pallas_call(attend_kernel, in_specs=[pl.BlockSpec(memory_space=pltpu.V...  2.87 us
    pallas_call x2, Pallas kernels, project_stale(): pl.pallas_call(functools.partial(stale_kernel, first), in_specs=[pl.Block...  2.27 us
    pallas_call x1, Pallas kernels, attend_own(): pl.pallas_call(attend_own_kernel, in_specs=[vmem] * 6 + [pl.BlockSpec(mem...  2.11 us
    ppermute x1, waiting for transfers between devices, body(): lax.ppermute(noise, 'guide', [(i, i ^ 1) for i in range(lax.axis_size('gu...  1.95 us
    pallas_call x1, Pallas kernels, project_fresh(): pl.pallas_call(fresh_kernel, in_specs=[pl.BlockSpec(memory_space=pltpu.VM...  1.53 us
  transfers between devices with their start and end apart: 12, of which 8 were waited for; matrix products, arithmetic and copies ran while one was open for 0% of the time, Pallas kernels for 10%

profile of v2, /device:TPU:2, one launch (start us, length us, event | category | flops | bytes accessed | tf_op | source)
XLA Modules:
  0.0 48.5 jit_solution(16043300999626853361)
XLA Ops:
  0.1 0.8 %copy-done.3 = bf16[1,64,1152]{2,1,0:T(8,128)(2,1)S(1)} copy-done((bf16[1,64,1152]{2,1,0:T(8,128)(2,1)S(1)}, bf16[1,64,1152]{2,1,0:T(8,128)(2,1)}, u32[]{:S(2)}) %copy-start.3) | copy-done | bytes 147480
  0.9 4.6 %collective-permute-start.2 = (bf16[64,1152]{1,0:T(8,128)(2,1)S(1)}, bf16[64,1152]{1,0:T(8,128)(2,1)S(1)}, u32[]{:S(2)}, u32[]{:S(2)}) collective-permute-start(bf16[64,1152]{1,0:T(8,128)(2,1)S(1)} %bitcast.15), channel_id=1, source_target_pairs={{0,48},{8,56},{16,0},{24,8},{32,16},{40,24},{48,32},{56,40},{64,11... | collective-permute-start | bytes 442376 | tf_op jit(solution)/shard_map/ppermute | solution.py:45
  5.5 0.7 %collective-permute-start = (bf16[64,1152]{1,0:T(8,128)(2,1)S(1)}, bf16[64,1152]{1,0:T(8,128)(2,1)S(1)}, u32[]{:S(2)}, u32[]{:S(2)}) collective-permute-start(bf16[64,1152]{1,0:T(8,128)(2,1)S(1)} %bitcast.17), channel_id=1, source_target_pairs={{0,32},{8,40},{16,48},{24,56},{32,0},{40,8},{48,16},{56,24},{64,96... | collective-permute-start | bytes 442376 | tf_op jit(solution)/shard_map/ppermute | solution.py:45
  6.2 1.5 %fresh_qkv.1.fresh_ref = bf16[64,3456]{1,0:T(8,128)(2,1)S(1)} custom-call(bf16[64,1152]{1,0:T(8,128)(2,1)S(1)} %bitcast.13, f32[5,1,1152]{2,1,0:T(1,128)S(1)} %bitcast.20, bf16[1152,3456]{1,0:T(8,128)(2,1)S(1)} %copy-done), custom_call_target="tpu_custom_call" | custom-call | flops 509607936 | bytes 7962624 | tf_op jit(solution)/shard_map/fresh_qkv/pallas_call | solution.py:81
  7.8 3.3 %collective-permute-start.3 = (bf16[64,1152]{1,0:T(8,128)(2,1)S(1)}, bf16[64,1152]{1,0:T(8,128)(2,1)S(1)}, u32[]{:S(2)}, u32[]{:S(2)}) collective-permute-start(bf16[64,1152]{1,0:T(8,128)(2,1)S(1)} %slice.20.q_ref), channel_id=1, source_target_pairs={{0,128},{8,136},{16,144},{24,152},{32,160},{40,168},{48,176},{56,1... | collective-permute-start | bytes 442376 | tf_op jit(solution)/shard_map/ppermute | solution.py:45
  11.1 1.1 %collective-permute-start.5 = (bf16[64,1152]{1,0:T(8,128)(2,1)S(1)}, bf16[64,1152]{1,0:T(8,128)(2,1)S(1)}, u32[]{:S(2)}, u32[]{:S(2)}) collective-permute-start(bf16[64,1152]{1,0:T(8,128)(2,1)S(1)} %slice.20.q_ref), channel_id=1, source_target_pairs={{0,192},{8,200},{16,208},{24,216},{32,224},{40,232},{48,240},{56,2... | collective-permute-start | bytes 442376 | tf_op jit(solution)/shard_map/ppermute | solution.py:45
  12.1 0.0 collective-permute-done.2.x3
  12.1 1.0 %collective-permute-start.4 = (bf16[64,1152]{1,0:T(8,128)(2,1)S(1)}, bf16[64,1152]{1,0:T(8,128)(2,1)S(1)}, u32[]{:S(2)}, u32[]{:S(2)}) collective-permute-start(bf16[64,1152]{1,0:T(8,128)(2,1)S(1)} %slice.20.q_ref), channel_id=1, source_target_pairs={{0,64},{8,72},{16,80},{24,88},{32,96},{40,104},{48,112},{56,120},{... | collective-permute-start | bytes 442376 | tf_op jit(solution)/shard_map/ppermute | solution.py:45
  13.1 1.1 %collective-permute-done.1.x2 = bf16[64,1152]{1,0:T(8,128)(2,1)S(1)} collective-permute-done((bf16[64,1152]{1,0:T(8,128)(2,1)S(1)}, bf16[64,1152]{1,0:T(8,128)(2,1)S(1)}, u32[]{:S(2)}, u32[]{:S(2)}) %collective-permute-start.1) | collective-permute-done | bytes 147488 | tf_op jit(solution)/shard_map/ppermute | solution.py:45
  14.2 3.9 %collective-permute-done.x1 = bf16[64,1152]{1,0:T(8,128)(2,1)S(1)} collective-permute-done((bf16[64,1152]{1,0:T(8,128)(2,1)S(1)}, bf16[64,1152]{1,0:T(8,128)(2,1)S(1)}, u32[]{:S(2)}, u32[]{:S(2)}) %collective-permute-start) | collective-permute-done | bytes 147488 | tf_op jit(solution)/shard_map/ppermute | solution.py:45
  18.1 1.1 %stale_keys.1.k_mine = bf16[256,1152]{1,0:T(8,128)(2,1)S(1)} custom-call(bf16[64,1152]{1,0:T(8,128)(2,1)S(1)} %bitcast.18, bf16[64,1152]{1,0:T(8,128)(2,1)S(1)} %collective-permute-done.x1, bf16[64,1152]{1,0:T(8,128)(2,1)S(1)} %collective-permute-done.1.x2, bf16[64,1152]{1,0:T(8,128)(2,1)S(1)} %collective-permute-done.2.x3, bf16[1152,3456]{1,0:T(8,128)(2,1)S(1)} %copy-done), custom_call_target="tpu_custom_call" | custom-call | flops 679477248 | bytes 2654208 | tf_op jit(solution)/shard_map/stale_keys/pallas_call | solution.py:107
  19.2 0.0 copy-start.6
  19.2 0.0 copy-start.7
  19.2 0.0 copy-start.1
  19.2 0.0 copy-start.5
  19.3 1.1 %stale_values.1.v_mine = bf16[256,1152]{1,0:T(8,128)(2,1)S(1)} custom-call(bf16[64,1152]{1,0:T(8,128)(2,1)S(1)} %bitcast.19, bf16[64,1152]{1,0:T(8,128)(2,1)S(1)} %collective-permute-done.x1, bf16[64,1152]{1,0:T(8,128)(2,1)S(1)} %collective-permute-done.1.x2, bf16[64,1152]{1,0:T(8,128)(2,1)S(1)} %collective-permute-done.2.x3, bf16[1152,3456]{1,0:T(8,128)(2,1)S(1)} %copy-done), custom_call_target="tpu_custom_call" | custom-call | flops 679477248 | bytes 2654208 | tf_op jit(solution)/shard_map/stale_values/pallas_call | solution.py:107
  20.4 0.1 collective-permute-start.7
  20.5 0.5 %collective-permute-start.6 = (bf16[256,1152]{1,0:T(8,128)(2,1)S(1)}, bf16[256,1152]{1,0:T(8,128)(2,1)S(1)}, u32[]{:S(2)}, u32[]{:S(2)}) collective-permute-start(bf16[256,1152]{1,0:T(8,128)(2,1)S(1)} %stale_keys.1.k_mine), channel_id=1, source_target_pairs={{0,8},{8,0},{16,24},{24,16},{32,40},{40,32},{48,56},{56,48},{64,72... | collective-permute-start | bytes 1769480 | tf_op jit(solution)/shard_map/ppermute | solution.py:45
  21.1 1.5 %collective-permute-done.7.v_other = bf16[256,1152]{1,0:T(8,128)(2,1)S(1)} collective-permute-done((bf16[256,1152]{1,0:T(8,128)(2,1)S(1)}, bf16[256,1152]{1,0:T(8,128)(2,1)S(1)}, u32[]{:S(2)}, u32[]{:S(2)}) %collective-permute-start.7) | collective-permute-done | bytes 589856 | tf_op jit(solution)/shard_map/ppermute | solution.py:45
  22.5 0.8 %collective-permute-done.6.k_other = bf16[256,1152]{1,0:T(8,128)(2,1)S(1)} collective-permute-done((bf16[256,1152]{1,0:T(8,128)(2,1)S(1)}, bf16[256,1152]{1,0:T(8,128)(2,1)S(1)}, u32[]{:S(2)}, u32[]{:S(2)}) %collective-permute-start.6) | collective-permute-done | bytes 589856 | tf_op jit(solution)/shard_map/ppermute | solution.py:45
  23.4 2.9 %attend.1 = bf16[192,1280]{1,0:T(8,128)(2,1)S(1)} custom-call(bf16[192,1152]{1,0:T(8,128)(2,1)S(1)} %pad_maximum_fusion.q_ref, bf16[256,1152]{1,0:T(8,128)(2,1)S(1)} %stale_keys.1.k_mine, bf16[256,1152]{1,0:T(8,128)(2,1)S(1)} %collective-permute-done.6.k_other, bf16[256,1152]{1,0:T(8,128)(2,1)S(1)} %stale_values.1.v_mine, ...), custom_call_target="tpu_custom_call" | custom-call | flops 1610612736 | bytes 2359296 | tf_op jit(solution)/shard_map/attend/pallas_call | solution.py:209
  26.3 1.8 %collective-permute-start.10 = (bf16[64,1280]{1,0:T(8,128)(2,1)S(1)}, bf16[64,1280]{1,0:T(8,128)(2,1)S(1)}, u32[]{:S(2)}, u32[]{:S(2)}) collective-permute-start(bf16[64,1280]{1,0:T(8,128)(2,1)S(1)} %get-tuple-element.45), channel_id=1, source_target_pairs={{0,64},{8,72},{16,80},{24,88},{32,96},{40,104},{48,112},{56,120},{... | collective-permute-start | bytes 491528 | tf_op jit(solution)/shard_map/ppermute | solution.py:45
  28.1 1.7 %collective-permute-start.9 = (bf16[64,1280]{1,0:T(8,128)(2,1)S(1)}, bf16[64,1280]{1,0:T(8,128)(2,1)S(1)}, u32[]{:S(2)}, u32[]{:S(2)}) collective-permute-start(bf16[64,1280]{1,0:T(8,128)(2,1)S(1)} %get-tuple-element.46), channel_id=1, source_target_pairs={{0,192},{8,200},{16,208},{24,216},{32,224},{40,232},{48,240},{56,2... | collective-permute-start | bytes 491528 | tf_op jit(solution)/shard_map/ppermute | solution.py:45
  29.8 2.0 %collective-permute-start.8 = (bf16[64,1280]{1,0:T(8,128)(2,1)S(1)}, bf16[64,1280]{1,0:T(8,128)(2,1)S(1)}, u32[]{:S(2)}, u32[]{:S(2)}) collective-permute-start(bf16[64,1280]{1,0:T(8,128)(2,1)S(1)} %get-tuple-element.47), channel_id=1, source_target_pairs={{0,128},{8,136},{16,144},{24,152},{32,160},{40,168},{48,176},{56,1... | collective-permute-start | bytes 491528 | tf_op jit(solution)/shard_map/ppermute | solution.py:45
  31.8 2.1 %attend_own.1 = (bf16[64,1280]{1,0:T(8,128)(2,1)S(1)}, f32[8,128]{1,0:T(8,128)S(1)}, f32[2,8,128]{2,1,0:T(8,128)S(1)}) custom-call(bf16[64,1152]{1,0:T(8,128)(2,1)S(1)} %slice.20.q_ref, bf16[256,1152]{1,0:T(8,128)(2,1)S(1)} %stale_keys.1.k_mine, bf16[256,1152]{1,0:T(8,128)(2,1)S(1)} %collective-permute-done.6.k_other, ...), custom_call_target="tpu_custom_call" | custom-call | flops 536870912 | bytes 2359296 | tf_op jit(solution)/shard_map/attend_own/pallas_call | solution.py:240
  33.9 0.2 collective-permute-done.10.p3
  34.0 2.9 %collective-permute-done.9.p2 = bf16[64,1280]{1,0:T(8,128)(2,1)S(1)} collective-permute-done((bf16[64,1280]{1,0:T(8,128)(2,1)S(1)}, bf16[64,1280]{1,0:T(8,128)(2,1)S(1)}, u32[]{:S(2)}, u32[]{:S(2)}) %collective-permute-start.9) | collective-permute-done | bytes 163872 | tf_op jit(solution)/shard_map/ppermute | solution.py:45
  36.9 1.8 %collective-permute-done.8.p1 = bf16[64,1280]{1,0:T(8,128)(2,1)S(1)} collective-permute-done((bf16[64,1280]{1,0:T(8,128)(2,1)S(1)}, bf16[64,1280]{1,0:T(8,128)(2,1)S(1)}, u32[]{:S(2)}, u32[]{:S(2)}) %collective-permute-start.8) | collective-permute-done | bytes 163872 | tf_op jit(solution)/shard_map/ppermute | solution.py:45
  38.7 1.5 %post.1 = (f32[8,128]{1,0:T(8,128)S(1)}, f32[8,128]{1,0:T(8,128)S(1)}) custom-call(bf16[64,1280]{1,0:T(8,128)(2,1)S(1)} %get-tuple-element.36.p0, bf16[64,1280]{1,0:T(8,128)(2,1)S(1)} %collective-permute-done.8.p1, bf16[64,1280]{1,0:T(8,128)(2,1)S(1)} %collective-permute-done.9.p2, bf16[64,1280]{1,0:T(8,128)(2,1)S(1)} %collective-permute-done.10.p3, ...), custom_call_target="tpu_custom_call" | custom-call | flops 169869312 | bytes 2654208 | tf_op jit(solution)/shard_map/post/pallas_call | solution.py:289
  40.3 5.6 %collective-permute-start.11 = (f32[8,128]{1,0:T(8,128)S(1)}, f32[8,128]{1,0:T(8,128)S(1)}, u32[]{:S(2)}, u32[]{:S(2)}) collective-permute-start(f32[8,128]{1,0:T(8,128)S(1)} %get-tuple-element.44), channel_id=1, source_target_pairs={{0,1},{1,0},{2,3},{3,2},{4,5},{5,4},{6,7},{7,6},{8,9},{9,8},{10,11... | collective-permute-start | bytes 12296 | tf_op jit(solution)/shard_map/ppermute | solution.py:328
  45.9 2.0 %collective-permute-done.11 = f32[8,128]{1,0:T(8,128)S(1)} collective-permute-done((f32[8,128]{1,0:T(8,128)S(1)}, f32[8,128]{1,0:T(8,128)S(1)}, u32[]{:S(2)}, u32[]{:S(2)}) %collective-permute-start.11) | collective-permute-done | bytes 4128 | tf_op jit(solution)/shard_map/ppermute | solution.py:328
  47.9 0.6 %fusion.1 = f32[1,8,128]{2,1,0:T(8,128)} fusion(f32[8,128]{1,0:T(8,128)S(1)} %get-tuple-element.43, f32[8,128]{1,0:T(8,128)S(1)} %collective-permute-done.11, f32[2,8,128]{2,1,0:T(8,128)S(1)} %get-tuple-element.41.gain_ref), kind=kLoop, calls=%fused_computation.3 | loop fusion | flops 2048 | bytes 16384 | tf_op jit(solution)/shard_map/broadcast_in_dim | solution.py:331
  (19 shorter events, 0.2 us)
Async XLA Ops:
  0.0 0.9 %copy-start.3 = (bf16[1,64,1152]{2,1,0:T(8,128)(2,1)S(1)}, bf16[1,64,1152]{2,1,0:T(8,128)(2,1)}, u32[]{:S(2)}) copy-start(bf16[1,64,1152]{2,1,0:T(8,128)(2,1)} %param.9) | copy-start | bytes 442372
  0.0 6.2 %copy-start = (bf16[1152,3456]{1,0:T(8,128)(2,1)S(1)}, bf16[1152,3456]{1,0:T(8,128)(2,1)}, u32[]{:S(2)}) copy-start(bf16[1152,3456]{1,0:T(8,128)(2,1)} %w_ref.5) | copy-start | bytes 23887876
  0.0 6.2 %copy-start.4 = (f32[1,5,1152]{2,0,1:T(1,128)S(1)}, f32[1,5,1152]{2,0,1:T(1,128)}, u32[]{:S(2)}) copy-start(f32[1,5,1152]{2,0,1:T(1,128)} %param.10) | copy-start | bytes 69124
  0.0 6.2 %copy-start.2 = (bf16[1,64,1152]{2,1,0:T(8,128)(2,1)S(1)}, bf16[1,64,1152]{2,1,0:T(8,128)(2,1)}, u32[]{:S(2)}) copy-start(bf16[1,64,1152]{2,1,0:T(8,128)(2,1)} %param.8) | copy-start | bytes 442372
  0.9 11.2 %collective-permute-start.2 = (bf16[64,1152]{1,0:T(8,128)(2,1)S(1)}, bf16[64,1152]{1,0:T(8,128)(2,1)S(1)}, u32[]{:S(2)}, u32[]{:S(2)}) collective-permute-start(bf16[64,1152]{1,0:T(8,128)(2,1)S(1)} %bitcast.15), channel_id=1, source_target_pairs={{0,48},{8,56},{16,0},{24,8},{32,16},{40,24},{48,32},{56,40},{64,11... | collective-permute-start | bytes 442376 | tf_op jit(solution)/shard_map/ppermute | solution.py:45
  5.5 8.6 %collective-permute-start.1 = (bf16[64,1152]{1,0:T(8,128)(2,1)S(1)}, bf16[64,1152]{1,0:T(8,128)(2,1)S(1)}, u32[]{:S(2)}, u32[]{:S(2)}) collective-permute-start(bf16[64,1152]{1,0:T(8,128)(2,1)S(1)} %bitcast.16), channel_id=1, source_target_pairs={{0,16},{8,24},{16,32},{24,40},{32,48},{40,56},{48,0},{56,8},{64,80... | collective-permute-start | bytes 442376 | tf_op jit(solution)/shard_map/ppermute | solution.py:45
  5.5 12.5 %collective-permute-start = (bf16[64,1152]{1,0:T(8,128)(2,1)S(1)}, bf16[64,1152]{1,0:T(8,128)(2,1)S(1)}, u32[]{:S(2)}, u32[]{:S(2)}) collective-permute-start(bf16[64,1152]{1,0:T(8,128)(2,1)S(1)} %bitcast.17), channel_id=1, source_target_pairs={{0,32},{8,40},{16,48},{24,56},{32,0},{40,8},{48,16},{56,24},{64,96... | collective-permute-start | bytes 442376 | tf_op jit(solution)/shard_map/ppermute | solution.py:45
  7.8 10.3 %collective-permute-start.3 = (bf16[64,1152]{1,0:T(8,128)(2,1)S(1)}, bf16[64,1152]{1,0:T(8,128)(2,1)S(1)}, u32[]{:S(2)}, u32[]{:S(2)}) collective-permute-start(bf16[64,1152]{1,0:T(8,128)(2,1)S(1)} %slice.20.q_ref), channel_id=1, source_target_pairs={{0,128},{8,136},{16,144},{24,152},{32,160},{40,168},{48,176},{56,1... | collective-permute-start | bytes 442376 | tf_op jit(solution)/shard_map/ppermute | solution.py:45
  11.1 8.2 %collective-permute-start.5 = (bf16[64,1152]{1,0:T(8,128)(2,1)S(1)}, bf16[64,1152]{1,0:T(8,128)(2,1)S(1)}, u32[]{:S(2)}, u32[]{:S(2)}) collective-permute-start(bf16[64,1152]{1,0:T(8,128)(2,1)S(1)} %slice.20.q_ref), channel_id=1, source_target_pairs={{0,192},{8,200},{16,208},{24,216},{32,224},{40,232},{48,240},{56,2... | collective-permute-start | bytes 442376 | tf_op jit(solution)/shard_map/ppermute | solution.py:45
  12.1 7.2 %collective-permute-start.4 = (bf16[64,1152]{1,0:T(8,128)(2,1)S(1)}, bf16[64,1152]{1,0:T(8,128)(2,1)S(1)}, u32[]{:S(2)}, u32[]{:S(2)}) collective-permute-start(bf16[64,1152]{1,0:T(8,128)(2,1)S(1)} %slice.20.q_ref), channel_id=1, source_target_pairs={{0,64},{8,72},{16,80},{24,88},{32,96},{40,104},{48,112},{56,120},{... | collective-permute-start | bytes 442376 | tf_op jit(solution)/shard_map/ppermute | solution.py:45
  19.2 12.5 %copy-start.6 = (f32[1,8,128]{2,1,0:T(8,128)S(1)}, f32[1,8,128]{2,1,0:T(8,128)}, u32[]{:S(2)}) copy-start(f32[1,8,128]{2,1,0:T(8,128)} %param.11) | copy-start | bytes 12292
  19.2 12.5 %copy-start.7 = (s32[4]{0:T(128)S(1)}, s32[4]{0:T(128)}, u32[]{:S(2)}) copy-start(s32[4]{0:T(128)} %time_ref.1) | copy-start | bytes 52
  19.2 19.5 %copy-start.1 = (bf16[1152,1152]{1,0:T(8,128)(2,1)S(1)}, bf16[1152,1152]{1,0:T(8,128)(2,1)}, u32[]{:S(2)}) copy-start(bf16[1152,1152]{1,0:T(8,128)(2,1)} %w_out_ref.1) | copy-start | bytes 7962628
  19.2 19.5 %copy-start.5 = (bf16[1152,16]{0,1:T(8,128)(2,1)S(1)}, bf16[1152,16]{0,1:T(8,128)(2,1)}, u32[]{:S(2)}) copy-start(bf16[1152,16]{0,1:T(8,128)(2,1)} %param.15) | copy-start | bytes 110596
  20.4 2.1 %collective-permute-start.7 = (bf16[256,1152]{1,0:T(8,128)(2,1)S(1)}, bf16[256,1152]{1,0:T(8,128)(2,1)S(1)}, u32[]{:S(2)}, u32[]{:S(2)}) collective-permute-start(bf16[256,1152]{1,0:T(8,128)(2,1)S(1)} %stale_values.1.v_mine), channel_id=1, source_target_pairs={{0,8},{8,0},{16,24},{24,16},{32,40},{40,32},{48,56},{56,48},{64,72... | collective-permute-start | bytes 1769480 | tf_op jit(solution)/shard_map/ppermute | solution.py:45
  20.5 2.8 %collective-permute-start.6 = (bf16[256,1152]{1,0:T(8,128)(2,1)S(1)}, bf16[256,1152]{1,0:T(8,128)(2,1)S(1)}, u32[]{:S(2)}, u32[]{:S(2)}) collective-permute-start(bf16[256,1152]{1,0:T(8,128)(2,1)S(1)} %stale_keys.1.k_mine), channel_id=1, source_target_pairs={{0,8},{8,0},{16,24},{24,16},{32,40},{40,32},{48,56},{56,48},{64,72... | collective-permute-start | bytes 1769480 | tf_op jit(solution)/shard_map/ppermute | solution.py:45
  26.3 7.8 %collective-permute-start.10 = (bf16[64,1280]{1,0:T(8,128)(2,1)S(1)}, bf16[64,1280]{1,0:T(8,128)(2,1)S(1)}, u32[]{:S(2)}, u32[]{:S(2)}) collective-permute-start(bf16[64,1280]{1,0:T(8,128)(2,1)S(1)} %get-tuple-element.45), channel_id=1, source_target_pairs={{0,64},{8,72},{16,80},{24,88},{32,96},{40,104},{48,112},{56,120},{... | collective-permute-start | bytes 491528 | tf_op jit(solution)/shard_map/ppermute | solution.py:45
  28.1 8.8 %collective-permute-start.9 = (bf16[64,1280]{1,0:T(8,128)(2,1)S(1)}, bf16[64,1280]{1,0:T(8,128)(2,1)S(1)}, u32[]{:S(2)}, u32[]{:S(2)}) collective-permute-start(bf16[64,1280]{1,0:T(8,128)(2,1)S(1)} %get-tuple-element.46), channel_id=1, source_target_pairs={{0,192},{8,200},{16,208},{24,216},{32,224},{40,232},{48,240},{56,2... | collective-permute-start | bytes 491528 | tf_op jit(solution)/shard_map/ppermute | solution.py:45
  29.8 9.0 %collective-permute-start.8 = (bf16[64,1280]{1,0:T(8,128)(2,1)S(1)}, bf16[64,1280]{1,0:T(8,128)(2,1)S(1)}, u32[]{:S(2)}, u32[]{:S(2)}) collective-permute-start(bf16[64,1280]{1,0:T(8,128)(2,1)S(1)} %get-tuple-element.47), channel_id=1, source_target_pairs={{0,128},{8,136},{16,144},{24,152},{32,160},{40,168},{48,176},{56,1... | collective-permute-start | bytes 491528 | tf_op jit(solution)/shard_map/ppermute | solution.py:45
  40.3 7.6 %collective-permute-start.11 = (f32[8,128]{1,0:T(8,128)S(1)}, f32[8,128]{1,0:T(8,128)S(1)}, u32[]{:S(2)}, u32[]{:S(2)}) collective-permute-start(f32[8,128]{1,0:T(8,128)S(1)} %get-tuple-element.44), channel_id=1, source_target_pairs={{0,1},{1,0},{2,3},{3,2},{4,5},{5,4},{6,7},{7,6},{8,9},{9,8},{10,11... | collective-permute-start | bytes 12296 | tf_op jit(solution)/shard_map/ppermute | solution.py:328

commit v3 on v2

--- a/solution.py
+++ b/solution.py
@@ -31,18 +31,26 @@
     return jnp.cos(angle) ** 2
 
 
-def patch_pairs(dy, dz, dc):
+def send(value, route):
     pairs = []
     for y in range(NY):
         for z in range(NZ):
             for c in range(NC):
-                target = (((y + dy) % NY) * NZ + (z + dz) % NZ) * NC + (c + dc) % NC
-                pairs.append(((y * NZ + z) * NC + c, target))
-    return pairs
-
-
-def send(value, dy=0, dz=0, dc=0):
-    return lax.ppermute(value, "patch", patch_pairs(dy, dz, dc))
+                ty, tz, tc = route(y, z, c)
+                pairs.append(((y * NZ + z) * NC + c, ((ty % NY) * NZ + tz) * NC + tc))
+    return lax.ppermute(value, "patch", pairs)
+
+
+def z_xor(mask):
+    return lambda y, z, c: (y, z ^ mask, c)
+
+
+def other_core(y, z, c):
+    return y, z, c ^ 1
+
+
+def y_shift(step):
+    return lambda y, z, c: (y + step, z, c)
 
 
 def selector_kernel(out_ref):
@@ -91,30 +99,60 @@
     )(hidden, mod, w_qkv)
 
 
-def stale_kernel(first, x0, x1, x2, x3, w_ref, out_ref):
-    keys = jnp.concatenate([x0[...], x1[...], x2[...], x3[...]], axis=0)
+def stale_kernel(*refs):
+    *blocks, w_ref, out_ref = refs
+    keys = jnp.concatenate([x[...] for x in blocks], axis=0)
     for start in range(0, out_ref.shape[1], CHUNK):
         out_ref[:, start : start + CHUNK] = jnp.dot(
             keys,
-            w_ref[:, first + start : first + start + CHUNK],
+            w_ref[:, WIDTH + start : WIDTH + start + CHUNK],
             preferred_element_type=F32,
         ).astype(BF16)
 
 
-def project_stale(blocks, w_qkv, first, name):
+def project_stale(blocks, w_qkv, flops):
     rows = len(blocks) * blocks[0].shape[0]
-    width = w_qkv.shape[0]
-    return pl.pallas_call(
-        functools.partial(stale_kernel, first),
-        in_specs=[pl.BlockSpec(memory_space=pltpu.VMEM)] * 5,
+    width, cols = w_qkv.shape
+    cols -= width
+    return pl.pallas_call(
+        stale_kernel,
+        in_specs=[pl.BlockSpec(memory_space=pltpu.VMEM)] * (len(blocks) + 1),
         out_specs=pl.BlockSpec(memory_space=pltpu.VMEM),
-        out_shape=jax.ShapeDtypeStruct((rows, width), BF16),
-        compiler_params=pltpu.CompilerParams(vmem_limit_bytes=VMEM_LIMIT),
-        cost_estimate=pl.CostEstimate(
-            flops=2 * rows * width * width, bytes_accessed=2 * width * width, transcendentals=0
-        ),
-        name=name,
+        out_shape=jax.ShapeDtypeStruct((rows, cols), BF16),
+        compiler_params=pltpu.CompilerParams(vmem_limit_bytes=VMEM_LIMIT),
+        cost_estimate=pl.CostEstimate(
+            flops=flops, bytes_accessed=1, transcendentals=0
+        ),
+        name="stale_kv",
     )(*blocks, w_qkv)
+
+
+def gather_kernel(counts, *refs):
+    first = 0
+    for out_ref, count in zip(refs[sum(counts) :], counts):
+        for n in range(count):
+            block = refs[first + n]
+            rows = block.shape[0]
+            out_ref[n * rows : (n + 1) * rows, :] = block[...]
+        first += count
+
+
+def gather_blocks(*groups):
+    blocks = [block for group in groups for block in group]
+    rows, width = blocks[0].shape
+    counts = tuple(len(group) for group in groups)
+    vmem = pl.BlockSpec(memory_space=pltpu.VMEM)
+    return pl.pallas_call(
+        functools.partial(gather_kernel, counts),
+        in_specs=[vmem] * len(blocks),
+        out_specs=[vmem] * len(groups),
+        out_shape=[jax.ShapeDtypeStruct((n * rows, width), BF16) for n in counts],
+        compiler_params=pltpu.CompilerParams(vmem_limit_bytes=4 * 1024 * 1024),
+        cost_estimate=pl.CostEstimate(
+            flops=2 * 10**10, bytes_accessed=4 * 10**7, transcendentals=0
+        ),
+        name="gather_blocks",
+    )(*blocks)
 
 
 WINDOWS = (
@@ -129,7 +167,19 @@
 )
 
 
-def attend_kernel(q_ref, k_mine, k_other, v_mine, v_other, out_ref, fresh_ref=None):
+def split_stats(stats, lane):
+    high = stats.astype(BF16)
+    rest = stats - high.astype(F32)
+    middle = rest.astype(BF16)
+    low = (rest - middle.astype(F32)).astype(BF16)
+    split = lane // HEADS
+    packed = jnp.where(split == 2, low.astype(F32), 0.0)
+    packed = jnp.where(split == 1, middle.astype(F32), packed)
+    return jnp.where(split == 0, high.astype(F32), packed)
+
+
+def attend_kernel(q_ref, *refs, fresh_ref=None):
+    *keyval, out_ref = refs
     rows = q_ref.shape[0]
     scale = HEAD ** (-0.5)
     lane = lax.broadcasted_iota(jnp.int32, (rows, 256), 1)
@@ -137,14 +187,14 @@
     stats = jnp.zeros((rows, STATS), F32)
     blocks = [None] * (WIDTH // 128)
 
-    def window(mine_ref, other_ref, first, start):
-        cols = slice(start, start + 256)
+    def window(first):
+        cols = slice(first, first + 256)
+        pieces = [ref[:, cols] for ref in keyval]
         if fresh_ref is not None:
             n_own = fresh_ref.shape[0]
-            pieces = [fresh_ref[:, first + start : first + start + 256], mine_ref[n_own:, cols]]
-        else:
-            pieces = [mine_ref[:, cols]]
-        return jnp.concatenate(pieces + [other_ref[:, cols]], axis=0)
+            own = fresh_ref[:, WIDTH + first : WIDTH + first + 256]
+            pieces[0:1] = [own, keyval[0][n_own:, cols]]
+        return jnp.concatenate(pieces, axis=0)
 
     def inside(start, head):
         first = head * HEAD - start
@@ -159,7 +209,7 @@
             scores.append(
                 lax.dot_general(
                     jnp.concatenate(stack, axis=0),
-                    window(k_mine, k_other, WIDTH, start),
+                    window(start),
                     (((1,), (1,)), ((), ())),
                     preferred_element_type=F32,
                 )
@@ -170,7 +220,7 @@
         for (start, heads), top, expo, total in zip(part, tops, expos, totals):
             value = jnp.dot(
                 expo.astype(BF16),
-                window(v_mine, v_other, 2 * WIDTH, start),
+                window(WIDTH + start),
                 preferred_element_type=F32,
             )
             value = value * (1.0 / total)
@@ -183,14 +233,7 @@
                     piece = picked[:, 128 * j : 128 * j + 128]
                     blocks[block] = piece if blocks[block] is None else blocks[block] + piece
                 stats = jnp.where(stat_lane % HEADS == head, stat[mine], stats)
-    high = stats.astype(BF16)
-    rest = stats - high.astype(F32)
-    middle = rest.astype(BF16)
-    low = (rest - middle.astype(F32)).astype(BF16)
-    split = stat_lane // HEADS
-    packed = jnp.where(split == 2, low.astype(F32), 0.0)
-    packed = jnp.where(split == 1, middle.astype(F32), packed)
-    packed = jnp.where(split == 0, high.astype(F32), packed)
+    packed = split_stats(stats, stat_lane)
     for block, values in enumerate(blocks):
         out_ref[:, 128 * block : 128 * block + 128] = values.astype(BF16)
     out_ref[:, WIDTH:] = packed.astype(BF16)
@@ -208,18 +251,17 @@
     rows = query.shape[0]
     return pl.pallas_call(
         attend_kernel,
-        in_specs=[pl.BlockSpec(memory_space=pltpu.VMEM)] * 5,
+        in_specs=[pl.BlockSpec(memory_space=pltpu.VMEM)] * (1 + len(keyval)),
         out_specs=pl.BlockSpec(memory_space=pltpu.VMEM),
         out_shape=jax.ShapeDtypeStruct((rows, WIDTH + STATS), BF16),
         compiler_params=pltpu.CompilerParams(vmem_limit_bytes=VMEM_LIMIT),
-        cost_estimate=attend_cost(rows, 2 * keyval[0].shape[0]),
+        cost_estimate=attend_cost(rows, sum(x.shape[0] for x in keyval)),
         name="attend",
     )(query, *keyval)
 
 
 def attend_own_kernel(
-    q_ref, k_mine, k_other, v_mine, v_other, fresh_ref, time_ref, latent_ref,
-    out_ref, base_ref, gain_ref,
+    q_ref, kv0, kv1, kv2, kv3, fresh_ref, time_ref, latent_ref, out_ref, base_ref, gain_ref
 ):
     image = lax.axis_index("guide")
     now = jnp.full(latent_ref.shape, time_ref[image // 2], jnp.int32)
@@ -231,7 +273,7 @@
     base_ref[...] = latent_gain * latent_ref[...]
     gain_ref[0] = noise_gain * jnp.where(is_cond, 4.5, -3.5)
     gain_ref[1] = noise_gain * jnp.where(is_cond, -3.5, 4.5)
-    attend_kernel(q_ref, k_mine, k_other, v_mine, v_other, out_ref, fresh_ref)
+    attend_kernel(q_ref, kv0, kv1, kv2, kv3, out_ref, fresh_ref=fresh_ref)
 
 
 def attend_own(query, keyval, fresh, timestep, latent):
@@ -247,7 +289,7 @@
             jax.ShapeDtypeStruct((2, *latent.shape), F32),
         ],
         compiler_params=pltpu.CompilerParams(vmem_limit_bytes=VMEM_LIMIT),
-        cost_estimate=attend_cost(rows, 2 * keyval[0].shape[0]),
+        cost_estimate=attend_cost(rows, sum(x.shape[0] for x in keyval)),
         name="attend_own",
     )(query, *keyval, fresh, timestep, latent)
 
@@ -305,23 +347,23 @@
     rows = hidden.shape[0]
 
     stale, pick = lax.optimization_barrier((stale, head_selector()))
-    stale_z = [send(stale, dz=k) for k in (2, 1, 3)]
+    stale_1, stale_2, stale_3 = [send(stale, z_xor(mask)) for mask in (1, 2, 3)]
     fresh = project_fresh(hidden, mod, w_qkv)
     query = fresh[:, :WIDTH]
-    query_y = [send(query, dy=k) for k in (2, 1, 3)]
-
-    blocks = [stale] + stale_z
-    blocks, query_y[0] = lax.optimization_barrier((blocks, query_y[0]))
-    k_mine = project_stale(blocks, w_qkv, WIDTH, "stale_keys")
-    k_other = send(k_mine, dc=1)
-    blocks, k_mine, query_y = lax.optimization_barrier((blocks, k_mine, query_y))
-    v_mine = project_stale(blocks, w_qkv, 2 * WIDTH, "stale_values")
-    v_other = send(v_mine, dc=1)
-    keyval = (k_mine, k_other, v_mine, v_other)
-
-    partial = attend(jnp.concatenate(query_y, axis=0), keyval)
+    query_far, query_up, query_down = [send(query, y_shift(step)) for step in (2, 1, -1)]
+
+    early = project_stale([stale, stale_1], w_qkv, 1)
+    early_other = send(early, other_core)
+    queries, blocks = gather_blocks((query_far, query_up, query_down), (stale_2, stale_3))
+    blocks, early_other = lax.optimization_barrier((blocks, early_other))
+    late = project_stale([blocks], w_qkv, 1)
+    late_other = send(late, other_core)
+    keyval = (early, late, early_other, late_other)
+
+    partial = attend(queries, keyval)
     back = [
-        send(partial[n * rows : (n + 1) * rows], dy=-k) for n, k in enumerate((2, 1, 3))
+        send(partial[n * rows : (n + 1) * rows], y_shift(step))
+        for n, step in enumerate((-2, -1, 1))
     ]
     own, scaled, gain = attend_own(query, keyval, fresh, timestep, latent[0])
     noise, base = post([own] + back, hidden, mod, w_out, w_final.T, scaled, gain, pick)

time: 48.6 us -> 47.7 us (0.981)
  starting transfers between devices: 22.3 us -> 20.7 us
  waiting for transfers between devices: 14.1 us -> 14.8 us
    ppermute x11, starting transfers between devices: 16.7 us -> 15.4 us  [send(): return lax.ppermute(value, 'patch', pairs)]
    pallas_call x2 -> x3, Pallas kernels: 2.27 us -> 2.38 us  [the longest x2 2.32 us: project_stale(): pl.pallas_call(stale_kernel, in_specs=[pl.BlockSpec(memory_space=pltpu.VM...]
  transfers between devices with their start and end apart: 12 -> 12, of which waited for: 8 -> 7; matrix products, arithmetic and copies ran while one was open for 0% -> 0% of each run, Pallas kernels for 10% -> 10%
where the time goes in v3:
time: 47.7 us; the launch traced here: 47.6 us
  starting transfers between devices  20.7 us (43%)
  waiting for transfers between devices  14.8 us (31%)
  Pallas kernels  10.4 us (22%)
  local copies, waits for them, and re-layouts  0.92 us (2%)
  other arithmetic  0.6 us (1%)
    ppermute x11, starting transfers between devices, send(): return lax.ppermute(value, 'patch', pairs)  15.4 us
    ppermute x11, waiting for transfers between devices, send(): return lax.ppermute(value, 'patch', pairs)  12.5 us
    ppermute x1, starting transfers between devices, body(): lax.ppermute(noise, 'guide', [(i, i ^ 1) for i in range(lax.axis_size('gu...  5.29 us
    pallas_call x1, Pallas kernels, attend(): pl.pallas_call(attend_kernel, in_specs=[pl.BlockSpec(memory_space=pltpu.V...  2.88 us
    pallas_call x2, Pallas kernels, project_stale(): pl.pallas_call(stale_kernel, in_specs=[pl.BlockSpec(memory_space=pltpu.VM...  2.32 us
    ppermute x1, waiting for transfers between devices, body(): lax.ppermute(noise, 'guide', [(i, i ^ 1) for i in range(lax.axis_size('gu...  2.31 us
    pallas_call x1, Pallas kernels, attend_own(): pl.pallas_call(attend_own_kernel, in_specs=[vmem] * 6 + [pl.BlockSpec(mem...  2.1 us
    pallas_call x1, Pallas kernels, project_fresh(): pl.pallas_call(fresh_kernel, in_specs=[pl.BlockSpec(memory_space=pltpu.VM...  1.52 us
  transfers between devices with their start and end apart: 12, of which 7 were waited for; matrix products, arithmetic and copies ran while one was open for 0% of the time, Pallas kernels for 10%

profile of v3, /device:TPU:2, one launch (start us, length us, event | category | flops | bytes accessed | tf_op | source)
XLA Modules:
  0.0 47.6 jit_solution(17839017310730290454)
XLA Ops:
  0.1 0.8 %copy-done.3 = bf16[1,64,1152]{2,1,0:T(8,128)(2,1)S(1)} copy-done((bf16[1,64,1152]{2,1,0:T(8,128)(2,1)S(1)}, bf16[1,64,1152]{2,1,0:T(8,128)(2,1)}, u32[]{:S(2)}) %copy-start.3) | copy-done | bytes 147480
  0.9 1.9 %collective-permute-start = (bf16[64,1152]{1,0:T(8,128)(2,1)S(1)}, bf16[64,1152]{1,0:T(8,128)(2,1)S(1)}, u32[]{:S(2)}, u32[]{:S(2)}) collective-permute-start(bf16[64,1152]{1,0:T(8,128)(2,1)S(1)} %bitcast.15), channel_id=1, source_target_pairs={{0,16},{8,24},{16,0},{24,8},{32,48},{40,56},{48,32},{56,40},{64,80... | collective-permute-start | bytes 442376 | tf_op jit(solution)/shard_map/ppermute | solution.py:41
  2.8 2.8 %collective-permute-start.5 = (bf16[64,1152]{1,0:T(8,128)(2,1)S(1)}, bf16[64,1152]{1,0:T(8,128)(2,1)S(1)}, u32[]{:S(2)}, u32[]{:S(2)}) collective-permute-start(bf16[64,1152]{1,0:T(8,128)(2,1)S(1)} %bitcast.16), channel_id=1, source_target_pairs={{0,48},{8,56},{16,32},{24,40},{32,16},{40,24},{48,0},{56,8},{64,11... | collective-permute-start | bytes 442376 | tf_op jit(solution)/shard_map/ppermute | solution.py:41
  5.6 0.5 collective-permute-start.4
  6.1 1.5 %fresh_qkv.1.fresh_ref = bf16[64,3456]{1,0:T(8,128)(2,1)S(1)} custom-call(bf16[64,1152]{1,0:T(8,128)(2,1)S(1)} %bitcast.13, f32[5,1,1152]{2,1,0:T(1,128)S(1)} %bitcast.19, bf16[1152,3456]{1,0:T(8,128)(2,1)S(1)} %copy-done), custom_call_target="tpu_custom_call" | custom-call | flops 509607936 | bytes 7962624 | tf_op jit(solution)/shard_map/fresh_qkv/pallas_call | solution.py:89
  7.7 3.1 %collective-permute-start.3 = (bf16[64,1152]{1,0:T(8,128)(2,1)S(1)}, bf16[64,1152]{1,0:T(8,128)(2,1)S(1)}, u32[]{:S(2)}, u32[]{:S(2)}) collective-permute-start(bf16[64,1152]{1,0:T(8,128)(2,1)S(1)} %slice.20.q_ref), channel_id=1, source_target_pairs={{0,192},{8,200},{16,208},{24,216},{32,224},{40,232},{48,240},{56,2... | collective-permute-start | bytes 442376 | tf_op jit(solution)/shard_map/ppermute | solution.py:41
  10.8 2.2 %collective-permute-start.1 = (bf16[64,1152]{1,0:T(8,128)(2,1)S(1)}, bf16[64,1152]{1,0:T(8,128)(2,1)S(1)}, u32[]{:S(2)}, u32[]{:S(2)}) collective-permute-start(bf16[64,1152]{1,0:T(8,128)(2,1)S(1)} %slice.20.q_ref), channel_id=1, source_target_pairs={{0,128},{8,136},{16,144},{24,152},{32,160},{40,168},{48,176},{56,1... | collective-permute-start | bytes 442376 | tf_op jit(solution)/shard_map/ppermute | solution.py:41
  13.0 1.2 %stale_kv.2.kv0.refs_0_ = bf16[128,2304]{1,0:T(8,128)(2,1)S(1)} custom-call(bf16[64,1152]{1,0:T(8,128)(2,1)S(1)} %bitcast.18, bf16[64,1152]{1,0:T(8,128)(2,1)S(1)} %collective-permute-done.refs_1_, bf16[1152,3456]{1,0:T(8,128)(2,1)S(1)} %copy-done), custom_call_target="tpu_custom_call" | custom-call | flops 1 | bytes 1 | tf_op jit(solution)/shard_map/stale_kv/pallas_call | solution.py:117
  14.1 0.1 collective-permute-start.6
  14.2 4.9 %collective-permute-done.4.refs_3_ = bf16[64,1152]{1,0:T(8,128)(2,1)S(1)} collective-permute-done((bf16[64,1152]{1,0:T(8,128)(2,1)S(1)}, bf16[64,1152]{1,0:T(8,128)(2,1)S(1)}, u32[]{:S(2)}, u32[]{:S(2)}) %collective-permute-start.4) | collective-permute-done | bytes 147488 | tf_op jit(solution)/shard_map/ppermute | solution.py:41
  19.1 0.7 %collective-permute-done.2.refs_1_ = bf16[64,1152]{1,0:T(8,128)(2,1)S(1)} collective-permute-done((bf16[64,1152]{1,0:T(8,128)(2,1)S(1)}, bf16[64,1152]{1,0:T(8,128)(2,1)S(1)}, u32[]{:S(2)}, u32[]{:S(2)}) %collective-permute-start.2) | collective-permute-done | bytes 147488 | tf_op jit(solution)/shard_map/ppermute | solution.py:41
  19.9 0.0 collective-permute-done.1.refs_0_
  19.9 0.1 gather_blocks.1
  19.9 0.0 copy-start.6
  20.0 0.0 copy-start.7
  20.0 0.0 copy-start.1
  20.0 0.0 copy-start.5
  20.0 1.2 %stale_kv.3.kv1.refs_1_ = bf16[128,2304]{1,0:T(8,128)(2,1)S(1)} custom-call(bf16[128,1152]{1,0:T(8,128)(2,1)S(1)} %get-tuple-element.18.refs_0_, bf16[1152,3456]{1,0:T(8,128)(2,1)S(1)} %copy-done), custom_call_target="tpu_custom_call" | custom-call | flops 1 | bytes 1 | tf_op jit(solution)/shard_map/stale_kv/pallas_call | solution.py:117
  21.2 0.1 collective-permute-start.7
  21.3 2.0 %collective-permute-done.7.kv3.refs_3_ = bf16[128,2304]{1,0:T(8,128)(2,1)S(1)} collective-permute-done((bf16[128,2304]{1,0:T(8,128)(2,1)S(1)}, bf16[128,2304]{1,0:T(8,128)(2,1)S(1)}, u32[]{:S(2)}, u32[]{:S(2)}) %collective-permute-start.7) | collective-permute-done | bytes 589856 | tf_op jit(solution)/shard_map/ppermute | solution.py:41
  23.3 2.9 %attend.1 = bf16[192,1280]{1,0:T(8,128)(2,1)S(1)} custom-call(bf16[192,1152]{1,0:T(8,128)(2,1)S(1)} %get-tuple-element.21.q_ref, bf16[128,2304]{1,0:T(8,128)(2,1)S(1)} %stale_kv.2.kv0.refs_0_, bf16[128,2304]{1,0:T(8,128)(2,1)S(1)} %stale_kv.3.kv1.refs_1_, bf16[128,2304]{1,0:T(8,128)(2,1)S(1)} %collective-permute-done.6.kv2.refs_2_, ...), custom_call_target="tpu_custom_call" | custom-call | flops 1610612736 | bytes 2359296 | tf_op jit(solution)/shard_map/attend/pallas_call | solution.py:252
  26.2 1.1 %collective-permute-start.10 = (bf16[64,1280]{1,0:T(8,128)(2,1)S(1)}, bf16[64,1280]{1,0:T(8,128)(2,1)S(1)}, u32[]{:S(2)}, u32[]{:S(2)}) collective-permute-start(bf16[64,1280]{1,0:T(8,128)(2,1)S(1)} %get-tuple-element.27), channel_id=1, source_target_pairs={{0,64},{8,72},{16,80},{24,88},{32,96},{40,104},{48,112},{56,120},{... | collective-permute-start | bytes 491528 | tf_op jit(solution)/shard_map/ppermute | solution.py:41
  27.3 2.4 %collective-permute-start.9 = (bf16[64,1280]{1,0:T(8,128)(2,1)S(1)}, bf16[64,1280]{1,0:T(8,128)(2,1)S(1)}, u32[]{:S(2)}, u32[]{:S(2)}) collective-permute-start(bf16[64,1280]{1,0:T(8,128)(2,1)S(1)} %get-tuple-element.28), channel_id=1, source_target_pairs={{0,192},{8,200},{16,208},{24,216},{32,224},{40,232},{48,240},{56,2... | collective-permute-start | bytes 491528 | tf_op jit(solution)/shard_map/ppermute | solution.py:41
  29.7 1.3 %collective-permute-start.8 = (bf16[64,1280]{1,0:T(8,128)(2,1)S(1)}, bf16[64,1280]{1,0:T(8,128)(2,1)S(1)}, u32[]{:S(2)}, u32[]{:S(2)}) collective-permute-start(bf16[64,1280]{1,0:T(8,128)(2,1)S(1)} %get-tuple-element.29), channel_id=1, source_target_pairs={{0,128},{8,136},{16,144},{24,152},{32,160},{40,168},{48,176},{56,1... | collective-permute-start | bytes 491528 | tf_op jit(solution)/shard_map/ppermute | solution.py:41
  31.0 2.1 %attend_own.1 = (bf16[64,1280]{1,0:T(8,128)(2,1)S(1)}, f32[8,128]{1,0:T(8,128)S(1)}, f32[2,8,128]{2,1,0:T(8,128)S(1)}) custom-call(bf16[64,1152]{1,0:T(8,128)(2,1)S(1)} %slice.20.q_ref, bf16[128,2304]{1,0:T(8,128)(2,1)S(1)} %stale_kv.2.kv0.refs_0_, bf16[128,2304]{1,0:T(8,128)(2,1)S(1)} %stale_kv.3.kv1.refs_1_, ...), custom_call_target="tpu_custom_call" | custom-call | flops 536870912 | bytes 2359296 | tf_op jit(solution)/shard_map/attend_own/pallas_call | solution.py:282
  33.1 1.1 %collective-permute-done.10.p3 = bf16[64,1280]{1,0:T(8,128)(2,1)S(1)} collective-permute-done((bf16[64,1280]{1,0:T(8,128)(2,1)S(1)}, bf16[64,1280]{1,0:T(8,128)(2,1)S(1)}, u32[]{:S(2)}, u32[]{:S(2)}) %collective-permute-start.10) | collective-permute-done | bytes 163872 | tf_op jit(solution)/shard_map/ppermute | solution.py:41
  34.2 2.5 %collective-permute-done.9.p2 = bf16[64,1280]{1,0:T(8,128)(2,1)S(1)} collective-permute-done((bf16[64,1280]{1,0:T(8,128)(2,1)S(1)}, bf16[64,1280]{1,0:T(8,128)(2,1)S(1)}, u32[]{:S(2)}, u32[]{:S(2)}) %collective-permute-start.9) | collective-permute-done | bytes 163872 | tf_op jit(solution)/shard_map/ppermute | solution.py:41
  36.7 1.2 %collective-permute-done.8.p1 = bf16[64,1280]{1,0:T(8,128)(2,1)S(1)} collective-permute-done((bf16[64,1280]{1,0:T(8,128)(2,1)S(1)}, bf16[64,1280]{1,0:T(8,128)(2,1)S(1)}, u32[]{:S(2)}, u32[]{:S(2)}) %collective-permute-start.8) | collective-permute-done | bytes 163872 | tf_op jit(solution)/shard_map/ppermute | solution.py:41
  37.9 1.5 %post.1 = (f32[8,128]{1,0:T(8,128)S(1)}, f32[8,128]{1,0:T(8,128)S(1)}) custom-call(bf16[64,1280]{1,0:T(8,128)(2,1)S(1)} %get-tuple-element.20.p0, bf16[64,1280]{1,0:T(8,128)(2,1)S(1)} %collective-permute-done.8.p1, bf16[64,1280]{1,0:T(8,128)(2,1)S(1)} %collective-permute-done.9.p2, bf16[64,1280]{1,0:T(8,128)(2,1)S(1)} %collective-permute-done.10.p3, ...), custom_call_target="tpu_custom_call" | custom-call | flops 169869312 | bytes 2654208 | tf_op jit(solution)/shard_map/post/pallas_call | solution.py:331
  39.4 5.3 %collective-permute-start.11 = (f32[8,128]{1,0:T(8,128)S(1)}, f32[8,128]{1,0:T(8,128)S(1)}, u32[]{:S(2)}, u32[]{:S(2)}) collective-permute-start(f32[8,128]{1,0:T(8,128)S(1)} %get-tuple-element.26), channel_id=1, source_target_pairs={{0,1},{1,0},{2,3},{3,2},{4,5},{5,4},{6,7},{7,6},{8,9},{9,8},{10,11... | collective-permute-start | bytes 12296 | tf_op jit(solution)/shard_map/ppermute | solution.py:370
  44.7 2.3 %collective-permute-done.11 = f32[8,128]{1,0:T(8,128)S(1)} collective-permute-done((f32[8,128]{1,0:T(8,128)S(1)}, f32[8,128]{1,0:T(8,128)S(1)}, u32[]{:S(2)}, u32[]{:S(2)}) %collective-permute-start.11) | collective-permute-done | bytes 4128 | tf_op jit(solution)/shard_map/ppermute | solution.py:370
  47.0 0.6 %fusion.1 = f32[1,8,128]{2,1,0:T(8,128)} fusion(f32[8,128]{1,0:T(8,128)S(1)} %get-tuple-element.25, f32[8,128]{1,0:T(8,128)S(1)} %collective-permute-done.11, f32[2,8,128]{2,1,0:T(8,128)S(1)} %get-tuple-element.23.gain_ref), kind=kLoop, calls=%fused_computation.2 | loop fusion | flops 2048 | bytes 16384 | tf_op jit(solution)/shard_map/broadcast_in_dim | solution.py:373
  (19 shorter events, 0.1 us)
Async XLA Ops:
  0.0 0.9 %copy-start.3 = (bf16[1,64,1152]{2,1,0:T(8,128)(2,1)S(1)}, bf16[1,64,1152]{2,1,0:T(8,128)(2,1)}, u32[]{:S(2)}) copy-start(bf16[1,64,1152]{2,1,0:T(8,128)(2,1)} %param.9) | copy-start | bytes 442372
  0.0 6.1 %copy-start = (bf16[1152,3456]{1,0:T(8,128)(2,1)S(1)}, bf16[1152,3456]{1,0:T(8,128)(2,1)}, u32[]{:S(2)}) copy-start(bf16[1152,3456]{1,0:T(8,128)(2,1)} %refs_1_.1) | copy-start | bytes 23887876
  0.0 6.1 %copy-start.4 = (f32[1,5,1152]{2,0,1:T(1,128)S(1)}, f32[1,5,1152]{2,0,1:T(1,128)}, u32[]{:S(2)}) copy-start(f32[1,5,1152]{2,0,1:T(1,128)} %param.10) | copy-start | bytes 69124
  0.0 6.1 %copy-start.2 = (bf16[1,64,1152]{2,1,0:T(8,128)(2,1)S(1)}, bf16[1,64,1152]{2,1,0:T(8,128)(2,1)}, u32[]{:S(2)}) copy-start(bf16[1,64,1152]{2,1,0:T(8,128)(2,1)} %param.8) | copy-start | bytes 442372
  0.9 9.9 %collective-permute-start = (bf16[64,1152]{1,0:T(8,128)(2,1)S(1)}, bf16[64,1152]{1,0:T(8,128)(2,1)S(1)}, u32[]{:S(2)}, u32[]{:S(2)}) collective-permute-start(bf16[64,1152]{1,0:T(8,128)(2,1)S(1)} %bitcast.15), channel_id=1, source_target_pairs={{0,16},{8,24},{16,0},{24,8},{32,48},{40,56},{48,32},{56,40},{64,80... | collective-permute-start | bytes 442376 | tf_op jit(solution)/shard_map/ppermute | solution.py:41
  2.8 11.3 %collective-permute-start.5 = (bf16[64,1152]{1,0:T(8,128)(2,1)S(1)}, bf16[64,1152]{1,0:T(8,128)(2,1)S(1)}, u32[]{:S(2)}, u32[]{:S(2)}) collective-permute-start(bf16[64,1152]{1,0:T(8,128)(2,1)S(1)} %bitcast.16), channel_id=1, source_target_pairs={{0,48},{8,56},{16,32},{24,40},{32,16},{40,24},{48,0},{56,8},{64,11... | collective-permute-start | bytes 442376 | tf_op jit(solution)/shard_map/ppermute | solution.py:41
  5.6 13.5 %collective-permute-start.4 = (bf16[64,1152]{1,0:T(8,128)(2,1)S(1)}, bf16[64,1152]{1,0:T(8,128)(2,1)S(1)}, u32[]{:S(2)}, u32[]{:S(2)}) collective-permute-start(bf16[64,1152]{1,0:T(8,128)(2,1)S(1)} %bitcast.17), channel_id=1, source_target_pairs={{0,32},{8,40},{16,48},{24,56},{32,0},{40,8},{48,16},{56,24},{64,96... | collective-permute-start | bytes 442376 | tf_op jit(solution)/shard_map/ppermute | solution.py:41
  7.7 11.5 %collective-permute-start.3 = (bf16[64,1152]{1,0:T(8,128)(2,1)S(1)}, bf16[64,1152]{1,0:T(8,128)(2,1)S(1)}, u32[]{:S(2)}, u32[]{:S(2)}) collective-permute-start(bf16[64,1152]{1,0:T(8,128)(2,1)S(1)} %slice.20.q_ref), channel_id=1, source_target_pairs={{0,192},{8,200},{16,208},{24,216},{32,224},{40,232},{48,240},{56,2... | collective-permute-start | bytes 442376 | tf_op jit(solution)/shard_map/ppermute | solution.py:41
  10.8 9.1 %collective-permute-start.2 = (bf16[64,1152]{1,0:T(8,128)(2,1)S(1)}, bf16[64,1152]{1,0:T(8,128)(2,1)S(1)}, u32[]{:S(2)}, u32[]{:S(2)}) collective-permute-start(bf16[64,1152]{1,0:T(8,128)(2,1)S(1)} %slice.20.q_ref), channel_id=1, source_target_pairs={{0,64},{8,72},{16,80},{24,88},{32,96},{40,104},{48,112},{56,120},{... | collective-permute-start | bytes 442376 | tf_op jit(solution)/shard_map/ppermute | solution.py:41
  10.8 9.1 %collective-permute-start.1 = (bf16[64,1152]{1,0:T(8,128)(2,1)S(1)}, bf16[64,1152]{1,0:T(8,128)(2,1)S(1)}, u32[]{:S(2)}, u32[]{:S(2)}) collective-permute-start(bf16[64,1152]{1,0:T(8,128)(2,1)S(1)} %slice.20.q_ref), channel_id=1, source_target_pairs={{0,128},{8,136},{16,144},{24,152},{32,160},{40,168},{48,176},{56,1... | collective-permute-start | bytes 442376 | tf_op jit(solution)/shard_map/ppermute | solution.py:41
  14.1 5.8 %collective-permute-start.6 = (bf16[128,2304]{1,0:T(8,128)(2,1)S(1)}, bf16[128,2304]{1,0:T(8,128)(2,1)S(1)}, u32[]{:S(2)}, u32[]{:S(2)}) collective-permute-start(bf16[128,2304]{1,0:T(8,128)(2,1)S(1)} %stale_kv.2.kv0.refs_0_), channel_id=1, source_target_pairs={{0,8},{8,0},{16,24},{24,16},{32,40},{40,32},{48,56},{56,48},{64,72... | collective-permute-start | bytes 1769480 | tf_op jit(solution)/shard_map/ppermute | solution.py:41
  19.9 11.0 %copy-start.6 = (f32[1,8,128]{2,1,0:T(8,128)S(1)}, f32[1,8,128]{2,1,0:T(8,128)}, u32[]{:S(2)}) copy-start(f32[1,8,128]{2,1,0:T(8,128)} %param.11) | copy-start | bytes 12292
  20.0 11.0 %copy-start.7 = (s32[4]{0:T(128)S(1)}, s32[4]{0:T(128)}, u32[]{:S(2)}) copy-start(s32[4]{0:T(128)} %time_ref.1) | copy-start | bytes 52
  20.0 18.0 %copy-start.1 = (bf16[1152,1152]{1,0:T(8,128)(2,1)S(1)}, bf16[1152,1152]{1,0:T(8,128)(2,1)}, u32[]{:S(2)}) copy-start(bf16[1152,1152]{1,0:T(8,128)(2,1)} %w_out_ref.1) | copy-start | bytes 7962628
  20.0 17.9 %copy-start.5 = (bf16[1152,16]{0,1:T(8,128)(2,1)S(1)}, bf16[1152,16]{0,1:T(8,128)(2,1)}, u32[]{:S(2)}) copy-start(bf16[1152,16]{0,1:T(8,128)(2,1)} %param.15) | copy-start | bytes 110596
  21.2 2.1 %collective-permute-start.7 = (bf16[128,2304]{1,0:T(8,128)(2,1)S(1)}, bf16[128,2304]{1,0:T(8,128)(2,1)S(1)}, u32[]{:S(2)}, u32[]{:S(2)}) collective-permute-start(bf16[128,2304]{1,0:T(8,128)(2,1)S(1)} %stale_kv.3.kv1.refs_1_), channel_id=1, source_target_pairs={{0,8},{8,0},{16,24},{24,16},{32,40},{40,32},{48,56},{56,48},{64,72... | collective-permute-start | bytes 1769480 | tf_op jit(solution)/shard_map/ppermute | solution.py:41
  26.2 8.0 %collective-permute-start.10 = (bf16[64,1280]{1,0:T(8,128)(2,1)S(1)}, bf16[64,1280]{1,0:T(8,128)(2,1)S(1)}, u32[]{:S(2)}, u32[]{:S(2)}) collective-permute-start(bf16[64,1280]{1,0:T(8,128)(2,1)S(1)} %get-tuple-element.27), channel_id=1, source_target_pairs={{0,64},{8,72},{16,80},{24,88},{32,96},{40,104},{48,112},{56,120},{... | collective-permute-start | bytes 491528 | tf_op jit(solution)/shard_map/ppermute | solution.py:41
  27.3 9.4 %collective-permute-start.9 = (bf16[64,1280]{1,0:T(8,128)(2,1)S(1)}, bf16[64,1280]{1,0:T(8,128)(2,1)S(1)}, u32[]{:S(2)}, u32[]{:S(2)}) collective-permute-start(bf16[64,1280]{1,0:T(8,128)(2,1)S(1)} %get-tuple-element.28), channel_id=1, source_target_pairs={{0,192},{8,200},{16,208},{24,216},{32,224},{40,232},{48,240},{56,2... | collective-permute-start | bytes 491528 | tf_op jit(solution)/shard_map/ppermute | solution.py:41
  29.7 8.2 %collective-permute-start.8 = (bf16[64,1280]{1,0:T(8,128)(2,1)S(1)}, bf16[64,1280]{1,0:T(8,128)(2,1)S(1)}, u32[]{:S(2)}, u32[]{:S(2)}) collective-permute-start(bf16[64,1280]{1,0:T(8,128)(2,1)S(1)} %get-tuple-element.29), channel_id=1, source_target_pairs={{0,128},{8,136},{16,144},{24,152},{32,160},{40,168},{48,176},{56,1... | collective-permute-start | bytes 491528 | tf_op jit(solution)/shard_map/ppermute | solution.py:41
  39.4 7.6 %collective-permute-start.11 = (f32[8,128]{1,0:T(8,128)S(1)}, f32[8,128]{1,0:T(8,128)S(1)}, u32[]{:S(2)}, u32[]{:S(2)}) collective-permute-start(f32[8,128]{1,0:T(8,128)S(1)} %get-tuple-element.26), channel_id=1, source_target_pairs={{0,1},{1,0},{2,3},{3,2},{4,5},{5,4},{6,7},{7,6},{8,9},{9,8},{10,11... | collective-permute-start | bytes 12296 | tf_op jit(solution)/shard_map/ppermute | solution.py:370

commit v4 on v3

--- a/solution.py
+++ b/solution.py
@@ -15,6 +15,7 @@
 NY, NZ, NC = 4, 4, 2
 STATS = 128
 CHUNK = 384
+LOG2_E = 1.4426950408889634
 BF16, F32 = jnp.bfloat16, jnp.float32
 VMEM_LIMIT = 32 * 1024 * 1024
 
@@ -200,7 +201,7 @@
         first = head * HEAD - start
         return (lane >= first) & (lane < first + HEAD)
 
-    for part in (WINDOWS[:4], WINDOWS[4:]):
+    for part in (WINDOWS,):
         scores = []
         for start, heads in part:
             query = q_ref[:, start : start + 256]
@@ -215,7 +216,7 @@
                 )
             )
         tops = [jnp.max(s, axis=-1, keepdims=True) for s in scores]
-        expos = [jnp.exp((s - t) * scale) for s, t in zip(scores, tops)]
+        expos = [jnp.exp2((s - t) * (scale * LOG2_E)) for s, t in zip(scores, tops)]
         totals = [jnp.sum(e, axis=-1, keepdims=True) for e in expos]
         for (start, heads), top, expo, total in zip(part, tops, expos, totals):
             value = jnp.dot(
@@ -350,11 +351,11 @@
     stale_1, stale_2, stale_3 = [send(stale, z_xor(mask)) for mask in (1, 2, 3)]
     fresh = project_fresh(hidden, mod, w_qkv)
     query = fresh[:, :WIDTH]
-    query_far, query_up, query_down = [send(query, y_shift(step)) for step in (2, 1, -1)]
+    query_up, query_down, query_far = [send(query, y_shift(step)) for step in (1, -1, 2)]
 
     early = project_stale([stale, stale_1], w_qkv, 1)
     early_other = send(early, other_core)
-    queries, blocks = gather_blocks((query_far, query_up, query_down), (stale_2, stale_3))
+    queries, blocks = gather_blocks((query_up, query_down, query_far), (stale_2, stale_3))
     blocks, early_other = lax.optimization_barrier((blocks, early_other))
     late = project_stale([blocks], w_qkv, 1)
     late_other = send(late, other_core)
@@ -363,7 +364,7 @@
     partial = attend(queries, keyval)
     back = [
         send(partial[n * rows : (n + 1) * rows], y_shift(step))
-        for n, step in enumerate((-2, -1, 1))
+        for n, step in enumerate((-1, 1, -2))
     ]
     own, scaled, gain = attend_own(query, keyval, fresh, timestep, latent[0])
     noise, base = post([own] + back, hidden, mod, w_out, w_final.T, scaled, gain, pick)

time: 47.7 us -> 46.8 us (0.981)
  waiting for transfers between devices: 14.8 us -> 12.5 us
  starting transfers between devices: 20.7 us -> 22.5 us
    ppermute x11, waiting for transfers between devices: 12.5 us -> 10.2 us  [send(): return lax.ppermute(value, 'patch', pairs)]
    ppermute x11, starting transfers between devices: 15.4 us -> 17.2 us  [send(): return lax.ppermute(value, 'patch', pairs)]
  transfers between devices with their start and end apart: 12 -> 12, of which waited for: 7 -> 6; matrix products, arithmetic and copies ran while one was open for 0% -> 0% of each run, Pallas kernels for 10% -> 10%
where the time goes in v4:
time: 46.8 us
  starting transfers between devices  22.5 us (48%)
  waiting for transfers between devices  12.5 us (27%)
  Pallas kernels  10.1 us (22%)
  local copies, waits for them, and re-layouts  0.92 us (2%)
  other arithmetic  0.6 us (1%)
    ppermute x11, starting transfers between devices, send(): return lax.ppermute(value, 'patch', pairs)  17.2 us
    ppermute x11, waiting for transfers between devices, send(): return lax.ppermute(value, 'patch', pairs)  10.2 us
    ppermute x1, starting transfers between devices, body(): lax.ppermute(noise, 'guide', [(i, i ^ 1) for i in range(lax.axis_size('gu...  5.29 us
    pallas_call x1, Pallas kernels, attend(): pl.pallas_call(attend_kernel, in_specs=[pl.BlockSpec(memory_space=pltpu.V...  2.76 us
    pallas_call x2, Pallas kernels, project_stale(): pl.pallas_call(stale_kernel, in_specs=[pl.BlockSpec(memory_space=pltpu.VM...  2.32 us
    ppermute x1, waiting for transfers between devices, body(): lax.ppermute(noise, 'guide', [(i, i ^ 1) for i in range(lax.axis_size('gu...  2.31 us
    pallas_call x1, Pallas kernels, attend_own(): pl.pallas_call(attend_own_kernel, in_specs=[vmem] * 6 + [pl.BlockSpec(mem...  1.83 us
    pallas_call x1, Pallas kernels, project_fresh(): pl.pallas_call(fresh_kernel, in_specs=[pl.BlockSpec(memory_space=pltpu.VM...  1.52 us
  transfers between devices with their start and end apart: 12, of which 6 were waited for; matrix products, arithmetic and copies ran while one was open for 0% of the time, Pallas kernels for 10%

profile of v4, /device:TPU:2, one launch (start us, length us, event | category | flops | bytes accessed | tf_op | source)
XLA Modules:
  0.0 46.8 jit_solution(7159274505212521724)
XLA Ops:
  0.1 0.8 %copy-done.3 = bf16[1,64,1152]{2,1,0:T(8,128)(2,1)S(1)} copy-done((bf16[1,64,1152]{2,1,0:T(8,128)(2,1)S(1)}, bf16[1,64,1152]{2,1,0:T(8,128)(2,1)}, u32[]{:S(2)}) %copy-start.3) | copy-done | bytes 147480
  0.9 1.9 %collective-permute-start = (bf16[64,1152]{1,0:T(8,128)(2,1)S(1)}, bf16[64,1152]{1,0:T(8,128)(2,1)S(1)}, u32[]{:S(2)}, u32[]{:S(2)}) collective-permute-start(bf16[64,1152]{1,0:T(8,128)(2,1)S(1)} %bitcast.15), channel_id=1, source_target_pairs={{0,16},{8,24},{16,0},{24,8},{32,48},{40,56},{48,32},{56,40},{64,80... | collective-permute-start | bytes 442376 | tf_op jit(solution)/shard_map/ppermute | solution.py:42
  2.8 2.8 %collective-permute-start.5 = (bf16[64,1152]{1,0:T(8,128)(2,1)S(1)}, bf16[64,1152]{1,0:T(8,128)(2,1)S(1)}, u32[]{:S(2)}, u32[]{:S(2)}) collective-permute-start(bf16[64,1152]{1,0:T(8,128)(2,1)S(1)} %bitcast.16), channel_id=1, source_target_pairs={{0,48},{8,56},{16,32},{24,40},{32,16},{40,24},{48,0},{56,8},{64,11... | collective-permute-start | bytes 442376 | tf_op jit(solution)/shard_map/ppermute | solution.py:42
  5.6 0.5 collective-permute-start.4
  6.1 1.5 %fresh_qkv.1.fresh_ref = bf16[64,3456]{1,0:T(8,128)(2,1)S(1)} custom-call(bf16[64,1152]{1,0:T(8,128)(2,1)S(1)} %bitcast.13, f32[5,1,1152]{2,1,0:T(1,128)S(1)} %bitcast.19, bf16[1152,3456]{1,0:T(8,128)(2,1)S(1)} %copy-done), custom_call_target="tpu_custom_call" | custom-call | flops 509607936 | bytes 7962624 | tf_op jit(solution)/shard_map/fresh_qkv/pallas_call | solution.py:90
  7.7 3.3 %collective-permute-start.3 = (bf16[64,1152]{1,0:T(8,128)(2,1)S(1)}, bf16[64,1152]{1,0:T(8,128)(2,1)S(1)}, u32[]{:S(2)}, u32[]{:S(2)}) collective-permute-start(bf16[64,1152]{1,0:T(8,128)(2,1)S(1)} %slice.20.q_ref), channel_id=1, source_target_pairs={{0,128},{8,136},{16,144},{24,152},{32,160},{40,168},{48,176},{56,1... | collective-permute-start | bytes 442376 | tf_op jit(solution)/shard_map/ppermute | solution.py:42
  10.9 1.1 %collective-permute-start.2 = (bf16[64,1152]{1,0:T(8,128)(2,1)S(1)}, bf16[64,1152]{1,0:T(8,128)(2,1)S(1)}, u32[]{:S(2)}, u32[]{:S(2)}) collective-permute-start(bf16[64,1152]{1,0:T(8,128)(2,1)S(1)} %slice.20.q_ref), channel_id=1, source_target_pairs={{0,192},{8,200},{16,208},{24,216},{32,224},{40,232},{48,240},{56,2... | collective-permute-start | bytes 442376 | tf_op jit(solution)/shard_map/ppermute | solution.py:42
  12.0 0.0 collective-permute-done.refs_1_
  12.0 1.0 %collective-permute-start.1 = (bf16[64,1152]{1,0:T(8,128)(2,1)S(1)}, bf16[64,1152]{1,0:T(8,128)(2,1)S(1)}, u32[]{:S(2)}, u32[]{:S(2)}) collective-permute-start(bf16[64,1152]{1,0:T(8,128)(2,1)S(1)} %slice.20.q_ref), channel_id=1, source_target_pairs={{0,64},{8,72},{16,80},{24,88},{32,96},{40,104},{48,112},{56,120},{... | collective-permute-start | bytes 442376 | tf_op jit(solution)/shard_map/ppermute | solution.py:42
  13.0 1.2 %stale_kv.2.kv0.refs_0_ = bf16[128,2304]{1,0:T(8,128)(2,1)S(1)} custom-call(bf16[64,1152]{1,0:T(8,128)(2,1)S(1)} %bitcast.18, bf16[64,1152]{1,0:T(8,128)(2,1)S(1)} %collective-permute-done.refs_1_, bf16[1152,3456]{1,0:T(8,128)(2,1)S(1)} %copy-done), custom_call_target="tpu_custom_call" | custom-call | flops 1 | bytes 1 | tf_op jit(solution)/shard_map/stale_kv/pallas_call | solution.py:118
  14.2 0.1 collective-permute-start.6
  14.3 4.9 %collective-permute-done.4.refs_3_ = bf16[64,1152]{1,0:T(8,128)(2,1)S(1)} collective-permute-done((bf16[64,1152]{1,0:T(8,128)(2,1)S(1)}, bf16[64,1152]{1,0:T(8,128)(2,1)S(1)}, u32[]{:S(2)}, u32[]{:S(2)}) %collective-permute-start.4) | collective-permute-done | bytes 147488 | tf_op jit(solution)/shard_map/ppermute | solution.py:42
  19.2 0.1 gather_blocks.1
  19.2 0.0 copy-start.6
  19.2 0.0 copy-start.7
  19.3 0.0 copy-start.1
  19.3 0.0 copy-start.5
  19.3 1.2 %stale_kv.3.kv1.refs_1_ = bf16[128,2304]{1,0:T(8,128)(2,1)S(1)} custom-call(bf16[128,1152]{1,0:T(8,128)(2,1)S(1)} %get-tuple-element.18.refs_0_, bf16[1152,3456]{1,0:T(8,128)(2,1)S(1)} %copy-done), custom_call_target="tpu_custom_call" | custom-call | flops 1 | bytes 1 | tf_op jit(solution)/shard_map/stale_kv/pallas_call | solution.py:118
  20.5 0.1 collective-permute-start.7
  20.6 2.0 %collective-permute-done.7.kv3.refs_3_ = bf16[128,2304]{1,0:T(8,128)(2,1)S(1)} collective-permute-done((bf16[128,2304]{1,0:T(8,128)(2,1)S(1)}, bf16[128,2304]{1,0:T(8,128)(2,1)S(1)}, u32[]{:S(2)}, u32[]{:S(2)}) %collective-permute-start.7) | collective-permute-done | bytes 589856 | tf_op jit(solution)/shard_map/ppermute | solution.py:42
  22.5 2.8 %attend.1 = bf16[192,1280]{1,0:T(8,128)(2,1)S(1)} custom-call(bf16[192,1152]{1,0:T(8,128)(2,1)S(1)} %get-tuple-element.21.q_ref, bf16[128,2304]{1,0:T(8,128)(2,1)S(1)} %stale_kv.2.kv0.refs_0_, bf16[128,2304]{1,0:T(8,128)(2,1)S(1)} %stale_kv.3.kv1.refs_1_, bf16[128,2304]{1,0:T(8,128)(2,1)S(1)} %collective-permute-done.6.kv2.refs_2_, ...), custom_call_target="tpu_custom_call" | custom-call | flops 1610612736 | bytes 2359296 | tf_op jit(solution)/shard_map/attend/pallas_call | solution.py:253
  25.4 3.3 %collective-permute-start.10 = (bf16[64,1280]{1,0:T(8,128)(2,1)S(1)}, bf16[64,1280]{1,0:T(8,128)(2,1)S(1)}, u32[]{:S(2)}, u32[]{:S(2)}) collective-permute-start(bf16[64,1280]{1,0:T(8,128)(2,1)S(1)} %get-tuple-element.27), channel_id=1, source_target_pairs={{0,128},{8,136},{16,144},{24,152},{32,160},{40,168},{48,176},{56,1... | collective-permute-start | bytes 491528 | tf_op jit(solution)/shard_map/ppermute | solution.py:42
  28.6 0.7 %collective-permute-start.9 = (bf16[64,1280]{1,0:T(8,128)(2,1)S(1)}, bf16[64,1280]{1,0:T(8,128)(2,1)S(1)}, u32[]{:S(2)}, u32[]{:S(2)}) collective-permute-start(bf16[64,1280]{1,0:T(8,128)(2,1)S(1)} %get-tuple-element.28), channel_id=1, source_target_pairs={{0,64},{8,72},{16,80},{24,88},{32,96},{40,104},{48,112},{56,120},{... | collective-permute-start | bytes 491528 | tf_op jit(solution)/shard_map/ppermute | solution.py:42
  29.3 2.6 %collective-permute-start.8 = (bf16[64,1280]{1,0:T(8,128)(2,1)S(1)}, bf16[64,1280]{1,0:T(8,128)(2,1)S(1)}, u32[]{:S(2)}, u32[]{:S(2)}) collective-permute-start(bf16[64,1280]{1,0:T(8,128)(2,1)S(1)} %get-tuple-element.29), channel_id=1, source_target_pairs={{0,192},{8,200},{16,208},{24,216},{32,224},{40,232},{48,240},{56,2... | collective-permute-start | bytes 491528 | tf_op jit(solution)/shard_map/ppermute | solution.py:42
  31.9 1.8 %attend_own.1 = (bf16[64,1280]{1,0:T(8,128)(2,1)S(1)}, f32[8,128]{1,0:T(8,128)S(1)}, f32[2,8,128]{2,1,0:T(8,128)S(1)}) custom-call(bf16[64,1152]{1,0:T(8,128)(2,1)S(1)} %slice.20.q_ref, bf16[128,2304]{1,0:T(8,128)(2,1)S(1)} %stale_kv.2.kv0.refs_0_, bf16[128,2304]{1,0:T(8,128)(2,1)S(1)} %stale_kv.3.kv1.refs_1_, ...), custom_call_target="tpu_custom_call" | custom-call | flops 536870912 | bytes 2359296 | tf_op jit(solution)/shard_map/attend_own/pallas_call | solution.py:283
  33.7 0.3 collective-permute-done.10.p3
  34.0 2.7 %collective-permute-done.9.p2 = bf16[64,1280]{1,0:T(8,128)(2,1)S(1)} collective-permute-done((bf16[64,1280]{1,0:T(8,128)(2,1)S(1)}, bf16[64,1280]{1,0:T(8,128)(2,1)S(1)}, u32[]{:S(2)}, u32[]{:S(2)}) %collective-permute-start.9) | collective-permute-done | bytes 163872 | tf_op jit(solution)/shard_map/ppermute | solution.py:42
  36.7 0.3 collective-permute-done.8.p1
  37.0 1.5 %post.1 = (f32[8,128]{1,0:T(8,128)S(1)}, f32[8,128]{1,0:T(8,128)S(1)}) custom-call(bf16[64,1280]{1,0:T(8,128)(2,1)S(1)} %get-tuple-element.20.p0, bf16[64,1280]{1,0:T(8,128)(2,1)S(1)} %collective-permute-done.8.p1, bf16[64,1280]{1,0:T(8,128)(2,1)S(1)} %collective-permute-done.9.p2, bf16[64,1280]{1,0:T(8,128)(2,1)S(1)} %collective-permute-done.10.p3, ...), custom_call_target="tpu_custom_call" | custom-call | flops 169869312 | bytes 2654208 | tf_op jit(solution)/shard_map/post/pallas_call | solution.py:332
  38.6 5.3 %collective-permute-start.11 = (f32[8,128]{1,0:T(8,128)S(1)}, f32[8,128]{1,0:T(8,128)S(1)}, u32[]{:S(2)}, u32[]{:S(2)}) collective-permute-start(f32[8,128]{1,0:T(8,128)S(1)} %get-tuple-element.26), channel_id=1, source_target_pairs={{0,1},{1,0},{2,3},{3,2},{4,5},{5,4},{6,7},{7,6},{8,9},{9,8},{10,11... | collective-permute-start | bytes 12296 | tf_op jit(solution)/shard_map/ppermute | solution.py:371
  43.9 2.3 %collective-permute-done.11 = f32[8,128]{1,0:T(8,128)S(1)} collective-permute-done((f32[8,128]{1,0:T(8,128)S(1)}, f32[8,128]{1,0:T(8,128)S(1)}, u32[]{:S(2)}, u32[]{:S(2)}) %collective-permute-start.11) | collective-permute-done | bytes 4128 | tf_op jit(solution)/shard_map/ppermute | solution.py:371
  46.2 0.6 %fusion.1 = f32[1,8,128]{2,1,0:T(8,128)} fusion(f32[8,128]{1,0:T(8,128)S(1)} %get-tuple-element.25, f32[8,128]{1,0:T(8,128)S(1)} %collective-permute-done.11, f32[2,8,128]{2,1,0:T(8,128)S(1)} %get-tuple-element.23.gain_ref), kind=kLoop, calls=%fused_computation.2 | loop fusion | flops 2048 | bytes 16384 | tf_op jit(solution)/shard_map/broadcast_in_dim | solution.py:374
  (19 shorter events, 0.1 us)
Async XLA Ops:
  0.0 0.9 %copy-start.3 = (bf16[1,64,1152]{2,1,0:T(8,128)(2,1)S(1)}, bf16[1,64,1152]{2,1,0:T(8,128)(2,1)}, u32[]{:S(2)}) copy-start(bf16[1,64,1152]{2,1,0:T(8,128)(2,1)} %param.9) | copy-start | bytes 442372
  0.0 6.1 %copy-start = (bf16[1152,3456]{1,0:T(8,128)(2,1)S(1)}, bf16[1152,3456]{1,0:T(8,128)(2,1)}, u32[]{:S(2)}) copy-start(bf16[1152,3456]{1,0:T(8,128)(2,1)} %refs_1_.1) | copy-start | bytes 23887876
  0.0 6.1 %copy-start.4 = (f32[1,5,1152]{2,0,1:T(1,128)S(1)}, f32[1,5,1152]{2,0,1:T(1,128)}, u32[]{:S(2)}) copy-start(f32[1,5,1152]{2,0,1:T(1,128)} %param.10) | copy-start | bytes 69124
  0.0 6.1 %copy-start.2 = (bf16[1,64,1152]{2,1,0:T(8,128)(2,1)S(1)}, bf16[1,64,1152]{2,1,0:T(8,128)(2,1)}, u32[]{:S(2)}) copy-start(bf16[1,64,1152]{2,1,0:T(8,128)(2,1)} %param.8) | copy-start | bytes 442372
  0.9 11.1 %collective-permute-start = (bf16[64,1152]{1,0:T(8,128)(2,1)S(1)}, bf16[64,1152]{1,0:T(8,128)(2,1)S(1)}, u32[]{:S(2)}, u32[]{:S(2)}) collective-permute-start(bf16[64,1152]{1,0:T(8,128)(2,1)S(1)} %bitcast.15), channel_id=1, source_target_pairs={{0,16},{8,24},{16,0},{24,8},{32,48},{40,56},{48,32},{56,40},{64,80... | collective-permute-start | bytes 442376 | tf_op jit(solution)/shard_map/ppermute | solution.py:42
  2.8 11.3 %collective-permute-start.5 = (bf16[64,1152]{1,0:T(8,128)(2,1)S(1)}, bf16[64,1152]{1,0:T(8,128)(2,1)S(1)}, u32[]{:S(2)}, u32[]{:S(2)}) collective-permute-start(bf16[64,1152]{1,0:T(8,128)(2,1)S(1)} %bitcast.16), channel_id=1, source_target_pairs={{0,48},{8,56},{16,32},{24,40},{32,16},{40,24},{48,0},{56,8},{64,11... | collective-permute-start | bytes 442376 | tf_op jit(solution)/shard_map/ppermute | solution.py:42
  5.6 13.5 %collective-permute-start.4 = (bf16[64,1152]{1,0:T(8,128)(2,1)S(1)}, bf16[64,1152]{1,0:T(8,128)(2,1)S(1)}, u32[]{:S(2)}, u32[]{:S(2)}) collective-permute-start(bf16[64,1152]{1,0:T(8,128)(2,1)S(1)} %bitcast.17), channel_id=1, source_target_pairs={{0,32},{8,40},{16,48},{24,56},{32,0},{40,8},{48,16},{56,24},{64,96... | collective-permute-start | bytes 442376 | tf_op jit(solution)/shard_map/ppermute | solution.py:42
  7.7 11.5 %collective-permute-start.3 = (bf16[64,1152]{1,0:T(8,128)(2,1)S(1)}, bf16[64,1152]{1,0:T(8,128)(2,1)S(1)}, u32[]{:S(2)}, u32[]{:S(2)}) collective-permute-start(bf16[64,1152]{1,0:T(8,128)(2,1)S(1)} %slice.20.q_ref), channel_id=1, source_target_pairs={{0,128},{8,136},{16,144},{24,152},{32,160},{40,168},{48,176},{56,1... | collective-permute-start | bytes 442376 | tf_op jit(solution)/shard_map/ppermute | solution.py:42
  10.9 8.2 %collective-permute-start.2 = (bf16[64,1152]{1,0:T(8,128)(2,1)S(1)}, bf16[64,1152]{1,0:T(8,128)(2,1)S(1)}, u32[]{:S(2)}, u32[]{:S(2)}) collective-permute-start(bf16[64,1152]{1,0:T(8,128)(2,1)S(1)} %slice.20.q_ref), channel_id=1, source_target_pairs={{0,192},{8,200},{16,208},{24,216},{32,224},{40,232},{48,240},{56,2... | collective-permute-start | bytes 442376 | tf_op jit(solution)/shard_map/ppermute | solution.py:42
  12.0 7.2 %collective-permute-start.1 = (bf16[64,1152]{1,0:T(8,128)(2,1)S(1)}, bf16[64,1152]{1,0:T(8,128)(2,1)S(1)}, u32[]{:S(2)}, u32[]{:S(2)}) collective-permute-start(bf16[64,1152]{1,0:T(8,128)(2,1)S(1)} %slice.20.q_ref), channel_id=1, source_target_pairs={{0,64},{8,72},{16,80},{24,88},{32,96},{40,104},{48,112},{56,120},{... | collective-permute-start | bytes 442376 | tf_op jit(solution)/shard_map/ppermute | solution.py:42
  14.2 5.1 %collective-permute-start.6 = (bf16[128,2304]{1,0:T(8,128)(2,1)S(1)}, bf16[128,2304]{1,0:T(8,128)(2,1)S(1)}, u32[]{:S(2)}, u32[]{:S(2)}) collective-permute-start(bf16[128,2304]{1,0:T(8,128)(2,1)S(1)} %stale_kv.2.kv0.refs_0_), channel_id=1, source_target_pairs={{0,8},{8,0},{16,24},{24,16},{32,40},{40,32},{48,56},{56,48},{64,72... | collective-permute-start | bytes 1769480 | tf_op jit(solution)/shard_map/ppermute | solution.py:42
  19.2 12.7 %copy-start.6 = (f32[1,8,128]{2,1,0:T(8,128)S(1)}, f32[1,8,128]{2,1,0:T(8,128)}, u32[]{:S(2)}) copy-start(f32[1,8,128]{2,1,0:T(8,128)} %param.11) | copy-start | bytes 12292
  19.2 12.6 %copy-start.7 = (s32[4]{0:T(128)S(1)}, s32[4]{0:T(128)}, u32[]{:S(2)}) copy-start(s32[4]{0:T(128)} %time_ref.1) | copy-start | bytes 52
  19.3 17.8 %copy-start.1 = (bf16[1152,1152]{1,0:T(8,128)(2,1)S(1)}, bf16[1152,1152]{1,0:T(8,128)(2,1)}, u32[]{:S(2)}) copy-start(bf16[1152,1152]{1,0:T(8,128)(2,1)} %w_out_ref.1) | copy-start | bytes 7962628
  19.3 17.8 %copy-start.5 = (bf16[1152,16]{0,1:T(8,128)(2,1)S(1)}, bf16[1152,16]{0,1:T(8,128)(2,1)}, u32[]{:S(2)}) copy-start(bf16[1152,16]{0,1:T(8,128)(2,1)} %param.15) | copy-start | bytes 110596
  20.5 2.1 %collective-permute-start.7 = (bf16[128,2304]{1,0:T(8,128)(2,1)S(1)}, bf16[128,2304]{1,0:T(8,128)(2,1)S(1)}, u32[]{:S(2)}, u32[]{:S(2)}) collective-permute-start(bf16[128,2304]{1,0:T(8,128)(2,1)S(1)} %stale_kv.3.kv1.refs_1_), channel_id=1, source_target_pairs={{0,8},{8,0},{16,24},{24,16},{32,40},{40,32},{48,56},{56,48},{64,72... | collective-permute-start | bytes 1769480 | tf_op jit(solution)/shard_map/ppermute | solution.py:42
  25.4 8.6 %collective-permute-start.10 = (bf16[64,1280]{1,0:T(8,128)(2,1)S(1)}, bf16[64,1280]{1,0:T(8,128)(2,1)S(1)}, u32[]{:S(2)}, u32[]{:S(2)}) collective-permute-start(bf16[64,1280]{1,0:T(8,128)(2,1)S(1)} %get-tuple-element.27), channel_id=1, source_target_pairs={{0,128},{8,136},{16,144},{24,152},{32,160},{40,168},{48,176},{56,1... | collective-permute-start | bytes 491528 | tf_op jit(solution)/shard_map/ppermute | solution.py:42
  28.6 8.1 %collective-permute-start.9 = (bf16[64,1280]{1,0:T(8,128)(2,1)S(1)}, bf16[64,1280]{1,0:T(8,128)(2,1)S(1)}, u32[]{:S(2)}, u32[]{:S(2)}) collective-permute-start(bf16[64,1280]{1,0:T(8,128)(2,1)S(1)} %get-tuple-element.28), channel_id=1, source_target_pairs={{0,64},{8,72},{16,80},{24,88},{32,96},{40,104},{48,112},{56,120},{... | collective-permute-start | bytes 491528 | tf_op jit(solution)/shard_map/ppermute | solution.py:42
  29.3 7.7 %collective-permute-start.8 = (bf16[64,1280]{1,0:T(8,128)(2,1)S(1)}, bf16[64,1280]{1,0:T(8,128)(2,1)S(1)}, u32[]{:S(2)}, u32[]{:S(2)}) collective-permute-start(bf16[64,1280]{1,0:T(8,128)(2,1)S(1)} %get-tuple-element.29), channel_id=1, source_target_pairs={{0,192},{8,200},{16,208},{24,216},{32,224},{40,232},{48,240},{56,2... | collective-permute-start | bytes 491528 | tf_op jit(solution)/shard_map/ppermute | solution.py:42
  38.6 7.6 %collective-permute-start.11 = (f32[8,128]{1,0:T(8,128)S(1)}, f32[8,128]{1,0:T(8,128)S(1)}, u32[]{:S(2)}, u32[]{:S(2)}) collective-permute-start(f32[8,128]{1,0:T(8,128)S(1)} %get-tuple-element.26), channel_id=1, source_target_pairs={{0,1},{1,0},{2,3},{3,2},{4,5},{5,4},{6,7},{7,6},{8,9},{9,8},{10,11... | collective-permute-start | bytes 12296 | tf_op jit(solution)/shard_map/ppermute | solution.py:371

commit v5 on v4

--- a/solution.py
+++ b/solution.py
@@ -347,13 +347,14 @@
     mod = jnp.transpose(modulation, (1, 0, 2))
     rows = hidden.shape[0]
 
-    stale, pick = lax.optimization_barrier((stale, head_selector()))
-    stale_1, stale_2, stale_3 = [send(stale, z_xor(mask)) for mask in (1, 2, 3)]
+    sent, pick = lax.optimization_barrier((stale, head_selector()))
+    stale_1 = send(stale, z_xor(1))
+    stale_2, stale_3 = [send(sent, z_xor(mask)) for mask in (2, 3)]
     fresh = project_fresh(hidden, mod, w_qkv)
     query = fresh[:, :WIDTH]
     query_up, query_down, query_far = [send(query, y_shift(step)) for step in (1, -1, 2)]
 
-    early = project_stale([stale, stale_1], w_qkv, 1)
+    early = project_stale([stale, stale_1], w_qkv, 2 * 10**10)
     early_other = send(early, other_core)
     queries, blocks = gather_blocks((query_up, query_down, query_far), (stale_2, stale_3))
     blocks, early_other = lax.optimization_barrier((blocks, early_other))

time: 46.8 us -> 46.2 us (0.987)
  local copies, waits for them, and re-layouts: 0.92 us -> 0.09 us
  starting transfers between devices: 22.5 us -> 23 us
    unnamed x16 -> x18, local copies, waits for them, and re-layouts: 0.87 us -> 0.04 us
where the time goes in v5:
time: 46.2 us; the launch traced here: 46.1 us
  starting transfers between devices  23 us (50%)
  waiting for transfers between devices  12.2 us (26%)
  Pallas kernels  10.1 us (22%)
  other arithmetic  0.6 us (1%)
    ppermute x11, starting transfers between devices, send(): return lax.ppermute(value, 'patch', pairs)  17.6 us
    ppermute x11, waiting for transfers between devices, send(): return lax.ppermute(value, 'patch', pairs)  9.95 us
    ppermute x1, starting transfers between devices, body(): lax.ppermute(noise, 'guide', [(i, i ^ 1) for i in range(lax.axis_size('gu...  5.36 us
    pallas_call x1, Pallas kernels, attend(): pl.pallas_call(attend_kernel, in_specs=[pl.BlockSpec(memory_space=pltpu.V...  2.76 us
    pallas_call x2, Pallas kernels, project_stale(): pl.pallas_call(stale_kernel, in_specs=[pl.BlockSpec(memory_space=pltpu.VM...  2.32 us
    ppermute x1, waiting for transfers between devices, body(): lax.ppermute(noise, 'guide', [(i, i ^ 1) for i in range(lax.axis_size('gu...  2.24 us
    pallas_call x1, Pallas kernels, attend_own(): pl.pallas_call(attend_own_kernel, in_specs=[vmem] * 6 + [pl.BlockSpec(mem...  1.83 us
    pallas_call x1, Pallas kernels, project_fresh(): pl.pallas_call(fresh_kernel, in_specs=[pl.BlockSpec(memory_space=pltpu.VM...  1.53 us
  transfers between devices with their start and end apart: 12, of which 6 were waited for; matrix products, arithmetic and copies ran while one was open for 0% of the time, Pallas kernels for 10%

profile of v5, /device:TPU:2, one launch (start us, length us, event | category | flops | bytes accessed | tf_op | source)
XLA Modules:
  0.0 46.1 jit_solution(18103252918520785095)
XLA Ops:
  0.0 2.0 %collective-permute-start = (bf16[64,1152]{1,0:T(8,128)(2,1)}, bf16[64,1152]{1,0:T(8,128)(2,1)S(1)}, u32[]{:S(2)}, u32[]{:S(2)}) collective-permute-start(bf16[64,1152]{1,0:T(8,128)(2,1)} %bitcast.21), channel_id=1, source_target_pairs={{0,16},{8,24},{16,0},{24,8},{32,48},{40,56},{48,32},{56,40},{64,80... | collective-permute-start | bytes 442376 | tf_op jit(solution)/shard_map/ppermute | solution.py:42
  2.1 3.6 %collective-permute-start.5 = (bf16[64,1152]{1,0:T(8,128)(2,1)S(1)}, bf16[64,1152]{1,0:T(8,128)(2,1)S(1)}, u32[]{:S(2)}, u32[]{:S(2)}) collective-permute-start(bf16[64,1152]{1,0:T(8,128)(2,1)S(1)} %bitcast.22), channel_id=1, source_target_pairs={{0,48},{8,56},{16,32},{24,40},{32,16},{40,24},{48,0},{56,8},{64,11... | collective-permute-start | bytes 442376 | tf_op jit(solution)/shard_map/ppermute | solution.py:42
  5.7 0.0 collective-permute-start.4
  5.7 1.5 %fresh_qkv.1.fresh_ref = bf16[64,3456]{1,0:T(8,128)(2,1)S(1)} custom-call(bf16[64,1152]{1,0:T(8,128)(2,1)S(1)} %bitcast.15, f32[5,1,1152]{2,1,0:T(1,128)S(1)} %bitcast.17, bf16[1152,3456]{1,0:T(8,128)(2,1)S(1)} %bitcast.14), custom_call_target="tpu_custom_call" | custom-call | flops 509607936 | bytes 7962624 | tf_op jit(solution)/shard_map/fresh_qkv/pallas_call | solution.py:90
  7.3 3.3 %collective-permute-start.3 = (bf16[64,1152]{1,0:T(8,128)(2,1)S(1)}, bf16[64,1152]{1,0:T(8,128)(2,1)S(1)}, u32[]{:S(2)}, u32[]{:S(2)}) collective-permute-start(bf16[64,1152]{1,0:T(8,128)(2,1)S(1)} %slice.20.q_ref), channel_id=1, source_target_pairs={{0,128},{8,136},{16,144},{24,152},{32,160},{40,168},{48,176},{56,1... | collective-permute-start | bytes 442376 | tf_op jit(solution)/shard_map/ppermute | solution.py:42
  10.6 1.1 %collective-permute-start.2 = (bf16[64,1152]{1,0:T(8,128)(2,1)S(1)}, bf16[64,1152]{1,0:T(8,128)(2,1)S(1)}, u32[]{:S(2)}, u32[]{:S(2)}) collective-permute-start(bf16[64,1152]{1,0:T(8,128)(2,1)S(1)} %slice.20.q_ref), channel_id=1, source_target_pairs={{0,192},{8,200},{16,208},{24,216},{32,224},{40,232},{48,240},{56,2... | collective-permute-start | bytes 442376 | tf_op jit(solution)/shard_map/ppermute | solution.py:42
  11.6 0.0 collective-permute-done.refs_1_
  11.6 1.0 %collective-permute-start.1 = (bf16[64,1152]{1,0:T(8,128)(2,1)S(1)}, bf16[64,1152]{1,0:T(8,128)(2,1)S(1)}, u32[]{:S(2)}, u32[]{:S(2)}) collective-permute-start(bf16[64,1152]{1,0:T(8,128)(2,1)S(1)} %slice.20.q_ref), channel_id=1, source_target_pairs={{0,64},{8,72},{16,80},{24,88},{32,96},{40,104},{48,112},{56,120},{... | collective-permute-start | bytes 442376 | tf_op jit(solution)/shard_map/ppermute | solution.py:42
  12.6 1.2 %stale_kv.2.kv0.refs_0_ = bf16[128,2304]{1,0:T(8,128)(2,1)S(1)} custom-call(bf16[64,1152]{1,0:T(8,128)(2,1)S(1)} %bitcast.24, bf16[64,1152]{1,0:T(8,128)(2,1)S(1)} %collective-permute-done.refs_1_, bf16[1152,3456]{1,0:T(8,128)(2,1)S(1)} %bitcast.14), custom_call_target="tpu_custom_call" | custom-call | flops 20000000000 | bytes 1 | tf_op jit(solution)/shard_map/stale_kv/pallas_call | solution.py:118
  13.8 0.1 collective-permute-start.6
  13.9 4.6 %collective-permute-done.4.refs_3_ = bf16[64,1152]{1,0:T(8,128)(2,1)S(1)} collective-permute-done((bf16[64,1152]{1,0:T(8,128)(2,1)S(1)}, bf16[64,1152]{1,0:T(8,128)(2,1)S(1)}, u32[]{:S(2)}, u32[]{:S(2)}) %collective-permute-start.4) | collective-permute-done | bytes 147488 | tf_op jit(solution)/shard_map/ppermute | solution.py:42
  18.5 0.0 collective-permute-done.1.refs_0_
  18.5 0.1 gather_blocks.1
  18.6 0.0 copy-start.4
  18.6 0.0 copy-start.5
  18.6 0.0 copy-start
  18.6 0.0 copy-start.3
  18.6 1.2 %stale_kv.3.kv1.refs_1_ = bf16[128,2304]{1,0:T(8,128)(2,1)S(1)} custom-call(bf16[128,1152]{1,0:T(8,128)(2,1)S(1)} %get-tuple-element.18.refs_0_, bf16[1152,3456]{1,0:T(8,128)(2,1)S(1)} %bitcast.14), custom_call_target="tpu_custom_call" | custom-call | flops 1 | bytes 1 | tf_op jit(solution)/shard_map/stale_kv/pallas_call | solution.py:118
  19.8 0.1 collective-permute-start.7
  19.9 2.0 %collective-permute-done.7.kv3.refs_3_ = bf16[128,2304]{1,0:T(8,128)(2,1)S(1)} collective-permute-done((bf16[128,2304]{1,0:T(8,128)(2,1)S(1)}, bf16[128,2304]{1,0:T(8,128)(2,1)S(1)}, u32[]{:S(2)}, u32[]{:S(2)}) %collective-permute-start.7) | collective-permute-done | bytes 589856 | tf_op jit(solution)/shard_map/ppermute | solution.py:42
  21.9 2.8 %attend.1 = bf16[192,1280]{1,0:T(8,128)(2,1)S(1)} custom-call(bf16[192,1152]{1,0:T(8,128)(2,1)S(1)} %get-tuple-element.21.q_ref, bf16[128,2304]{1,0:T(8,128)(2,1)S(1)} %stale_kv.2.kv0.refs_0_, bf16[128,2304]{1,0:T(8,128)(2,1)S(1)} %stale_kv.3.kv1.refs_1_, bf16[128,2304]{1,0:T(8,128)(2,1)S(1)} %collective-permute-done.6.kv2.refs_2_, ...), custom_call_target="tpu_custom_call" | custom-call | flops 1610612736 | bytes 2359296 | tf_op jit(solution)/shard_map/attend/pallas_call | solution.py:253
  24.7 3.3 %collective-permute-start.10 = (bf16[64,1280]{1,0:T(8,128)(2,1)S(1)}, bf16[64,1280]{1,0:T(8,128)(2,1)S(1)}, u32[]{:S(2)}, u32[]{:S(2)}) collective-permute-start(bf16[64,1280]{1,0:T(8,128)(2,1)S(1)} %get-tuple-element.27), channel_id=1, source_target_pairs={{0,128},{8,136},{16,144},{24,152},{32,160},{40,168},{48,176},{56,1... | collective-permute-start | bytes 491528 | tf_op jit(solution)/shard_map/ppermute | solution.py:42
  28.0 0.7 %collective-permute-start.9 = (bf16[64,1280]{1,0:T(8,128)(2,1)S(1)}, bf16[64,1280]{1,0:T(8,128)(2,1)S(1)}, u32[]{:S(2)}, u32[]{:S(2)}) collective-permute-start(bf16[64,1280]{1,0:T(8,128)(2,1)S(1)} %get-tuple-element.28), channel_id=1, source_target_pairs={{0,64},{8,72},{16,80},{24,88},{32,96},{40,104},{48,112},{56,120},{... | collective-permute-start | bytes 491528 | tf_op jit(solution)/shard_map/ppermute | solution.py:42
  28.7 2.6 %collective-permute-start.8 = (bf16[64,1280]{1,0:T(8,128)(2,1)S(1)}, bf16[64,1280]{1,0:T(8,128)(2,1)S(1)}, u32[]{:S(2)}, u32[]{:S(2)}) collective-permute-start(bf16[64,1280]{1,0:T(8,128)(2,1)S(1)} %get-tuple-element.29), channel_id=1, source_target_pairs={{0,192},{8,200},{16,208},{24,216},{32,224},{40,232},{48,240},{56,2... | collective-permute-start | bytes 491528 | tf_op jit(solution)/shard_map/ppermute | solution.py:42
  31.2 1.8 %attend_own.1 = (bf16[64,1280]{1,0:T(8,128)(2,1)S(1)}, f32[8,128]{1,0:T(8,128)S(1)}, f32[2,8,128]{2,1,0:T(8,128)S(1)}) custom-call(bf16[64,1152]{1,0:T(8,128)(2,1)S(1)} %slice.20.q_ref, bf16[128,2304]{1,0:T(8,128)(2,1)S(1)} %stale_kv.2.kv0.refs_0_, bf16[128,2304]{1,0:T(8,128)(2,1)S(1)} %stale_kv.3.kv1.refs_1_, ...), custom_call_target="tpu_custom_call" | custom-call | flops 536870912 | bytes 2359296 | tf_op jit(solution)/shard_map/attend_own/pallas_call | solution.py:283
  33.1 0.3 collective-permute-done.10.p3
  33.4 2.7 %collective-permute-done.9.p2 = bf16[64,1280]{1,0:T(8,128)(2,1)S(1)} collective-permute-done((bf16[64,1280]{1,0:T(8,128)(2,1)S(1)}, bf16[64,1280]{1,0:T(8,128)(2,1)S(1)}, u32[]{:S(2)}, u32[]{:S(2)}) %collective-permute-start.9) | collective-permute-done | bytes 163872 | tf_op jit(solution)/shard_map/ppermute | solution.py:42
  36.1 0.3 collective-permute-done.8.p1
  36.4 1.5 %post.1 = (f32[8,128]{1,0:T(8,128)S(1)}, f32[8,128]{1,0:T(8,128)S(1)}) custom-call(bf16[64,1280]{1,0:T(8,128)(2,1)S(1)} %get-tuple-element.20.p0, bf16[64,1280]{1,0:T(8,128)(2,1)S(1)} %collective-permute-done.8.p1, bf16[64,1280]{1,0:T(8,128)(2,1)S(1)} %collective-permute-done.9.p2, bf16[64,1280]{1,0:T(8,128)(2,1)S(1)} %collective-permute-done.10.p3, ...), custom_call_target="tpu_custom_call" | custom-call | flops 169869312 | bytes 2654208 | tf_op jit(solution)/shard_map/post/pallas_call | solution.py:332
  37.9 5.4 %collective-permute-start.11 = (f32[8,128]{1,0:T(8,128)S(1)}, f32[8,128]{1,0:T(8,128)S(1)}, u32[]{:S(2)}, u32[]{:S(2)}) collective-permute-start(f32[8,128]{1,0:T(8,128)S(1)} %get-tuple-element.26), channel_id=1, source_target_pairs={{0,1},{1,0},{2,3},{3,2},{4,5},{5,4},{6,7},{7,6},{8,9},{9,8},{10,11... | collective-permute-start | bytes 12296 | tf_op jit(solution)/shard_map/ppermute | solution.py:372
  43.3 2.2 %collective-permute-done.11 = f32[8,128]{1,0:T(8,128)S(1)} collective-permute-done((f32[8,128]{1,0:T(8,128)S(1)}, f32[8,128]{1,0:T(8,128)S(1)}, u32[]{:S(2)}, u32[]{:S(2)}) %collective-permute-start.11) | collective-permute-done | bytes 4128 | tf_op jit(solution)/shard_map/ppermute | solution.py:372
  45.5 0.6 %fusion.1 = f32[1,8,128]{2,1,0:T(8,128)} fusion(f32[8,128]{1,0:T(8,128)S(1)} %get-tuple-element.25, f32[8,128]{1,0:T(8,128)S(1)} %collective-permute-done.11, f32[2,8,128]{2,1,0:T(8,128)S(1)} %get-tuple-element.23.gain_ref), kind=kLoop, calls=%fused_computation.2 | loop fusion | flops 2048 | bytes 16384 | tf_op jit(solution)/shard_map/broadcast_in_dim | solution.py:375
  (22 shorter events, 0.1 us)
Async XLA Ops:
  0.0 5.7 %slice-start = ((s8[7962624]{0:T(1024)(128)(4,1)}), s8[4194304]{0:T(1024)(128)(4,1)S(1)}, s32[]{:S(2)}) async-start(s8[7962624]{0:T(1024)(128)(4,1)} %bitcast.13), calls=%async_computation | async-start | bytes 8388608
  0.0 2.1 %copy-start.6 = (bf16[1,64,1152]{2,1,0:T(8,128)(2,1)S(1)}, bf16[1,64,1152]{2,1,0:T(8,128)(2,1)}, u32[]{:S(2)}) copy-start(bf16[1,64,1152]{2,1,0:T(8,128)(2,1)} %param.9) | copy-start | bytes 442372
  0.0 5.7 %slice-start.1 = ((s8[7962624]{0:T(1024)(128)(4,1)}), s8[3768320]{0:T(1024)(128)(4,1)S(1)}, s32[]{:S(2)}) async-start(s8[7962624]{0:T(1024)(128)(4,1)} %bitcast.13), calls=%async_computation.1 | async-start | bytes 7536640
  0.0 5.7 %copy-start.1 = (bf16[1,64,1152]{2,1,0:T(8,128)(2,1)S(1)}, bf16[1,64,1152]{2,1,0:T(8,128)(2,1)}, u32[]{:S(2)}) copy-start(bf16[1,64,1152]{2,1,0:T(8,128)(2,1)} %param.8) | copy-start | bytes 442372
  0.0 5.7 %copy-start.2 = (f32[1,5,1152]{2,0,1:T(1,128)S(1)}, f32[1,5,1152]{2,0,1:T(1,128)}, u32[]{:S(2)}) copy-start(f32[1,5,1152]{2,0,1:T(1,128)} %param.10) | copy-start | bytes 69124
  0.0 11.6 %collective-permute-start = (bf16[64,1152]{1,0:T(8,128)(2,1)}, bf16[64,1152]{1,0:T(8,128)(2,1)S(1)}, u32[]{:S(2)}, u32[]{:S(2)}) collective-permute-start(bf16[64,1152]{1,0:T(8,128)(2,1)} %bitcast.21), channel_id=1, source_target_pairs={{0,16},{8,24},{16,0},{24,8},{32,48},{40,56},{48,32},{56,40},{64,80... | collective-permute-start | bytes 442376 | tf_op jit(solution)/shard_map/ppermute | solution.py:42
  2.1 11.7 %collective-permute-start.5 = (bf16[64,1152]{1,0:T(8,128)(2,1)S(1)}, bf16[64,1152]{1,0:T(8,128)(2,1)S(1)}, u32[]{:S(2)}, u32[]{:S(2)}) collective-permute-start(bf16[64,1152]{1,0:T(8,128)(2,1)S(1)} %bitcast.22), channel_id=1, source_target_pairs={{0,48},{8,56},{16,32},{24,40},{32,16},{40,24},{48,0},{56,8},{64,11... | collective-permute-start | bytes 442376 | tf_op jit(solution)/shard_map/ppermute | solution.py:42
  5.7 12.8 %collective-permute-start.4 = (bf16[64,1152]{1,0:T(8,128)(2,1)S(1)}, bf16[64,1152]{1,0:T(8,128)(2,1)S(1)}, u32[]{:S(2)}, u32[]{:S(2)}) collective-permute-start(bf16[64,1152]{1,0:T(8,128)(2,1)S(1)} %bitcast.23), channel_id=1, source_target_pairs={{0,32},{8,40},{16,48},{24,56},{32,0},{40,8},{48,16},{56,24},{64,96... | collective-permute-start | bytes 442376 | tf_op jit(solution)/shard_map/ppermute | solution.py:42
  7.3 11.2 %collective-permute-start.3 = (bf16[64,1152]{1,0:T(8,128)(2,1)S(1)}, bf16[64,1152]{1,0:T(8,128)(2,1)S(1)}, u32[]{:S(2)}, u32[]{:S(2)}) collective-permute-start(bf16[64,1152]{1,0:T(8,128)(2,1)S(1)} %slice.20.q_ref), channel_id=1, source_target_pairs={{0,128},{8,136},{16,144},{24,152},{32,160},{40,168},{48,176},{56,1... | collective-permute-start | bytes 442376 | tf_op jit(solution)/shard_map/ppermute | solution.py:42
  10.6 7.9 %collective-permute-start.2 = (bf16[64,1152]{1,0:T(8,128)(2,1)S(1)}, bf16[64,1152]{1,0:T(8,128)(2,1)S(1)}, u32[]{:S(2)}, u32[]{:S(2)}) collective-permute-start(bf16[64,1152]{1,0:T(8,128)(2,1)S(1)} %slice.20.q_ref), channel_id=1, source_target_pairs={{0,192},{8,200},{16,208},{24,216},{32,224},{40,232},{48,240},{56,2... | collective-permute-start | bytes 442376 | tf_op jit(solution)/shard_map/ppermute | solution.py:42
  11.6 6.9 %collective-permute-start.1 = (bf16[64,1152]{1,0:T(8,128)(2,1)S(1)}, bf16[64,1152]{1,0:T(8,128)(2,1)S(1)}, u32[]{:S(2)}, u32[]{:S(2)}) collective-permute-start(bf16[64,1152]{1,0:T(8,128)(2,1)S(1)} %slice.20.q_ref), channel_id=1, source_target_pairs={{0,64},{8,72},{16,80},{24,88},{32,96},{40,104},{48,112},{56,120},{... | collective-permute-start | bytes 442376 | tf_op jit(solution)/shard_map/ppermute | solution.py:42
  13.8 4.8 %collective-permute-start.6 = (bf16[128,2304]{1,0:T(8,128)(2,1)S(1)}, bf16[128,2304]{1,0:T(8,128)(2,1)S(1)}, u32[]{:S(2)}, u32[]{:S(2)}) collective-permute-start(bf16[128,2304]{1,0:T(8,128)(2,1)S(1)} %stale_kv.2.kv0.refs_0_), channel_id=1, source_target_pairs={{0,8},{8,0},{16,24},{24,16},{32,40},{40,32},{48,56},{56,48},{64,72... | collective-permute-start | bytes 1769480 | tf_op jit(solution)/shard_map/ppermute | solution.py:42
  18.6 12.7 %copy-start.4 = (f32[1,8,128]{2,1,0:T(8,128)S(1)}, f32[1,8,128]{2,1,0:T(8,128)}, u32[]{:S(2)}) copy-start(f32[1,8,128]{2,1,0:T(8,128)} %param.11) | copy-start | bytes 12292
  18.6 12.6 %copy-start.5 = (s32[4]{0:T(128)S(1)}, s32[4]{0:T(128)}, u32[]{:S(2)}) copy-start(s32[4]{0:T(128)} %time_ref.1) | copy-start | bytes 52
  18.6 17.8 %copy-start = (bf16[1152,1152]{1,0:T(8,128)(2,1)S(1)}, bf16[1152,1152]{1,0:T(8,128)(2,1)}, u32[]{:S(2)}) copy-start(bf16[1152,1152]{1,0:T(8,128)(2,1)} %w_out_ref.1) | copy-start | bytes 7962628
  18.6 17.8 %copy-start.3 = (bf16[1152,16]{0,1:T(8,128)(2,1)S(1)}, bf16[1152,16]{0,1:T(8,128)(2,1)}, u32[]{:S(2)}) copy-start(bf16[1152,16]{0,1:T(8,128)(2,1)} %param.15) | copy-start | bytes 110596
  19.8 2.1 %collective-permute-start.7 = (bf16[128,2304]{1,0:T(8,128)(2,1)S(1)}, bf16[128,2304]{1,0:T(8,128)(2,1)S(1)}, u32[]{:S(2)}, u32[]{:S(2)}) collective-permute-start(bf16[128,2304]{1,0:T(8,128)(2,1)S(1)} %stale_kv.3.kv1.refs_1_), channel_id=1, source_target_pairs={{0,8},{8,0},{16,24},{24,16},{32,40},{40,32},{48,56},{56,48},{64,72... | collective-permute-start | bytes 1769480 | tf_op jit(solution)/shard_map/ppermute | solution.py:42
  24.7 8.6 %collective-permute-start.10 = (bf16[64,1280]{1,0:T(8,128)(2,1)S(1)}, bf16[64,1280]{1,0:T(8,128)(2,1)S(1)}, u32[]{:S(2)}, u32[]{:S(2)}) collective-permute-start(bf16[64,1280]{1,0:T(8,128)(2,1)S(1)} %get-tuple-element.27), channel_id=1, source_target_pairs={{0,128},{8,136},{16,144},{24,152},{32,160},{40,168},{48,176},{56,1... | collective-permute-start | bytes 491528 | tf_op jit(solution)/shard_map/ppermute | solution.py:42
  28.0 8.1 %collective-permute-start.9 = (bf16[64,1280]{1,0:T(8,128)(2,1)S(1)}, bf16[64,1280]{1,0:T(8,128)(2,1)S(1)}, u32[]{:S(2)}, u32[]{:S(2)}) collective-permute-start(bf16[64,1280]{1,0:T(8,128)(2,1)S(1)} %get-tuple-element.28), channel_id=1, source_target_pairs={{0,64},{8,72},{16,80},{24,88},{32,96},{40,104},{48,112},{56,120},{... | collective-permute-start | bytes 491528 | tf_op jit(solution)/shard_map/ppermute | solution.py:42
  28.7 7.7 %collective-permute-start.8 = (bf16[64,1280]{1,0:T(8,128)(2,1)S(1)}, bf16[64,1280]{1,0:T(8,128)(2,1)S(1)}, u32[]{:S(2)}, u32[]{:S(2)}) collective-permute-start(bf16[64,1280]{1,0:T(8,128)(2,1)S(1)} %get-tuple-element.29), channel_id=1, source_target_pairs={{0,192},{8,200},{16,208},{24,216},{32,224},{40,232},{48,240},{56,2... | collective-permute-start | bytes 491528 | tf_op jit(solution)/shard_map/ppermute | solution.py:42
  37.9 7.6 %collective-permute-start.11 = (f32[8,128]{1,0:T(8,128)S(1)}, f32[8,128]{1,0:T(8,128)S(1)}, u32[]{:S(2)}, u32[]{:S(2)}) collective-permute-start(f32[8,128]{1,0:T(8,128)S(1)} %get-tuple-element.26), channel_id=1, source_target_pairs={{0,1},{1,0},{2,3},{3,2},{4,5},{5,4},{6,7},{7,6},{8,9},{9,8},{10,11... | collective-permute-start | bytes 12296 | tf_op jit(solution)/shard_map/ppermute | solution.py:372

commit v6 on v5

--- a/solution.py
+++ b/solution.py
@@ -179,8 +179,7 @@
     return jnp.where(split == 0, high.astype(F32), packed)
 
 
-def attend_kernel(q_ref, *refs, fresh_ref=None):
-    *keyval, out_ref = refs
+def attend_part(q_ref, keyval, fresh_ref=None):
     rows = q_ref.shape[0]
     scale = HEAD ** (-0.5)
     lane = lax.broadcasted_iota(jnp.int32, (rows, 256), 1)
@@ -234,10 +233,36 @@
                     piece = picked[:, 128 * j : 128 * j + 128]
                     blocks[block] = piece if blocks[block] is None else blocks[block] + piece
                 stats = jnp.where(stat_lane % HEADS == head, stat[mine], stats)
-    packed = split_stats(stats, stat_lane)
+    return blocks, stats, stat_lane
+
+
+def write_packed(out_ref, blocks, stats, lane):
     for block, values in enumerate(blocks):
         out_ref[:, 128 * block : 128 * block + 128] = values.astype(BF16)
-    out_ref[:, WIDTH:] = packed.astype(BF16)
+    out_ref[:, WIDTH:] = split_stats(stats, lane).astype(BF16)
+
+
+def attend_early_kernel(q_ref, kv0, kv1, out_ref, stats_ref):
+    blocks, stats, _ = attend_part(q_ref, (kv0, kv1))
+    for block, values in enumerate(blocks):
+        out_ref[:, 128 * block : 128 * block + 128] = values
+    stats_ref[...] = stats
+
+
+def attend_late_kernel(q_ref, kv0, kv1, early_ref, stats_ref, pick_ref, out_ref):
+    blocks, stats, lane = attend_part(q_ref, (kv0, kv1))
+    first = stats_ref[...]
+    top = jnp.maximum(first, stats)
+    weights = [jnp.exp(first - top), jnp.exp(stats - top)]
+    total = weights[0] + weights[1]
+    weights = [split_stats(w / total, lane).astype(BF16) for w in weights]
+    pick = pick_ref[...]
+    weights = [jnp.dot(w, pick, preferred_element_type=F32) for w in weights]
+    mixed = []
+    for block, values in enumerate(blocks):
+        cols = slice(128 * block, 128 * block + 128)
+        mixed.append(weights[0][:, cols] * early_ref[:, cols] + weights[1][:, cols] * values)
+    write_packed(out_ref, mixed, top + jnp.log(total), lane)
 
 
 def attend_cost(rows, keys):
@@ -248,17 +273,34 @@
     )
 
 
-def attend(query, keyval):
+def attend_early(query, keyval):
     rows = query.shape[0]
-    return pl.pallas_call(
-        attend_kernel,
-        in_specs=[pl.BlockSpec(memory_space=pltpu.VMEM)] * (1 + len(keyval)),
+    vmem = pl.BlockSpec(memory_space=pltpu.VMEM)
+    return pl.pallas_call(
+        attend_early_kernel,
+        in_specs=[vmem] * 3,
+        out_specs=[vmem] * 2,
+        out_shape=[
+            jax.ShapeDtypeStruct((rows, WIDTH), F32),
+            jax.ShapeDtypeStruct((rows, STATS), F32),
+        ],
+        compiler_params=pltpu.CompilerParams(vmem_limit_bytes=VMEM_LIMIT),
+        cost_estimate=pl.CostEstimate(flops=1, bytes_accessed=1, transcendentals=0),
+        name="attend_early",
+    )(query, *keyval)
+
+
+def attend_late(query, keyval, first, pick):
+    rows = query.shape[0]
+    return pl.pallas_call(
+        attend_late_kernel,
+        in_specs=[pl.BlockSpec(memory_space=pltpu.VMEM)] * 6,
         out_specs=pl.BlockSpec(memory_space=pltpu.VMEM),
         out_shape=jax.ShapeDtypeStruct((rows, WIDTH + STATS), BF16),
         compiler_params=pltpu.CompilerParams(vmem_limit_bytes=VMEM_LIMIT),
-        cost_estimate=attend_cost(rows, sum(x.shape[0] for x in keyval)),
-        name="attend",
-    )(query, *keyval)
+        cost_estimate=pl.CostEstimate(flops=1, bytes_accessed=1, transcendentals=0),
+        name="attend_late",
+    )(query, *keyval, *first, pick)
 
 
 def attend_own_kernel(
@@ -274,7 +316,7 @@
     base_ref[...] = latent_gain * latent_ref[...]
     gain_ref[0] = noise_gain * jnp.where(is_cond, 4.5, -3.5)
     gain_ref[1] = noise_gain * jnp.where(is_cond, -3.5, 4.5)
-    attend_kernel(q_ref, kv0, kv1, kv2, kv3, out_ref, fresh_ref=fresh_ref)
+    write_packed(out_ref, *attend_part(q_ref, (kv0, kv1, kv2, kv3), fresh_ref))
 
 
 def attend_own(query, keyval, fresh, timestep, latent):
@@ -362,7 +404,8 @@
     late_other = send(late, other_core)
     keyval = (early, late, early_other, late_other)
 
-    partial = attend(queries, keyval)
+    first = attend_early(queries, (early, early_other))
+    partial = attend_late(queries, (late, late_other), first, pick)
     back = [
         send(partial[n * rows : (n + 1) * rows], y_shift(step))
         for n, step in enumerate((-1, 1, -2))

time: 46.2 us -> 45.7 us (0.989)
  waiting for transfers between devices: 12.2 us -> 10.6 us
  Pallas kernels: 10.1 us -> 11 us
    ppermute x11, waiting for transfers between devices: 9.95 us -> 8.33 us  [send(): return lax.ppermute(value, 'patch', pairs)]
    pallas_call x1 -> x2, Pallas kernels: 2.76 us -> 3.7 us  [the longest x1 2.07 us: attend_late(): pl.pallas_call(attend_late_kernel, in_specs=[pl.BlockSpec(memory_space=pl...]
  transfers between devices with their start and end apart: 12 -> 12, of which waited for: 6 -> 6; matrix products, arithmetic and copies ran while one was open for 0% -> 0% of each run, Pallas kernels for 10% -> 14%
where the time goes in v6:
time: 45.7 us; the launch traced here: 45.6 us
  starting transfers between devices  23.2 us (51%)
  Pallas kernels  11 us (24%)
  waiting for transfers between devices  10.6 us (23%)
  other arithmetic  0.6 us (1%)
    ppermute x11, starting transfers between devices, send(): return lax.ppermute(value, 'patch', pairs)  17.8 us
    ppermute x11, waiting for transfers between devices, send(): return lax.ppermute(value, 'patch', pairs)  8.33 us
    ppermute x1, starting transfers between devices, body(): lax.ppermute(noise, 'guide', [(i, i ^ 1) for i in range(lax.axis_size('gu...  5.36 us
    pallas_call x2, Pallas kernels, project_stale(): pl.pallas_call(stale_kernel, in_specs=[pl.BlockSpec(memory_space=pltpu.VM...  2.32 us
    ppermute x1, waiting for transfers between devices, body(): lax.ppermute(noise, 'guide', [(i, i ^ 1) for i in range(lax.axis_size('gu...  2.24 us
    pallas_call x1, Pallas kernels, attend_late(): pl.pallas_call(attend_late_kernel, in_specs=[pl.BlockSpec(memory_space=pl...  2.07 us
    pallas_call x1, Pallas kernels, attend_own(): pl.pallas_call(attend_own_kernel, in_specs=[vmem] * 6 + [pl.BlockSpec(mem...  1.83 us
    pallas_call x1, Pallas kernels, attend_early(): pl.pallas_call(attend_early_kernel, in_specs=[vmem] * 3, out_specs=[vmem]...  1.63 us
  transfers between devices with their start and end apart: 12, of which 6 were waited for; matrix products, arithmetic and copies ran while one was open for 0% of the time, Pallas kernels for 14%

profile of v6, /device:TPU:2, one launch (start us, length us, event | category | flops | bytes accessed | tf_op | source)
XLA Modules:
  0.0 45.6 jit_solution(7363418644746020357)
XLA Ops:
  0.0 2.0 %collective-permute-start = (bf16[64,1152]{1,0:T(8,128)(2,1)}, bf16[64,1152]{1,0:T(8,128)(2,1)S(1)}, u32[]{:S(2)}, u32[]{:S(2)}) collective-permute-start(bf16[64,1152]{1,0:T(8,128)(2,1)} %bitcast.21), channel_id=1, source_target_pairs={{0,16},{8,24},{16,0},{24,8},{32,48},{40,56},{48,32},{56,40},{64,80... | collective-permute-start | bytes 442376 | tf_op jit(solution)/shard_map/ppermute | solution.py:42
  2.1 3.6 %collective-permute-start.5 = (bf16[64,1152]{1,0:T(8,128)(2,1)S(1)}, bf16[64,1152]{1,0:T(8,128)(2,1)S(1)}, u32[]{:S(2)}, u32[]{:S(2)}) collective-permute-start(bf16[64,1152]{1,0:T(8,128)(2,1)S(1)} %bitcast.22), channel_id=1, source_target_pairs={{0,48},{8,56},{16,32},{24,40},{32,16},{40,24},{48,0},{56,8},{64,11... | collective-permute-start | bytes 442376 | tf_op jit(solution)/shard_map/ppermute | solution.py:42
  5.7 1.5 %fresh_qkv.1.fresh_ref = bf16[64,3456]{1,0:T(8,128)(2,1)S(1)} custom-call(bf16[64,1152]{1,0:T(8,128)(2,1)S(1)} %bitcast.15, f32[5,1,1152]{2,1,0:T(1,128)S(1)} %bitcast.17, bf16[1152,3456]{1,0:T(8,128)(2,1)S(1)} %bitcast.14), custom_call_target="tpu_custom_call" | custom-call | flops 509607936 | bytes 7962624 | tf_op jit(solution)/shard_map/fresh_qkv/pallas_call | solution.py:90
  7.3 3.3 %collective-permute-start.3 = (bf16[64,1152]{1,0:T(8,128)(2,1)S(1)}, bf16[64,1152]{1,0:T(8,128)(2,1)S(1)}, u32[]{:S(2)}, u32[]{:S(2)}) collective-permute-start(bf16[64,1152]{1,0:T(8,128)(2,1)S(1)} %slice.20.q_ref), channel_id=1, source_target_pairs={{0,128},{8,136},{16,144},{24,152},{32,160},{40,168},{48,176},{56,1... | collective-permute-start | bytes 442376 | tf_op jit(solution)/shard_map/ppermute | solution.py:42
  10.6 1.1 %collective-permute-start.2 = (bf16[64,1152]{1,0:T(8,128)(2,1)S(1)}, bf16[64,1152]{1,0:T(8,128)(2,1)S(1)}, u32[]{:S(2)}, u32[]{:S(2)}) collective-permute-start(bf16[64,1152]{1,0:T(8,128)(2,1)S(1)} %slice.20.q_ref), channel_id=1, source_target_pairs={{0,192},{8,200},{16,208},{24,216},{32,224},{40,232},{48,240},{56,2... | collective-permute-start | bytes 442376 | tf_op jit(solution)/shard_map/ppermute | solution.py:42
  11.6 1.0 %collective-permute-start.1 = (bf16[64,1152]{1,0:T(8,128)(2,1)S(1)}, bf16[64,1152]{1,0:T(8,128)(2,1)S(1)}, u32[]{:S(2)}, u32[]{:S(2)}) collective-permute-start(bf16[64,1152]{1,0:T(8,128)(2,1)S(1)} %slice.20.q_ref), channel_id=1, source_target_pairs={{0,64},{8,72},{16,80},{24,88},{32,96},{40,104},{48,112},{56,120},{... | collective-permute-start | bytes 442376 | tf_op jit(solution)/shard_map/ppermute | solution.py:42
  12.6 1.2 %stale_kv.2.kv0 = bf16[128,2304]{1,0:T(8,128)(2,1)S(1)} custom-call(bf16[64,1152]{1,0:T(8,128)(2,1)S(1)} %bitcast.24, bf16[64,1152]{1,0:T(8,128)(2,1)S(1)} %collective-permute-done.refs_1_, bf16[1152,3456]{1,0:T(8,128)(2,1)S(1)} %bitcast.14), custom_call_target="tpu_custom_call" | custom-call | flops 20000000000 | bytes 1 | tf_op jit(solution)/shard_map/stale_kv/pallas_call | solution.py:118
  13.8 0.0 collective-permute-done.5.refs_4_
  13.8 0.1 collective-permute-start.6
  13.9 4.6 %collective-permute-done.4.refs_3_ = bf16[64,1152]{1,0:T(8,128)(2,1)S(1)} collective-permute-done((bf16[64,1152]{1,0:T(8,128)(2,1)S(1)}, bf16[64,1152]{1,0:T(8,128)(2,1)S(1)}, u32[]{:S(2)}, u32[]{:S(2)}) %collective-permute-start.4) | collective-permute-done | bytes 147488 | tf_op jit(solution)/shard_map/ppermute | solution.py:42
  18.5 0.0 collective-permute-done.3.refs_2_
  18.5 0.1 gather_blocks.1
  18.6 0.0 copy-start.4
  18.6 0.0 copy-start.5
  18.6 0.0 copy-start
  18.6 0.0 copy-start.3
  18.6 1.2 %stale_kv.3.kv1.kv0 = bf16[128,2304]{1,0:T(8,128)(2,1)S(1)} custom-call(bf16[128,1152]{1,0:T(8,128)(2,1)S(1)} %get-tuple-element.20.refs_0_, bf16[1152,3456]{1,0:T(8,128)(2,1)S(1)} %bitcast.14), custom_call_target="tpu_custom_call" | custom-call | flops 1 | bytes 1 | tf_op jit(solution)/shard_map/stale_kv/pallas_call | solution.py:118
  19.8 0.3 collective-permute-start.7
  20.1 1.6 %attend_early.1 = (f32[192,1152]{1,0:T(8,128)S(1)}, f32[192,128]{1,0:T(8,128)S(1)}) custom-call(bf16[192,1152]{1,0:T(8,128)(2,1)S(1)} %get-tuple-element.23.q_ref, bf16[128,2304]{1,0:T(8,128)(2,1)S(1)} %stale_kv.2.kv0, bf16[128,2304]{1,0:T(8,128)(2,1)S(1)} %collective-permute-done.6.kv2.kv1), custom_call_target="tpu_custom_call" | custom-call | flops 1 | bytes 1 | tf_op jit(solution)/shard_map/attend_early/pallas_call | solution.py:279
  21.7 0.3 collective-permute-done.7.kv3.kv1
  22.1 2.1 %attend_late.1 = bf16[192,1280]{1,0:T(8,128)(2,1)S(1)} custom-call(bf16[192,1152]{1,0:T(8,128)(2,1)S(1)} %get-tuple-element.23.q_ref, bf16[128,2304]{1,0:T(8,128)(2,1)S(1)} %stale_kv.3.kv1.kv0, bf16[128,2304]{1,0:T(8,128)(2,1)S(1)} %collective-permute-done.7.kv3.kv1, f32[192,1152]{1,0:T(8,128)S(1)} %get-tuple-element.24.early_ref, ...), custom_call_target="tpu_custom_call" | custom-call | flops 1 | bytes 1 | tf_op jit(solution)/shard_map/attend_late/pallas_call | solution.py:295
  24.2 3.3 %collective-permute-start.10 = (bf16[64,1280]{1,0:T(8,128)(2,1)S(1)}, bf16[64,1280]{1,0:T(8,128)(2,1)S(1)}, u32[]{:S(2)}, u32[]{:S(2)}) collective-permute-start(bf16[64,1280]{1,0:T(8,128)(2,1)S(1)} %get-tuple-element.31), channel_id=1, source_target_pairs={{0,128},{8,136},{16,144},{24,152},{32,160},{40,168},{48,176},{56,1... | collective-permute-start | bytes 491528 | tf_op jit(solution)/shard_map/ppermute | solution.py:42
  27.5 0.7 %collective-permute-start.9 = (bf16[64,1280]{1,0:T(8,128)(2,1)S(1)}, bf16[64,1280]{1,0:T(8,128)(2,1)S(1)}, u32[]{:S(2)}, u32[]{:S(2)}) collective-permute-start(bf16[64,1280]{1,0:T(8,128)(2,1)S(1)} %get-tuple-element.32), channel_id=1, source_target_pairs={{0,64},{8,72},{16,80},{24,88},{32,96},{40,104},{48,112},{56,120},{... | collective-permute-start | bytes 491528 | tf_op jit(solution)/shard_map/ppermute | solution.py:42
  28.2 2.6 %collective-permute-start.8 = (bf16[64,1280]{1,0:T(8,128)(2,1)S(1)}, bf16[64,1280]{1,0:T(8,128)(2,1)S(1)}, u32[]{:S(2)}, u32[]{:S(2)}) collective-permute-start(bf16[64,1280]{1,0:T(8,128)(2,1)S(1)} %get-tuple-element.33), channel_id=1, source_target_pairs={{0,192},{8,200},{16,208},{24,216},{32,224},{40,232},{48,240},{56,2... | collective-permute-start | bytes 491528 | tf_op jit(solution)/shard_map/ppermute | solution.py:42
  30.7 1.8 %attend_own.1 = (bf16[64,1280]{1,0:T(8,128)(2,1)S(1)}, f32[8,128]{1,0:T(8,128)S(1)}, f32[2,8,128]{2,1,0:T(8,128)S(1)}) custom-call(bf16[64,1152]{1,0:T(8,128)(2,1)S(1)} %slice.20.q_ref, bf16[128,2304]{1,0:T(8,128)(2,1)S(1)} %stale_kv.2.kv0, bf16[128,2304]{1,0:T(8,128)(2,1)S(1)} %stale_kv.3.kv1.kv0, bf16[128,2304]{1,0:T(8,128)(2,1)S(1)} %collective-permute-done.6.kv2.kv1, ...), custom_call_target="tpu_custom_call" | custom-call | flops 536870912 | bytes 2359296 | tf_op jit(solution)/shard_map/attend_own/pallas_call | solution.py:325
  32.6 0.3 collective-permute-done.10.p3
  32.8 2.7 %collective-permute-done.9.p2 = bf16[64,1280]{1,0:T(8,128)(2,1)S(1)} collective-permute-done((bf16[64,1280]{1,0:T(8,128)(2,1)S(1)}, bf16[64,1280]{1,0:T(8,128)(2,1)S(1)}, u32[]{:S(2)}, u32[]{:S(2)}) %collective-permute-start.9) | collective-permute-done | bytes 163872 | tf_op jit(solution)/shard_map/ppermute | solution.py:42
  35.6 0.4 collective-permute-done.8.p1
  35.9 1.5 %post.1 = (f32[8,128]{1,0:T(8,128)S(1)}, f32[8,128]{1,0:T(8,128)S(1)}) custom-call(bf16[64,1280]{1,0:T(8,128)(2,1)S(1)} %get-tuple-element.22.p0, bf16[64,1280]{1,0:T(8,128)(2,1)S(1)} %collective-permute-done.8.p1, bf16[64,1280]{1,0:T(8,128)(2,1)S(1)} %collective-permute-done.9.p2, bf16[64,1280]{1,0:T(8,128)(2,1)S(1)} %collective-permute-done.10.p3, ...), custom_call_target="tpu_custom_call" | custom-call | flops 169869312 | bytes 2654208 | tf_op jit(solution)/shard_map/post/pallas_call | solution.py:374
  37.4 5.4 %collective-permute-start.11 = (f32[8,128]{1,0:T(8,128)S(1)}, f32[8,128]{1,0:T(8,128)S(1)}, u32[]{:S(2)}, u32[]{:S(2)}) collective-permute-start(f32[8,128]{1,0:T(8,128)S(1)} %get-tuple-element.30), channel_id=1, source_target_pairs={{0,1},{1,0},{2,3},{3,2},{4,5},{5,4},{6,7},{7,6},{8,9},{9,8},{10,11... | collective-permute-start | bytes 12296 | tf_op jit(solution)/shard_map/ppermute | solution.py:415
  42.8 2.2 %collective-permute-done.11 = f32[8,128]{1,0:T(8,128)S(1)} collective-permute-done((f32[8,128]{1,0:T(8,128)S(1)}, f32[8,128]{1,0:T(8,128)S(1)}, u32[]{:S(2)}, u32[]{:S(2)}) %collective-permute-start.11) | collective-permute-done | bytes 4128 | tf_op jit(solution)/shard_map/ppermute | solution.py:415
  45.0 0.6 %fusion.1 = f32[1,8,128]{2,1,0:T(8,128)} fusion(f32[8,128]{1,0:T(8,128)S(1)} %get-tuple-element.29, f32[8,128]{1,0:T(8,128)S(1)} %collective-permute-done.11, f32[2,8,128]{2,1,0:T(8,128)S(1)} %get-tuple-element.28.gain_ref), kind=kLoop, calls=%fused_computation.2 | loop fusion | flops 2048 | bytes 16384 | tf_op jit(solution)/shard_map/broadcast_in_dim | solution.py:418
  (23 shorter events, 0.1 us)
Async XLA Ops:
  0.0 5.7 %slice-start = ((s8[7962624]{0:T(1024)(128)(4,1)}), s8[4194304]{0:T(1024)(128)(4,1)S(1)}, s32[]{:S(2)}) async-start(s8[7962624]{0:T(1024)(128)(4,1)} %bitcast.13), calls=%async_computation | async-start | bytes 8388608
  0.0 2.1 %copy-start.6 = (bf16[1,64,1152]{2,1,0:T(8,128)(2,1)S(1)}, bf16[1,64,1152]{2,1,0:T(8,128)(2,1)}, u32[]{:S(2)}) copy-start(bf16[1,64,1152]{2,1,0:T(8,128)(2,1)} %param.9) | copy-start | bytes 442372
  0.0 5.7 %slice-start.1 = ((s8[7962624]{0:T(1024)(128)(4,1)}), s8[3768320]{0:T(1024)(128)(4,1)S(1)}, s32[]{:S(2)}) async-start(s8[7962624]{0:T(1024)(128)(4,1)} %bitcast.13), calls=%async_computation.1 | async-start | bytes 7536640
  0.0 5.7 %copy-start.1 = (bf16[1,64,1152]{2,1,0:T(8,128)(2,1)S(1)}, bf16[1,64,1152]{2,1,0:T(8,128)(2,1)}, u32[]{:S(2)}) copy-start(bf16[1,64,1152]{2,1,0:T(8,128)(2,1)} %param.8) | copy-start | bytes 442372
  0.0 5.7 %copy-start.2 = (f32[1,5,1152]{2,0,1:T(1,128)S(1)}, f32[1,5,1152]{2,0,1:T(1,128)}, u32[]{:S(2)}) copy-start(f32[1,5,1152]{2,0,1:T(1,128)} %param.10) | copy-start | bytes 69124
  0.0 11.6 %collective-permute-start = (bf16[64,1152]{1,0:T(8,128)(2,1)}, bf16[64,1152]{1,0:T(8,128)(2,1)S(1)}, u32[]{:S(2)}, u32[]{:S(2)}) collective-permute-start(bf16[64,1152]{1,0:T(8,128)(2,1)} %bitcast.21), channel_id=1, source_target_pairs={{0,16},{8,24},{16,0},{24,8},{32,48},{40,56},{48,32},{56,40},{64,80... | collective-permute-start | bytes 442376 | tf_op jit(solution)/shard_map/ppermute | solution.py:42
  2.1 11.7 %collective-permute-start.5 = (bf16[64,1152]{1,0:T(8,128)(2,1)S(1)}, bf16[64,1152]{1,0:T(8,128)(2,1)S(1)}, u32[]{:S(2)}, u32[]{:S(2)}) collective-permute-start(bf16[64,1152]{1,0:T(8,128)(2,1)S(1)} %bitcast.22), channel_id=1, source_target_pairs={{0,48},{8,56},{16,32},{24,40},{32,16},{40,24},{48,0},{56,8},{64,11... | collective-permute-start | bytes 442376 | tf_op jit(solution)/shard_map/ppermute | solution.py:42
  5.7 12.8 %collective-permute-start.4 = (bf16[64,1152]{1,0:T(8,128)(2,1)S(1)}, bf16[64,1152]{1,0:T(8,128)(2,1)S(1)}, u32[]{:S(2)}, u32[]{:S(2)}) collective-permute-start(bf16[64,1152]{1,0:T(8,128)(2,1)S(1)} %bitcast.23), channel_id=1, source_target_pairs={{0,32},{8,40},{16,48},{24,56},{32,0},{40,8},{48,16},{56,24},{64,96... | collective-permute-start | bytes 442376 | tf_op jit(solution)/shard_map/ppermute | solution.py:42
  7.3 11.2 %collective-permute-start.3 = (bf16[64,1152]{1,0:T(8,128)(2,1)S(1)}, bf16[64,1152]{1,0:T(8,128)(2,1)S(1)}, u32[]{:S(2)}, u32[]{:S(2)}) collective-permute-start(bf16[64,1152]{1,0:T(8,128)(2,1)S(1)} %slice.20.q_ref), channel_id=1, source_target_pairs={{0,128},{8,136},{16,144},{24,152},{32,160},{40,168},{48,176},{56,1... | collective-permute-start | bytes 442376 | tf_op jit(solution)/shard_map/ppermute | solution.py:42
  10.6 7.9 %collective-permute-start.2 = (bf16[64,1152]{1,0:T(8,128)(2,1)S(1)}, bf16[64,1152]{1,0:T(8,128)(2,1)S(1)}, u32[]{:S(2)}, u32[]{:S(2)}) collective-permute-start(bf16[64,1152]{1,0:T(8,128)(2,1)S(1)} %slice.20.q_ref), channel_id=1, source_target_pairs={{0,192},{8,200},{16,208},{24,216},{32,224},{40,232},{48,240},{56,2... | collective-permute-start | bytes 442376 | tf_op jit(solution)/shard_map/ppermute | solution.py:42
  11.6 6.9 %collective-permute-start.1 = (bf16[64,1152]{1,0:T(8,128)(2,1)S(1)}, bf16[64,1152]{1,0:T(8,128)(2,1)S(1)}, u32[]{:S(2)}, u32[]{:S(2)}) collective-permute-start(bf16[64,1152]{1,0:T(8,128)(2,1)S(1)} %slice.20.q_ref), channel_id=1, source_target_pairs={{0,64},{8,72},{16,80},{24,88},{32,96},{40,104},{48,112},{56,120},{... | collective-permute-start | bytes 442376 | tf_op jit(solution)/shard_map/ppermute | solution.py:42
  13.8 4.8 %collective-permute-start.6 = (bf16[128,2304]{1,0:T(8,128)(2,1)S(1)}, bf16[128,2304]{1,0:T(8,128)(2,1)S(1)}, u32[]{:S(2)}, u32[]{:S(2)}) collective-permute-start(bf16[128,2304]{1,0:T(8,128)(2,1)S(1)} %stale_kv.2.kv0), channel_id=1, source_target_pairs={{0,8},{8,0},{16,24},{24,16},{32,40},{40,32},{48,56},{56,48},{64,72... | collective-permute-start | bytes 1769480 | tf_op jit(solution)/shard_map/ppermute | solution.py:42
  18.6 12.2 %copy-start.4 = (f32[1,8,128]{2,1,0:T(8,128)S(1)}, f32[1,8,128]{2,1,0:T(8,128)}, u32[]{:S(2)}) copy-start(f32[1,8,128]{2,1,0:T(8,128)} %param.11) | copy-start | bytes 12292
  18.6 12.1 %copy-start.5 = (s32[4]{0:T(128)S(1)}, s32[4]{0:T(128)}, u32[]{:S(2)}) copy-start(s32[4]{0:T(128)} %time_ref.1) | copy-start | bytes 52
  18.6 17.3 %copy-start = (bf16[1152,1152]{1,0:T(8,128)(2,1)S(1)}, bf16[1152,1152]{1,0:T(8,128)(2,1)}, u32[]{:S(2)}) copy-start(bf16[1152,1152]{1,0:T(8,128)(2,1)} %w_out_ref.1) | copy-start | bytes 7962628
  18.6 17.3 %copy-start.3 = (bf16[1152,16]{0,1:T(8,128)(2,1)S(1)}, bf16[1152,16]{0,1:T(8,128)(2,1)}, u32[]{:S(2)}) copy-start(bf16[1152,16]{0,1:T(8,128)(2,1)} %param.15) | copy-start | bytes 110596
  19.8 2.3 %collective-permute-start.7 = (bf16[128,2304]{1,0:T(8,128)(2,1)S(1)}, bf16[128,2304]{1,0:T(8,128)(2,1)S(1)}, u32[]{:S(2)}, u32[]{:S(2)}) collective-permute-start(bf16[128,2304]{1,0:T(8,128)(2,1)S(1)} %stale_kv.3.kv1.kv0), channel_id=1, source_target_pairs={{0,8},{8,0},{16,24},{24,16},{32,40},{40,32},{48,56},{56,48},{64,72... | collective-permute-start | bytes 1769480 | tf_op jit(solution)/shard_map/ppermute | solution.py:42
  24.2 8.6 %collective-permute-start.10 = (bf16[64,1280]{1,0:T(8,128)(2,1)S(1)}, bf16[64,1280]{1,0:T(8,128)(2,1)S(1)}, u32[]{:S(2)}, u32[]{:S(2)}) collective-permute-start(bf16[64,1280]{1,0:T(8,128)(2,1)S(1)} %get-tuple-element.31), channel_id=1, source_target_pairs={{0,128},{8,136},{16,144},{24,152},{32,160},{40,168},{48,176},{56,1... | collective-permute-start | bytes 491528 | tf_op jit(solution)/shard_map/ppermute | solution.py:42
  27.5 8.1 %collective-permute-start.9 = (bf16[64,1280]{1,0:T(8,128)(2,1)S(1)}, bf16[64,1280]{1,0:T(8,128)(2,1)S(1)}, u32[]{:S(2)}, u32[]{:S(2)}) collective-permute-start(bf16[64,1280]{1,0:T(8,128)(2,1)S(1)} %get-tuple-element.32), channel_id=1, source_target_pairs={{0,64},{8,72},{16,80},{24,88},{32,96},{40,104},{48,112},{56,120},{... | collective-permute-start | bytes 491528 | tf_op jit(solution)/shard_map/ppermute | solution.py:42
  28.2 7.7 %collective-permute-start.8 = (bf16[64,1280]{1,0:T(8,128)(2,1)S(1)}, bf16[64,1280]{1,0:T(8,128)(2,1)S(1)}, u32[]{:S(2)}, u32[]{:S(2)}) collective-permute-start(bf16[64,1280]{1,0:T(8,128)(2,1)S(1)} %get-tuple-element.33), channel_id=1, source_target_pairs={{0,192},{8,200},{16,208},{24,216},{32,224},{40,232},{48,240},{56,2... | collective-permute-start | bytes 491528 | tf_op jit(solution)/shard_map/ppermute | solution.py:42
  37.4 7.6 %collective-permute-start.11 = (f32[8,128]{1,0:T(8,128)S(1)}, f32[8,128]{1,0:T(8,128)S(1)}, u32[]{:S(2)}, u32[]{:S(2)}) collective-permute-start(f32[8,128]{1,0:T(8,128)S(1)} %get-tuple-element.30), channel_id=1, source_target_pairs={{0,1},{1,0},{2,3},{3,2},{4,5},{5,4},{6,7},{7,6},{8,9},{9,8},{10,11... | collective-permute-start | bytes 12296 | tf_op jit(solution)/shard_map/ppermute | solution.py:415

commit v7 on v6

--- a/solution.py
+++ b/solution.py
@@ -257,7 +257,9 @@
     total = weights[0] + weights[1]
     weights = [split_stats(w / total, lane).astype(BF16) for w in weights]
     pick = pick_ref[...]
-    weights = [jnp.dot(w, pick, preferred_element_type=F32) for w in weights]
+    rows = lane.shape[0]
+    weights = jnp.dot(jnp.concatenate(weights, axis=0), pick, preferred_element_type=F32)
+    weights = weights[:rows], weights[rows:]
     mixed = []
     for block, values in enumerate(blocks):
         cols = slice(128 * block, 128 * block + 128)
@@ -343,7 +345,10 @@
 ):
     pick = pick_ref[...]
     parts = (p0, p1, p2, p3)
-    sums = [jnp.dot(p[:, WIDTH:], pick, preferred_element_type=F32) for p in parts]
+    rows = p0.shape[0]
+    sums = jnp.concatenate([p[:, WIDTH:] for p in parts], axis=0)
+    sums = jnp.dot(sums, pick, preferred_element_type=F32)
+    sums = [sums[n * rows : (n + 1) * rows] for n in range(len(parts))]
     top = functools.reduce(jnp.maximum, sums)
     weights = [jnp.exp(s - top) for s in sums]
     total = functools.reduce(jnp.add, weights)
@@ -360,7 +365,6 @@
     wide = lax.dot_general(
         final_in, w_wide, (((1,), (1,)), ((), ())), preferred_element_type=F32
     )
-    rows = wide.shape[0]
     token = lax.broadcasted_iota(jnp.int32, wide.shape, 0) % 8
     place = lax.broadcasted_iota(jnp.int32, wide.shape, 1) // 16
     wide = jnp.where(token == place, wide, 0.0)

time: 45.7 us -> 45.6 us (level)
  no operation moved by 1% of the time
where the time goes in v7:
time: 45.6 us; the launch traced here: 45.5 us
  starting transfers between devices  23.2 us (51%)
  Pallas kernels  10.9 us (24%)
  waiting for transfers between devices  10.6 us (23%)
  other arithmetic  0.6 us (1%)
    ppermute x11, starting transfers between devices, send(): return lax.ppermute(value, 'patch', pairs)  17.8 us
    ppermute x11, waiting for transfers between devices, send(): return lax.ppermute(value, 'patch', pairs)  8.33 us
    ppermute x1, starting transfers between devices, body(): lax.ppermute(noise, 'guide', [(i, i ^ 1) for i in range(lax.axis_size('gu...  5.36 us
    pallas_call x2, Pallas kernels, project_stale(): pl.pallas_call(stale_kernel, in_specs=[pl.BlockSpec(memory_space=pltpu.VM...  2.32 us
    ppermute x1, waiting for transfers between devices, body(): lax.ppermute(noise, 'guide', [(i, i ^ 1) for i in range(lax.axis_size('gu...  2.25 us
    pallas_call x1, Pallas kernels, attend_late(): pl.pallas_call(attend_late_kernel, in_specs=[pl.BlockSpec(memory_space=pl...  2.08 us
    pallas_call x1, Pallas kernels, attend_own(): pl.pallas_call(attend_own_kernel, in_specs=[vmem] * 6 + [pl.BlockSpec(mem...  1.83 us
    pallas_call x1, Pallas kernels, attend_early(): pl.pallas_call(attend_early_kernel, in_specs=[vmem] * 3, out_specs=[vmem]...  1.63 us
  transfers between devices with their start and end apart: 12, of which 6 were waited for; matrix products, arithmetic and copies ran while one was open for 0% of the time, Pallas kernels for 14%

profile of v7, /device:TPU:2, one launch (start us, length us, event | category | flops | bytes accessed | tf_op | source)
XLA Modules:
  0.0 45.5 jit_solution(12516042045089022904)
XLA Ops:
  0.0 2.0 %collective-permute-start = (bf16[64,1152]{1,0:T(8,128)(2,1)}, bf16[64,1152]{1,0:T(8,128)(2,1)S(1)}, u32[]{:S(2)}, u32[]{:S(2)}) collective-permute-start(bf16[64,1152]{1,0:T(8,128)(2,1)} %bitcast.21), channel_id=1, source_target_pairs={{0,16},{8,24},{16,0},{24,8},{32,48},{40,56},{48,32},{56,40},{64,80... | collective-permute-start | bytes 442376 | tf_op jit(solution)/shard_map/ppermute | solution.py:42
  2.1 3.6 %collective-permute-start.5 = (bf16[64,1152]{1,0:T(8,128)(2,1)S(1)}, bf16[64,1152]{1,0:T(8,128)(2,1)S(1)}, u32[]{:S(2)}, u32[]{:S(2)}) collective-permute-start(bf16[64,1152]{1,0:T(8,128)(2,1)S(1)} %bitcast.22), channel_id=1, source_target_pairs={{0,48},{8,56},{16,32},{24,40},{32,16},{40,24},{48,0},{56,8},{64,11... | collective-permute-start | bytes 442376 | tf_op jit(solution)/shard_map/ppermute | solution.py:42
  5.7 0.0 collective-permute-start.4
  5.7 1.5 %fresh_qkv.1.fresh_ref = bf16[64,3456]{1,0:T(8,128)(2,1)S(1)} custom-call(bf16[64,1152]{1,0:T(8,128)(2,1)S(1)} %bitcast.15, f32[5,1,1152]{2,1,0:T(1,128)S(1)} %bitcast.17, bf16[1152,3456]{1,0:T(8,128)(2,1)S(1)} %bitcast.14), custom_call_target="tpu_custom_call" | custom-call | flops 509607936 | bytes 7962624 | tf_op jit(solution)/shard_map/fresh_qkv/pallas_call | solution.py:90
  7.3 3.3 %collective-permute-start.3 = (bf16[64,1152]{1,0:T(8,128)(2,1)S(1)}, bf16[64,1152]{1,0:T(8,128)(2,1)S(1)}, u32[]{:S(2)}, u32[]{:S(2)}) collective-permute-start(bf16[64,1152]{1,0:T(8,128)(2,1)S(1)} %slice.20.q_ref), channel_id=1, source_target_pairs={{0,128},{8,136},{16,144},{24,152},{32,160},{40,168},{48,176},{56,1... | collective-permute-start | bytes 442376 | tf_op jit(solution)/shard_map/ppermute | solution.py:42
  10.6 1.1 %collective-permute-start.2 = (bf16[64,1152]{1,0:T(8,128)(2,1)S(1)}, bf16[64,1152]{1,0:T(8,128)(2,1)S(1)}, u32[]{:S(2)}, u32[]{:S(2)}) collective-permute-start(bf16[64,1152]{1,0:T(8,128)(2,1)S(1)} %slice.20.q_ref), channel_id=1, source_target_pairs={{0,192},{8,200},{16,208},{24,216},{32,224},{40,232},{48,240},{56,2... | collective-permute-start | bytes 442376 | tf_op jit(solution)/shard_map/ppermute | solution.py:42
  11.6 0.0 collective-permute-done.refs_1_
  11.6 1.0 %collective-permute-start.1 = (bf16[64,1152]{1,0:T(8,128)(2,1)S(1)}, bf16[64,1152]{1,0:T(8,128)(2,1)S(1)}, u32[]{:S(2)}, u32[]{:S(2)}) collective-permute-start(bf16[64,1152]{1,0:T(8,128)(2,1)S(1)} %slice.20.q_ref), channel_id=1, source_target_pairs={{0,64},{8,72},{16,80},{24,88},{32,96},{40,104},{48,112},{56,120},{... | collective-permute-start | bytes 442376 | tf_op jit(solution)/shard_map/ppermute | solution.py:42
  12.6 1.2 %stale_kv.2.kv0 = bf16[128,2304]{1,0:T(8,128)(2,1)S(1)} custom-call(bf16[64,1152]{1,0:T(8,128)(2,1)S(1)} %bitcast.24, bf16[64,1152]{1,0:T(8,128)(2,1)S(1)} %collective-permute-done.refs_1_, bf16[1152,3456]{1,0:T(8,128)(2,1)S(1)} %bitcast.14), custom_call_target="tpu_custom_call" | custom-call | flops 20000000000 | bytes 1 | tf_op jit(solution)/shard_map/stale_kv/pallas_call | solution.py:118
  13.8 0.1 collective-permute-start.6
  13.9 4.6 %collective-permute-done.4.refs_3_ = bf16[64,1152]{1,0:T(8,128)(2,1)S(1)} collective-permute-done((bf16[64,1152]{1,0:T(8,128)(2,1)S(1)}, bf16[64,1152]{1,0:T(8,128)(2,1)S(1)}, u32[]{:S(2)}, u32[]{:S(2)}) %collective-permute-start.4) | collective-permute-done | bytes 147488 | tf_op jit(solution)/shard_map/ppermute | solution.py:42
  18.5 0.1 gather_blocks.1
  18.6 0.0 copy-start.4
  18.6 0.0 copy-start.5
  18.6 0.0 copy-start
  18.6 0.0 copy-start.3
  18.6 1.2 %stale_kv.3.kv1.kv0 = bf16[128,2304]{1,0:T(8,128)(2,1)S(1)} custom-call(bf16[128,1152]{1,0:T(8,128)(2,1)S(1)} %get-tuple-element.20.refs_0_, bf16[1152,3456]{1,0:T(8,128)(2,1)S(1)} %bitcast.14), custom_call_target="tpu_custom_call" | custom-call | flops 1 | bytes 1 | tf_op jit(solution)/shard_map/stale_kv/pallas_call | solution.py:118
  19.8 0.3 collective-permute-start.7
  20.1 1.6 %attend_early.1 = (f32[192,1152]{1,0:T(8,128)S(1)}, f32[192,128]{1,0:T(8,128)S(1)}) custom-call(bf16[192,1152]{1,0:T(8,128)(2,1)S(1)} %get-tuple-element.23.q_ref, bf16[128,2304]{1,0:T(8,128)(2,1)S(1)} %stale_kv.2.kv0, bf16[128,2304]{1,0:T(8,128)(2,1)S(1)} %collective-permute-done.6.kv2.kv1), custom_call_target="tpu_custom_call" | custom-call | flops 1 | bytes 1 | tf_op jit(solution)/shard_map/attend_early/pallas_call | solution.py:281
  21.7 0.3 collective-permute-done.7.kv3.kv1
  22.1 2.1 %attend_late.1 = bf16[192,1280]{1,0:T(8,128)(2,1)S(1)} custom-call(bf16[192,1152]{1,0:T(8,128)(2,1)S(1)} %get-tuple-element.23.q_ref, bf16[128,2304]{1,0:T(8,128)(2,1)S(1)} %stale_kv.3.kv1.kv0, bf16[128,2304]{1,0:T(8,128)(2,1)S(1)} %collective-permute-done.7.kv3.kv1, f32[192,1152]{1,0:T(8,128)S(1)} %get-tuple-element.24.early_ref, ...), custom_call_target="tpu_custom_call" | custom-call | flops 1 | bytes 1 | tf_op jit(solution)/shard_map/attend_late/pallas_call | solution.py:297
  24.2 3.3 %collective-permute-start.10 = (bf16[64,1280]{1,0:T(8,128)(2,1)S(1)}, bf16[64,1280]{1,0:T(8,128)(2,1)S(1)}, u32[]{:S(2)}, u32[]{:S(2)}) collective-permute-start(bf16[64,1280]{1,0:T(8,128)(2,1)S(1)} %get-tuple-element.31), channel_id=1, source_target_pairs={{0,128},{8,136},{16,144},{24,152},{32,160},{40,168},{48,176},{56,1... | collective-permute-start | bytes 491528 | tf_op jit(solution)/shard_map/ppermute | solution.py:42
  27.5 0.7 %collective-permute-start.9 = (bf16[64,1280]{1,0:T(8,128)(2,1)S(1)}, bf16[64,1280]{1,0:T(8,128)(2,1)S(1)}, u32[]{:S(2)}, u32[]{:S(2)}) collective-permute-start(bf16[64,1280]{1,0:T(8,128)(2,1)S(1)} %get-tuple-element.32), channel_id=1, source_target_pairs={{0,64},{8,72},{16,80},{24,88},{32,96},{40,104},{48,112},{56,120},{... | collective-permute-start | bytes 491528 | tf_op jit(solution)/shard_map/ppermute | solution.py:42
  28.2 2.6 %collective-permute-start.8 = (bf16[64,1280]{1,0:T(8,128)(2,1)S(1)}, bf16[64,1280]{1,0:T(8,128)(2,1)S(1)}, u32[]{:S(2)}, u32[]{:S(2)}) collective-permute-start(bf16[64,1280]{1,0:T(8,128)(2,1)S(1)} %get-tuple-element.33), channel_id=1, source_target_pairs={{0,192},{8,200},{16,208},{24,216},{32,224},{40,232},{48,240},{56,2... | collective-permute-start | bytes 491528 | tf_op jit(solution)/shard_map/ppermute | solution.py:42
  30.7 1.8 %attend_own.1 = (bf16[64,1280]{1,0:T(8,128)(2,1)S(1)}, f32[8,128]{1,0:T(8,128)S(1)}, f32[2,8,128]{2,1,0:T(8,128)S(1)}) custom-call(bf16[64,1152]{1,0:T(8,128)(2,1)S(1)} %slice.20.q_ref, bf16[128,2304]{1,0:T(8,128)(2,1)S(1)} %stale_kv.2.kv0, bf16[128,2304]{1,0:T(8,128)(2,1)S(1)} %stale_kv.3.kv1.kv0, bf16[128,2304]{1,0:T(8,128)(2,1)S(1)} %collective-permute-done.6.kv2.kv1, ...), custom_call_target="tpu_custom_call" | custom-call | flops 536870912 | bytes 2359296 | tf_op jit(solution)/shard_map/attend_own/pallas_call | solution.py:327
  32.6 0.3 collective-permute-done.10.p3
  32.8 2.7 %collective-permute-done.9.p2 = bf16[64,1280]{1,0:T(8,128)(2,1)S(1)} collective-permute-done((bf16[64,1280]{1,0:T(8,128)(2,1)S(1)}, bf16[64,1280]{1,0:T(8,128)(2,1)S(1)}, u32[]{:S(2)}, u32[]{:S(2)}) %collective-permute-start.9) | collective-permute-done | bytes 163872 | tf_op jit(solution)/shard_map/ppermute | solution.py:42
  35.6 0.4 collective-permute-done.8.p1
  35.9 1.4 %post.1 = (f32[8,128]{1,0:T(8,128)S(1)}, f32[8,128]{1,0:T(8,128)S(1)}) custom-call(bf16[64,1280]{1,0:T(8,128)(2,1)S(1)} %get-tuple-element.22.p0, bf16[64,1280]{1,0:T(8,128)(2,1)S(1)} %collective-permute-done.8.p1, bf16[64,1280]{1,0:T(8,128)(2,1)S(1)} %collective-permute-done.9.p2, bf16[64,1280]{1,0:T(8,128)(2,1)S(1)} %collective-permute-done.10.p3, ...), custom_call_target="tpu_custom_call" | custom-call | flops 169869312 | bytes 2654208 | tf_op jit(solution)/shard_map/post/pallas_call | solution.py:378
  37.3 5.4 %collective-permute-start.11 = (f32[8,128]{1,0:T(8,128)S(1)}, f32[8,128]{1,0:T(8,128)S(1)}, u32[]{:S(2)}, u32[]{:S(2)}) collective-permute-start(f32[8,128]{1,0:T(8,128)S(1)} %get-tuple-element.30), channel_id=1, source_target_pairs={{0,1},{1,0},{2,3},{3,2},{4,5},{5,4},{6,7},{7,6},{8,9},{9,8},{10,11... | collective-permute-start | bytes 12296 | tf_op jit(solution)/shard_map/ppermute | solution.py:419
  42.7 2.2 %collective-permute-done.11 = f32[8,128]{1,0:T(8,128)S(1)} collective-permute-done((f32[8,128]{1,0:T(8,128)S(1)}, f32[8,128]{1,0:T(8,128)S(1)}, u32[]{:S(2)}, u32[]{:S(2)}) %collective-permute-start.11) | collective-permute-done | bytes 4128 | tf_op jit(solution)/shard_map/ppermute | solution.py:419
  44.9 0.6 %fusion.1 = f32[1,8,128]{2,1,0:T(8,128)} fusion(f32[8,128]{1,0:T(8,128)S(1)} %get-tuple-element.29, f32[8,128]{1,0:T(8,128)S(1)} %collective-permute-done.11, f32[2,8,128]{2,1,0:T(8,128)S(1)} %get-tuple-element.28.gain_ref), kind=kLoop, calls=%fused_computation.2 | loop fusion | flops 2048 | bytes 16384 | tf_op jit(solution)/shard_map/broadcast_in_dim | solution.py:422
  (23 shorter events, 0.1 us)
Async XLA Ops:
  0.0 5.7 %slice-start = ((s8[7962624]{0:T(1024)(128)(4,1)}), s8[4194304]{0:T(1024)(128)(4,1)S(1)}, s32[]{:S(2)}) async-start(s8[7962624]{0:T(1024)(128)(4,1)} %bitcast.13), calls=%async_computation | async-start | bytes 8388608
  0.0 2.1 %copy-start.6 = (bf16[1,64,1152]{2,1,0:T(8,128)(2,1)S(1)}, bf16[1,64,1152]{2,1,0:T(8,128)(2,1)}, u32[]{:S(2)}) copy-start(bf16[1,64,1152]{2,1,0:T(8,128)(2,1)} %param.9) | copy-start | bytes 442372
  0.0 5.7 %slice-start.1 = ((s8[7962624]{0:T(1024)(128)(4,1)}), s8[3768320]{0:T(1024)(128)(4,1)S(1)}, s32[]{:S(2)}) async-start(s8[7962624]{0:T(1024)(128)(4,1)} %bitcast.13), calls=%async_computation.1 | async-start | bytes 7536640
  0.0 5.7 %copy-start.1 = (bf16[1,64,1152]{2,1,0:T(8,128)(2,1)S(1)}, bf16[1,64,1152]{2,1,0:T(8,128)(2,1)}, u32[]{:S(2)}) copy-start(bf16[1,64,1152]{2,1,0:T(8,128)(2,1)} %param.8) | copy-start | bytes 442372
  0.0 5.7 %copy-start.2 = (f32[1,5,1152]{2,0,1:T(1,128)S(1)}, f32[1,5,1152]{2,0,1:T(1,128)}, u32[]{:S(2)}) copy-start(f32[1,5,1152]{2,0,1:T(1,128)} %param.10) | copy-start | bytes 69124
  0.0 11.6 %collective-permute-start = (bf16[64,1152]{1,0:T(8,128)(2,1)}, bf16[64,1152]{1,0:T(8,128)(2,1)S(1)}, u32[]{:S(2)}, u32[]{:S(2)}) collective-permute-start(bf16[64,1152]{1,0:T(8,128)(2,1)} %bitcast.21), channel_id=1, source_target_pairs={{0,16},{8,24},{16,0},{24,8},{32,48},{40,56},{48,32},{56,40},{64,80... | collective-permute-start | bytes 442376 | tf_op jit(solution)/shard_map/ppermute | solution.py:42
  2.1 11.7 %collective-permute-start.5 = (bf16[64,1152]{1,0:T(8,128)(2,1)S(1)}, bf16[64,1152]{1,0:T(8,128)(2,1)S(1)}, u32[]{:S(2)}, u32[]{:S(2)}) collective-permute-start(bf16[64,1152]{1,0:T(8,128)(2,1)S(1)} %bitcast.22), channel_id=1, source_target_pairs={{0,48},{8,56},{16,32},{24,40},{32,16},{40,24},{48,0},{56,8},{64,11... | collective-permute-start | bytes 442376 | tf_op jit(solution)/shard_map/ppermute | solution.py:42
  5.7 12.8 %collective-permute-start.4 = (bf16[64,1152]{1,0:T(8,128)(2,1)S(1)}, bf16[64,1152]{1,0:T(8,128)(2,1)S(1)}, u32[]{:S(2)}, u32[]{:S(2)}) collective-permute-start(bf16[64,1152]{1,0:T(8,128)(2,1)S(1)} %bitcast.23), channel_id=1, source_target_pairs={{0,32},{8,40},{16,48},{24,56},{32,0},{40,8},{48,16},{56,24},{64,96... | collective-permute-start | bytes 442376 | tf_op jit(solution)/shard_map/ppermute | solution.py:42
  7.3 11.2 %collective-permute-start.3 = (bf16[64,1152]{1,0:T(8,128)(2,1)S(1)}, bf16[64,1152]{1,0:T(8,128)(2,1)S(1)}, u32[]{:S(2)}, u32[]{:S(2)}) collective-permute-start(bf16[64,1152]{1,0:T(8,128)(2,1)S(1)} %slice.20.q_ref), channel_id=1, source_target_pairs={{0,128},{8,136},{16,144},{24,152},{32,160},{40,168},{48,176},{56,1... | collective-permute-start | bytes 442376 | tf_op jit(solution)/shard_map/ppermute | solution.py:42
  10.6 7.9 %collective-permute-start.2 = (bf16[64,1152]{1,0:T(8,128)(2,1)S(1)}, bf16[64,1152]{1,0:T(8,128)(2,1)S(1)}, u32[]{:S(2)}, u32[]{:S(2)}) collective-permute-start(bf16[64,1152]{1,0:T(8,128)(2,1)S(1)} %slice.20.q_ref), channel_id=1, source_target_pairs={{0,192},{8,200},{16,208},{24,216},{32,224},{40,232},{48,240},{56,2... | collective-permute-start | bytes 442376 | tf_op jit(solution)/shard_map/ppermute | solution.py:42
  11.6 6.9 %collective-permute-start.1 = (bf16[64,1152]{1,0:T(8,128)(2,1)S(1)}, bf16[64,1152]{1,0:T(8,128)(2,1)S(1)}, u32[]{:S(2)}, u32[]{:S(2)}) collective-permute-start(bf16[64,1152]{1,0:T(8,128)(2,1)S(1)} %slice.20.q_ref), channel_id=1, source_target_pairs={{0,64},{8,72},{16,80},{24,88},{32,96},{40,104},{48,112},{56,120},{... | collective-permute-start | bytes 442376 | tf_op jit(solution)/shard_map/ppermute | solution.py:42
  13.8 4.8 %collective-permute-start.6 = (bf16[128,2304]{1,0:T(8,128)(2,1)S(1)}, bf16[128,2304]{1,0:T(8,128)(2,1)S(1)}, u32[]{:S(2)}, u32[]{:S(2)}) collective-permute-start(bf16[128,2304]{1,0:T(8,128)(2,1)S(1)} %stale_kv.2.kv0), channel_id=1, source_target_pairs={{0,8},{8,0},{16,24},{24,16},{32,40},{40,32},{48,56},{56,48},{64,72... | collective-permute-start | bytes 1769480 | tf_op jit(solution)/shard_map/ppermute | solution.py:42
  18.6 12.2 %copy-start.4 = (f32[1,8,128]{2,1,0:T(8,128)S(1)}, f32[1,8,128]{2,1,0:T(8,128)}, u32[]{:S(2)}) copy-start(f32[1,8,128]{2,1,0:T(8,128)} %param.11) | copy-start | bytes 12292
  18.6 12.1 %copy-start.5 = (s32[4]{0:T(128)S(1)}, s32[4]{0:T(128)}, u32[]{:S(2)}) copy-start(s32[4]{0:T(128)} %time_ref.1) | copy-start | bytes 52
  18.6 17.3 %copy-start = (bf16[1152,1152]{1,0:T(8,128)(2,1)S(1)}, bf16[1152,1152]{1,0:T(8,128)(2,1)}, u32[]{:S(2)}) copy-start(bf16[1152,1152]{1,0:T(8,128)(2,1)} %w_out_ref.1) | copy-start | bytes 7962628
  18.6 17.3 %copy-start.3 = (bf16[1152,16]{0,1:T(8,128)(2,1)S(1)}, bf16[1152,16]{0,1:T(8,128)(2,1)}, u32[]{:S(2)}) copy-start(bf16[1152,16]{0,1:T(8,128)(2,1)} %param.15) | copy-start | bytes 110596
  19.8 2.3 %collective-permute-start.7 = (bf16[128,2304]{1,0:T(8,128)(2,1)S(1)}, bf16[128,2304]{1,0:T(8,128)(2,1)S(1)}, u32[]{:S(2)}, u32[]{:S(2)}) collective-permute-start(bf16[128,2304]{1,0:T(8,128)(2,1)S(1)} %stale_kv.3.kv1.kv0), channel_id=1, source_target_pairs={{0,8},{8,0},{16,24},{24,16},{32,40},{40,32},{48,56},{56,48},{64,72... | collective-permute-start | bytes 1769480 | tf_op jit(solution)/shard_map/ppermute | solution.py:42
  24.2 8.6 %collective-permute-start.10 = (bf16[64,1280]{1,0:T(8,128)(2,1)S(1)}, bf16[64,1280]{1,0:T(8,128)(2,1)S(1)}, u32[]{:S(2)}, u32[]{:S(2)}) collective-permute-start(bf16[64,1280]{1,0:T(8,128)(2,1)S(1)} %get-tuple-element.31), channel_id=1, source_target_pairs={{0,128},{8,136},{16,144},{24,152},{32,160},{40,168},{48,176},{56,1... | collective-permute-start | bytes 491528 | tf_op jit(solution)/shard_map/ppermute | solution.py:42
  27.5 8.1 %collective-permute-start.9 = (bf16[64,1280]{1,0:T(8,128)(2,1)S(1)}, bf16[64,1280]{1,0:T(8,128)(2,1)S(1)}, u32[]{:S(2)}, u32[]{:S(2)}) collective-permute-start(bf16[64,1280]{1,0:T(8,128)(2,1)S(1)} %get-tuple-element.32), channel_id=1, source_target_pairs={{0,64},{8,72},{16,80},{24,88},{32,96},{40,104},{48,112},{56,120},{... | collective-permute-start | bytes 491528 | tf_op jit(solution)/shard_map/ppermute | solution.py:42
  28.2 7.7 %collective-permute-start.8 = (bf16[64,1280]{1,0:T(8,128)(2,1)S(1)}, bf16[64,1280]{1,0:T(8,128)(2,1)S(1)}, u32[]{:S(2)}, u32[]{:S(2)}) collective-permute-start(bf16[64,1280]{1,0:T(8,128)(2,1)S(1)} %get-tuple-element.33), channel_id=1, source_target_pairs={{0,192},{8,200},{16,208},{24,216},{32,224},{40,232},{48,240},{56,2... | collective-permute-start | bytes 491528 | tf_op jit(solution)/shard_map/ppermute | solution.py:42
  37.3 7.6 %collective-permute-start.11 = (f32[8,128]{1,0:T(8,128)S(1)}, f32[8,128]{1,0:T(8,128)S(1)}, u32[]{:S(2)}, u32[]{:S(2)}) collective-permute-start(f32[8,128]{1,0:T(8,128)S(1)} %get-tuple-element.30), channel_id=1, source_target_pairs={{0,1},{1,0},{2,3},{3,2},{4,5},{5,4},{6,7},{7,6},{8,9},{9,8},{10,11... | collective-permute-start | bytes 12296 | tf_op jit(solution)/shard_map/ppermute | solution.py:419

commit v8 on v7

--- a/solution.py
+++ b/solution.py
@@ -24,7 +24,7 @@
     mean = jnp.mean(values, axis=-1, keepdims=True)
     centred = values - mean
     var = jnp.mean(centred * centred, axis=-1, keepdims=True)
-    return centred / jnp.sqrt(var + 1e-06)
+    return centred * (1.0 / jnp.sqrt(var + 1e-06))
 
 
 def alpha_bar(step_index):

time: 45.6 us -> 45.6 us (level)
  no operation moved by 1% of the time
where the time goes in v8:
time: 45.6 us; the launch traced here: 45.5 us
  starting transfers between devices  23.2 us (51%)
  Pallas kernels  10.9 us (24%)
  waiting for transfers between devices  10.6 us (23%)
  other arithmetic  0.6 us (1%)
    ppermute x11, starting transfers between devices, send(): return lax.ppermute(value, 'patch', pairs)  17.8 us
    ppermute x11, waiting for transfers between devices, send(): return lax.ppermute(value, 'patch', pairs)  8.33 us
    ppermute x1, starting transfers between devices, body(): lax.ppermute(noise, 'guide', [(i, i ^ 1) for i in range(lax.axis_size('gu...  5.36 us
    pallas_call x2, Pallas kernels, project_stale(): pl.pallas_call(stale_kernel, in_specs=[pl.BlockSpec(memory_space=pltpu.VM...  2.32 us
    ppermute x1, waiting for transfers between devices, body(): lax.ppermute(noise, 'guide', [(i, i ^ 1) for i in range(lax.axis_size('gu...  2.25 us
    pallas_call x1, Pallas kernels, attend_late(): pl.pallas_call(attend_late_kernel, in_specs=[pl.BlockSpec(memory_space=pl...  2.08 us
    pallas_call x1, Pallas kernels, attend_own(): pl.pallas_call(attend_own_kernel, in_specs=[vmem] * 6 + [pl.BlockSpec(mem...  1.83 us
    pallas_call x1, Pallas kernels, attend_early(): pl.pallas_call(attend_early_kernel, in_specs=[vmem] * 3, out_specs=[vmem]...  1.63 us
  transfers between devices with their start and end apart: 12, of which 6 were waited for; matrix products, arithmetic and copies ran while one was open for 0% of the time, Pallas kernels for 14%

profile of v8, /device:TPU:2, one launch (start us, length us, event | category | flops | bytes accessed | tf_op | source)
XLA Modules:
  0.0 45.5 jit_solution(12516042045089022904)
XLA Ops:
  0.0 2.0 %collective-permute-start = (bf16[64,1152]{1,0:T(8,128)(2,1)}, bf16[64,1152]{1,0:T(8,128)(2,1)S(1)}, u32[]{:S(2)}, u32[]{:S(2)}) collective-permute-start(bf16[64,1152]{1,0:T(8,128)(2,1)} %bitcast.21), channel_id=1, source_target_pairs={{0,16},{8,24},{16,0},{24,8},{32,48},{40,56},{48,32},{56,40},{64,80... | collective-permute-start | bytes 442376 | tf_op jit(solution)/shard_map/ppermute | solution.py:42
  2.1 3.6 %collective-permute-start.5 = (bf16[64,1152]{1,0:T(8,128)(2,1)S(1)}, bf16[64,1152]{1,0:T(8,128)(2,1)S(1)}, u32[]{:S(2)}, u32[]{:S(2)}) collective-permute-start(bf16[64,1152]{1,0:T(8,128)(2,1)S(1)} %bitcast.22), channel_id=1, source_target_pairs={{0,48},{8,56},{16,32},{24,40},{32,16},{40,24},{48,0},{56,8},{64,11... | collective-permute-start | bytes 442376 | tf_op jit(solution)/shard_map/ppermute | solution.py:42
  5.7 0.0 collective-permute-start.4
  5.7 1.5 %fresh_qkv.1.fresh_ref = bf16[64,3456]{1,0:T(8,128)(2,1)S(1)} custom-call(bf16[64,1152]{1,0:T(8,128)(2,1)S(1)} %bitcast.15, f32[5,1,1152]{2,1,0:T(1,128)S(1)} %bitcast.17, bf16[1152,3456]{1,0:T(8,128)(2,1)S(1)} %bitcast.14), custom_call_target="tpu_custom_call" | custom-call | flops 509607936 | bytes 7962624 | tf_op jit(solution)/shard_map/fresh_qkv/pallas_call | solution.py:90
  7.3 3.3 %collective-permute-start.3 = (bf16[64,1152]{1,0:T(8,128)(2,1)S(1)}, bf16[64,1152]{1,0:T(8,128)(2,1)S(1)}, u32[]{:S(2)}, u32[]{:S(2)}) collective-permute-start(bf16[64,1152]{1,0:T(8,128)(2,1)S(1)} %slice.20.q_ref), channel_id=1, source_target_pairs={{0,128},{8,136},{16,144},{24,152},{32,160},{40,168},{48,176},{56,1... | collective-permute-start | bytes 442376 | tf_op jit(solution)/shard_map/ppermute | solution.py:42
  10.6 1.1 %collective-permute-start.2 = (bf16[64,1152]{1,0:T(8,128)(2,1)S(1)}, bf16[64,1152]{1,0:T(8,128)(2,1)S(1)}, u32[]{:S(2)}, u32[]{:S(2)}) collective-permute-start(bf16[64,1152]{1,0:T(8,128)(2,1)S(1)} %slice.20.q_ref), channel_id=1, source_target_pairs={{0,192},{8,200},{16,208},{24,216},{32,224},{40,232},{48,240},{56,2... | collective-permute-start | bytes 442376 | tf_op jit(solution)/shard_map/ppermute | solution.py:42
  11.6 0.0 collective-permute-done.refs_1_
  11.6 1.0 %collective-permute-start.1 = (bf16[64,1152]{1,0:T(8,128)(2,1)S(1)}, bf16[64,1152]{1,0:T(8,128)(2,1)S(1)}, u32[]{:S(2)}, u32[]{:S(2)}) collective-permute-start(bf16[64,1152]{1,0:T(8,128)(2,1)S(1)} %slice.20.q_ref), channel_id=1, source_target_pairs={{0,64},{8,72},{16,80},{24,88},{32,96},{40,104},{48,112},{56,120},{... | collective-permute-start | bytes 442376 | tf_op jit(solution)/shard_map/ppermute | solution.py:42
  12.6 1.2 %stale_kv.2.kv0 = bf16[128,2304]{1,0:T(8,128)(2,1)S(1)} custom-call(bf16[64,1152]{1,0:T(8,128)(2,1)S(1)} %bitcast.24, bf16[64,1152]{1,0:T(8,128)(2,1)S(1)} %collective-permute-done.refs_1_, bf16[1152,3456]{1,0:T(8,128)(2,1)S(1)} %bitcast.14), custom_call_target="tpu_custom_call" | custom-call | flops 20000000000 | bytes 1 | tf_op jit(solution)/shard_map/stale_kv/pallas_call | solution.py:118
  13.8 0.1 collective-permute-start.6
  13.9 4.6 %collective-permute-done.4.refs_3_ = bf16[64,1152]{1,0:T(8,128)(2,1)S(1)} collective-permute-done((bf16[64,1152]{1,0:T(8,128)(2,1)S(1)}, bf16[64,1152]{1,0:T(8,128)(2,1)S(1)}, u32[]{:S(2)}, u32[]{:S(2)}) %collective-permute-start.4) | collective-permute-done | bytes 147488 | tf_op jit(solution)/shard_map/ppermute | solution.py:42
  18.5 0.1 gather_blocks.1
  18.6 0.0 copy-start.4
  18.6 0.0 copy-start.5
  18.6 0.0 copy-start
  18.6 0.0 copy-start.3
  18.6 1.2 %stale_kv.3.kv1.kv0 = bf16[128,2304]{1,0:T(8,128)(2,1)S(1)} custom-call(bf16[128,1152]{1,0:T(8,128)(2,1)S(1)} %get-tuple-element.20.refs_0_, bf16[1152,3456]{1,0:T(8,128)(2,1)S(1)} %bitcast.14), custom_call_target="tpu_custom_call" | custom-call | flops 1 | bytes 1 | tf_op jit(solution)/shard_map/stale_kv/pallas_call | solution.py:118
  19.8 0.3 collective-permute-start.7
  20.1 1.6 %attend_early.1 = (f32[192,1152]{1,0:T(8,128)S(1)}, f32[192,128]{1,0:T(8,128)S(1)}) custom-call(bf16[192,1152]{1,0:T(8,128)(2,1)S(1)} %get-tuple-element.23.q_ref, bf16[128,2304]{1,0:T(8,128)(2,1)S(1)} %stale_kv.2.kv0, bf16[128,2304]{1,0:T(8,128)(2,1)S(1)} %collective-permute-done.6.kv2.kv1), custom_call_target="tpu_custom_call" | custom-call | flops 1 | bytes 1 | tf_op jit(solution)/shard_map/attend_early/pallas_call | solution.py:281
  21.7 0.3 collective-permute-done.7.kv3.kv1
  22.1 2.1 %attend_late.1 = bf16[192,1280]{1,0:T(8,128)(2,1)S(1)} custom-call(bf16[192,1152]{1,0:T(8,128)(2,1)S(1)} %get-tuple-element.23.q_ref, bf16[128,2304]{1,0:T(8,128)(2,1)S(1)} %stale_kv.3.kv1.kv0, bf16[128,2304]{1,0:T(8,128)(2,1)S(1)} %collective-permute-done.7.kv3.kv1, f32[192,1152]{1,0:T(8,128)S(1)} %get-tuple-element.24.early_ref, ...), custom_call_target="tpu_custom_call" | custom-call | flops 1 | bytes 1 | tf_op jit(solution)/shard_map/attend_late/pallas_call | solution.py:297
  24.2 3.3 %collective-permute-start.10 = (bf16[64,1280]{1,0:T(8,128)(2,1)S(1)}, bf16[64,1280]{1,0:T(8,128)(2,1)S(1)}, u32[]{:S(2)}, u32[]{:S(2)}) collective-permute-start(bf16[64,1280]{1,0:T(8,128)(2,1)S(1)} %get-tuple-element.31), channel_id=1, source_target_pairs={{0,128},{8,136},{16,144},{24,152},{32,160},{40,168},{48,176},{56,1... | collective-permute-start | bytes 491528 | tf_op jit(solution)/shard_map/ppermute | solution.py:42
  27.5 0.7 %collective-permute-start.9 = (bf16[64,1280]{1,0:T(8,128)(2,1)S(1)}, bf16[64,1280]{1,0:T(8,128)(2,1)S(1)}, u32[]{:S(2)}, u32[]{:S(2)}) collective-permute-start(bf16[64,1280]{1,0:T(8,128)(2,1)S(1)} %get-tuple-element.32), channel_id=1, source_target_pairs={{0,64},{8,72},{16,80},{24,88},{32,96},{40,104},{48,112},{56,120},{... | collective-permute-start | bytes 491528 | tf_op jit(solution)/shard_map/ppermute | solution.py:42
  28.2 2.6 %collective-permute-start.8 = (bf16[64,1280]{1,0:T(8,128)(2,1)S(1)}, bf16[64,1280]{1,0:T(8,128)(2,1)S(1)}, u32[]{:S(2)}, u32[]{:S(2)}) collective-permute-start(bf16[64,1280]{1,0:T(8,128)(2,1)S(1)} %get-tuple-element.33), channel_id=1, source_target_pairs={{0,192},{8,200},{16,208},{24,216},{32,224},{40,232},{48,240},{56,2... | collective-permute-start | bytes 491528 | tf_op jit(solution)/shard_map/ppermute | solution.py:42
  30.7 1.8 %attend_own.1 = (bf16[64,1280]{1,0:T(8,128)(2,1)S(1)}, f32[8,128]{1,0:T(8,128)S(1)}, f32[2,8,128]{2,1,0:T(8,128)S(1)}) custom-call(bf16[64,1152]{1,0:T(8,128)(2,1)S(1)} %slice.20.q_ref, bf16[128,2304]{1,0:T(8,128)(2,1)S(1)} %stale_kv.2.kv0, bf16[128,2304]{1,0:T(8,128)(2,1)S(1)} %stale_kv.3.kv1.kv0, bf16[128,2304]{1,0:T(8,128)(2,1)S(1)} %collective-permute-done.6.kv2.kv1, ...), custom_call_target="tpu_custom_call" | custom-call | flops 536870912 | bytes 2359296 | tf_op jit(solution)/shard_map/attend_own/pallas_call | solution.py:327
  32.6 0.3 collective-permute-done.10.p3
  32.8 2.7 %collective-permute-done.9.p2 = bf16[64,1280]{1,0:T(8,128)(2,1)S(1)} collective-permute-done((bf16[64,1280]{1,0:T(8,128)(2,1)S(1)}, bf16[64,1280]{1,0:T(8,128)(2,1)S(1)}, u32[]{:S(2)}, u32[]{:S(2)}) %collective-permute-start.9) | collective-permute-done | bytes 163872 | tf_op jit(solution)/shard_map/ppermute | solution.py:42
  35.6 0.4 collective-permute-done.8.p1
  35.9 1.4 %post.1 = (f32[8,128]{1,0:T(8,128)S(1)}, f32[8,128]{1,0:T(8,128)S(1)}) custom-call(bf16[64,1280]{1,0:T(8,128)(2,1)S(1)} %get-tuple-element.22.p0, bf16[64,1280]{1,0:T(8,128)(2,1)S(1)} %collective-permute-done.8.p1, bf16[64,1280]{1,0:T(8,128)(2,1)S(1)} %collective-permute-done.9.p2, bf16[64,1280]{1,0:T(8,128)(2,1)S(1)} %collective-permute-done.10.p3, ...), custom_call_target="tpu_custom_call" | custom-call | flops 169869312 | bytes 2654208 | tf_op jit(solution)/shard_map/post/pallas_call | solution.py:378
  37.3 5.4 %collective-permute-start.11 = (f32[8,128]{1,0:T(8,128)S(1)}, f32[8,128]{1,0:T(8,128)S(1)}, u32[]{:S(2)}, u32[]{:S(2)}) collective-permute-start(f32[8,128]{1,0:T(8,128)S(1)} %get-tuple-element.30), channel_id=1, source_target_pairs={{0,1},{1,0},{2,3},{3,2},{4,5},{5,4},{6,7},{7,6},{8,9},{9,8},{10,11... | collective-permute-start | bytes 12296 | tf_op jit(solution)/shard_map/ppermute | solution.py:419
  42.7 2.2 %collective-permute-done.11 = f32[8,128]{1,0:T(8,128)S(1)} collective-permute-done((f32[8,128]{1,0:T(8,128)S(1)}, f32[8,128]{1,0:T(8,128)S(1)}, u32[]{:S(2)}, u32[]{:S(2)}) %collective-permute-start.11) | collective-permute-done | bytes 4128 | tf_op jit(solution)/shard_map/ppermute | solution.py:419
  44.9 0.6 %fusion.1 = f32[1,8,128]{2,1,0:T(8,128)} fusion(f32[8,128]{1,0:T(8,128)S(1)} %get-tuple-element.29, f32[8,128]{1,0:T(8,128)S(1)} %collective-permute-done.11, f32[2,8,128]{2,1,0:T(8,128)S(1)} %get-tuple-element.28.gain_ref), kind=kLoop, calls=%fused_computation.2 | loop fusion | flops 2048 | bytes 16384 | tf_op jit(solution)/shard_map/broadcast_in_dim | solution.py:422
  (23 shorter events, 0.1 us)
Async XLA Ops:
  0.0 5.7 %slice-start = ((s8[7962624]{0:T(1024)(128)(4,1)}), s8[4194304]{0:T(1024)(128)(4,1)S(1)}, s32[]{:S(2)}) async-start(s8[7962624]{0:T(1024)(128)(4,1)} %bitcast.13), calls=%async_computation | async-start | bytes 8388608
  0.0 2.1 %copy-start.6 = (bf16[1,64,1152]{2,1,0:T(8,128)(2,1)S(1)}, bf16[1,64,1152]{2,1,0:T(8,128)(2,1)}, u32[]{:S(2)}) copy-start(bf16[1,64,1152]{2,1,0:T(8,128)(2,1)} %param.9) | copy-start | bytes 442372
  0.0 5.7 %slice-start.1 = ((s8[7962624]{0:T(1024)(128)(4,1)}), s8[3768320]{0:T(1024)(128)(4,1)S(1)}, s32[]{:S(2)}) async-start(s8[7962624]{0:T(1024)(128)(4,1)} %bitcast.13), calls=%async_computation.1 | async-start | bytes 7536640
  0.0 5.7 %copy-start.1 = (bf16[1,64,1152]{2,1,0:T(8,128)(2,1)S(1)}, bf16[1,64,1152]{2,1,0:T(8,128)(2,1)}, u32[]{:S(2)}) copy-start(bf16[1,64,1152]{2,1,0:T(8,128)(2,1)} %param.8) | copy-start | bytes 442372
  0.0 5.7 %copy-start.2 = (f32[1,5,1152]{2,0,1:T(1,128)S(1)}, f32[1,5,1152]{2,0,1:T(1,128)}, u32[]{:S(2)}) copy-start(f32[1,5,1152]{2,0,1:T(1,128)} %param.10) | copy-start | bytes 69124
  0.0 11.6 %collective-permute-start = (bf16[64,1152]{1,0:T(8,128)(2,1)}, bf16[64,1152]{1,0:T(8,128)(2,1)S(1)}, u32[]{:S(2)}, u32[]{:S(2)}) collective-permute-start(bf16[64,1152]{1,0:T(8,128)(2,1)} %bitcast.21), channel_id=1, source_target_pairs={{0,16},{8,24},{16,0},{24,8},{32,48},{40,56},{48,32},{56,40},{64,80... | collective-permute-start | bytes 442376 | tf_op jit(solution)/shard_map/ppermute | solution.py:42
  2.1 11.7 %collective-permute-start.5 = (bf16[64,1152]{1,0:T(8,128)(2,1)S(1)}, bf16[64,1152]{1,0:T(8,128)(2,1)S(1)}, u32[]{:S(2)}, u32[]{:S(2)}) collective-permute-start(bf16[64,1152]{1,0:T(8,128)(2,1)S(1)} %bitcast.22), channel_id=1, source_target_pairs={{0,48},{8,56},{16,32},{24,40},{32,16},{40,24},{48,0},{56,8},{64,11... | collective-permute-start | bytes 442376 | tf_op jit(solution)/shard_map/ppermute | solution.py:42
  5.7 12.8 %collective-permute-start.4 = (bf16[64,1152]{1,0:T(8,128)(2,1)S(1)}, bf16[64,1152]{1,0:T(8,128)(2,1)S(1)}, u32[]{:S(2)}, u32[]{:S(2)}) collective-permute-start(bf16[64,1152]{1,0:T(8,128)(2,1)S(1)} %bitcast.23), channel_id=1, source_target_pairs={{0,32},{8,40},{16,48},{24,56},{32,0},{40,8},{48,16},{56,24},{64,96... | collective-permute-start | bytes 442376 | tf_op jit(solution)/shard_map/ppermute | solution.py:42
  7.3 11.2 %collective-permute-start.3 = (bf16[64,1152]{1,0:T(8,128)(2,1)S(1)}, bf16[64,1152]{1,0:T(8,128)(2,1)S(1)}, u32[]{:S(2)}, u32[]{:S(2)}) collective-permute-start(bf16[64,1152]{1,0:T(8,128)(2,1)S(1)} %slice.20.q_ref), channel_id=1, source_target_pairs={{0,128},{8,136},{16,144},{24,152},{32,160},{40,168},{48,176},{56,1... | collective-permute-start | bytes 442376 | tf_op jit(solution)/shard_map/ppermute | solution.py:42
  10.6 7.9 %collective-permute-start.2 = (bf16[64,1152]{1,0:T(8,128)(2,1)S(1)}, bf16[64,1152]{1,0:T(8,128)(2,1)S(1)}, u32[]{:S(2)}, u32[]{:S(2)}) collective-permute-start(bf16[64,1152]{1,0:T(8,128)(2,1)S(1)} %slice.20.q_ref), channel_id=1, source_target_pairs={{0,192},{8,200},{16,208},{24,216},{32,224},{40,232},{48,240},{56,2... | collective-permute-start | bytes 442376 | tf_op jit(solution)/shard_map/ppermute | solution.py:42
  11.6 6.9 %collective-permute-start.1 = (bf16[64,1152]{1,0:T(8,128)(2,1)S(1)}, bf16[64,1152]{1,0:T(8,128)(2,1)S(1)}, u32[]{:S(2)}, u32[]{:S(2)}) collective-permute-start(bf16[64,1152]{1,0:T(8,128)(2,1)S(1)} %slice.20.q_ref), channel_id=1, source_target_pairs={{0,64},{8,72},{16,80},{24,88},{32,96},{40,104},{48,112},{56,120},{... | collective-permute-start | bytes 442376 | tf_op jit(solution)/shard_map/ppermute | solution.py:42
  13.8 4.8 %collective-permute-start.6 = (bf16[128,2304]{1,0:T(8,128)(2,1)S(1)}, bf16[128,2304]{1,0:T(8,128)(2,1)S(1)}, u32[]{:S(2)}, u32[]{:S(2)}) collective-permute-start(bf16[128,2304]{1,0:T(8,128)(2,1)S(1)} %stale_kv.2.kv0), channel_id=1, source_target_pairs={{0,8},{8,0},{16,24},{24,16},{32,40},{40,32},{48,56},{56,48},{64,72... | collective-permute-start | bytes 1769480 | tf_op jit(solution)/shard_map/ppermute | solution.py:42
  18.6 12.2 %copy-start.4 = (f32[1,8,128]{2,1,0:T(8,128)S(1)}, f32[1,8,128]{2,1,0:T(8,128)}, u32[]{:S(2)}) copy-start(f32[1,8,128]{2,1,0:T(8,128)} %param.11) | copy-start | bytes 12292
  18.6 12.1 %copy-start.5 = (s32[4]{0:T(128)S(1)}, s32[4]{0:T(128)}, u32[]{:S(2)}) copy-start(s32[4]{0:T(128)} %time_ref.1) | copy-start | bytes 52
  18.6 17.3 %copy-start = (bf16[1152,1152]{1,0:T(8,128)(2,1)S(1)}, bf16[1152,1152]{1,0:T(8,128)(2,1)}, u32[]{:S(2)}) copy-start(bf16[1152,1152]{1,0:T(8,128)(2,1)} %w_out_ref.1) | copy-start | bytes 7962628
  18.6 17.3 %copy-start.3 = (bf16[1152,16]{0,1:T(8,128)(2,1)S(1)}, bf16[1152,16]{0,1:T(8,128)(2,1)}, u32[]{:S(2)}) copy-start(bf16[1152,16]{0,1:T(8,128)(2,1)} %param.15) | copy-start | bytes 110596
  19.8 2.3 %collective-permute-start.7 = (bf16[128,2304]{1,0:T(8,128)(2,1)S(1)}, bf16[128,2304]{1,0:T(8,128)(2,1)S(1)}, u32[]{:S(2)}, u32[]{:S(2)}) collective-permute-start(bf16[128,2304]{1,0:T(8,128)(2,1)S(1)} %stale_kv.3.kv1.kv0), channel_id=1, source_target_pairs={{0,8},{8,0},{16,24},{24,16},{32,40},{40,32},{48,56},{56,48},{64,72... | collective-permute-start | bytes 1769480 | tf_op jit(solution)/shard_map/ppermute | solution.py:42
  24.2 8.6 %collective-permute-start.10 = (bf16[64,1280]{1,0:T(8,128)(2,1)S(1)}, bf16[64,1280]{1,0:T(8,128)(2,1)S(1)}, u32[]{:S(2)}, u32[]{:S(2)}) collective-permute-start(bf16[64,1280]{1,0:T(8,128)(2,1)S(1)} %get-tuple-element.31), channel_id=1, source_target_pairs={{0,128},{8,136},{16,144},{24,152},{32,160},{40,168},{48,176},{56,1... | collective-permute-start | bytes 491528 | tf_op jit(solution)/shard_map/ppermute | solution.py:42
  27.5 8.1 %collective-permute-start.9 = (bf16[64,1280]{1,0:T(8,128)(2,1)S(1)}, bf16[64,1280]{1,0:T(8,128)(2,1)S(1)}, u32[]{:S(2)}, u32[]{:S(2)}) collective-permute-start(bf16[64,1280]{1,0:T(8,128)(2,1)S(1)} %get-tuple-element.32), channel_id=1, source_target_pairs={{0,64},{8,72},{16,80},{24,88},{32,96},{40,104},{48,112},{56,120},{... | collective-permute-start | bytes 491528 | tf_op jit(solution)/shard_map/ppermute | solution.py:42
  28.2 7.7 %collective-permute-start.8 = (bf16[64,1280]{1,0:T(8,128)(2,1)S(1)}, bf16[64,1280]{1,0:T(8,128)(2,1)S(1)}, u32[]{:S(2)}, u32[]{:S(2)}) collective-permute-start(bf16[64,1280]{1,0:T(8,128)(2,1)S(1)} %get-tuple-element.33), channel_id=1, source_target_pairs={{0,192},{8,200},{16,208},{24,216},{32,224},{40,232},{48,240},{56,2... | collective-permute-start | bytes 491528 | tf_op jit(solution)/shard_map/ppermute | solution.py:42
  37.3 7.6 %collective-permute-start.11 = (f32[8,128]{1,0:T(8,128)S(1)}, f32[8,128]{1,0:T(8,128)S(1)}, u32[]{:S(2)}, u32[]{:S(2)}) collective-permute-start(f32[8,128]{1,0:T(8,128)S(1)} %get-tuple-element.30), channel_id=1, source_target_pairs={{0,1},{1,0},{2,3},{3,2},{4,5},{5,4},{6,7},{7,6},{8,9},{9,8},{10,11... | collective-permute-start | bytes 12296 | tf_op jit(solution)/shard_map/ppermute | solution.py:419
